TPU v7x, 32 devices: a whole 2x2x4 slice. The times are simulated.
32 devices in a mesh: rep: 4 (over x, core), fsdp: 8 (over z, y).
Axes of the slice: x: 2, y: 2, z: 4, core: 2. Of those that a mesh axis runs over, the one named last changes fastest.
Arguments:
- layer_input: bfloat16 [16384, 1536], P(('rep', 'fsdp')), may hold values from -6 to 6
- first_gain: float32 [1536], replicated, may hold values from 0.25 to 1.75
- qkv_weight: bfloat16 [1536, 4608], P('fsdp'), may hold values from -0.15625 to 0.15625
- conv_kernel: float32 [16, 6, 11], replicated, may hold values from -0.6 to 1.6
- head_mixing: float32 [8, 2, 2], replicated, may hold values from 0.25 to 1
- group_gain: float32 [1536], replicated, may hold values from 0.25 to 1.75
- out_weight: bfloat16 [1536, 1536], P('fsdp'), may hold values from -0.15625 to 0.15625
- second_gain: float32 [1536], replicated, may hold values from 0.25 to 1.75
- inner_weight: bfloat16 [1536, 8192], P('fsdp'), may hold values from -0.15625 to 0.15625
- down_weight: bfloat16 [4096, 1536], P('fsdp'), may hold values from -0.09375 to 0.09375
- doc_lengths: int32 [32, 4], P(('rep', 'fsdp')), may hold values from 1 to 256, 512 in all within a row
- cotangent: bfloat16 [16384, 1536], P(('rep', 'fsdp')), may hold values from -6 to 6
Outputs:
- layer_output: bfloat16 [16384, 1536], P(('rep', 'fsdp'))
- grad_input: float32 [16384, 1536], P(('rep', 'fsdp'))
- grad_first: float32 [1536], replicated
- grad_qkv: float32 [1536, 4608], P('fsdp')
- grad_kernel: float32 [16, 6, 11], replicated
- grad_mixing: float32 [8, 2, 2], replicated
- grad_group: float32 [1536], replicated
- grad_proj: float32 [1536, 1536], P('fsdp')
- grad_second: float32 [1536], replicated
- grad_inner: float32 [1536, 8192], P('fsdp')
- grad_down: float32 [4096, 1536], P('fsdp')
Inputs may be any that keep to these rules, and one draw needn't show every extreme that they name: `doc_lengths`: each sequence's lengths sum to 512, and its largest is 256.
All inputs are finite; a program needn't handle non-finite values.
Results may differ from a plain program's by a relative error of at most 0.02.
Values may be sent and summed in bfloat16 or wider, within the bound.
A program may use at most 320 MiB of HBM per device.

v0:
```python
import math

import jax
import jax.numpy as jnp
from jax import lax
from jax.sharding import PartitionSpec as P

HEADS = 16
HEAD_DIM = 96
CQ = 6
CK = 11


EPSILON = 1e-05


def rms_norm(values, gains):
    return values * lax.rsqrt(jnp.mean(values * values, axis=-1, keepdims=True) + EPSILON) * gains


def group_norm(values, gains):
    count_rows = values.shape[0]
    per_head = values.reshape(count_rows, HEADS, values.shape[1] // HEADS)
    centred = per_head - jnp.mean(per_head, axis=-1, keepdims=True)
    spread = jnp.mean(centred * centred, axis=-1, keepdims=True)
    return (centred * lax.rsqrt(spread + EPSILON)).reshape(count_rows, values.shape[1]) * gains


def swiglu(gate_up):
    middle_col = gate_up.shape[1] // 2
    return jax.nn.silu(gate_up[:, :middle_col]) * gate_up[:, middle_col:]


def shift_rows(values, amount):
    if amount == 0:
        return values
    filler = jnp.zeros(values.shape[:-2] + (amount, values.shape[-1]), values.dtype)
    return jnp.concatenate([filler, values[..., :-amount, :]], axis=-2)


def shift_cols(values, amount):
    if amount == 0:
        return values
    if amount > 0:
        filler = jnp.zeros(values.shape[:-1] + (amount,), values.dtype)
        return jnp.concatenate([filler, values[..., :-amount]], axis=-1)
    filler = jnp.zeros(values.shape[:-1] + (-amount,), values.dtype)
    return jnp.concatenate([values[..., -amount:], filler], axis=-1)


def mask_tables(length_row, seq_len, lags):
    ends = jnp.cumsum(length_row)[:-1]
    places = jnp.arange(seq_len, dtype=jnp.int32)
    segment = jnp.sum((places[:, None] >= ends[None, :]).astype(jnp.int32), axis=1)
    allowed = (places[None, :] <= places[:, None]) & (segment[:, None] == segment[None, :])
    padded = jnp.concatenate([jnp.full((lags,), -1, jnp.int32), segment])
    row_keep = jnp.stack(
        [
            padded[lags - row_shift : lags - row_shift + seq_len] == segment
            for row_shift in range(lags)
        ]
    )
    return (allowed, row_keep.astype(jnp.float32))


def score_mix(scores, kernel, mixing, allowed, row_keep):
    masked = jnp.where(allowed, scores, 0.0)
    centre = kernel.shape[2] // 2
    shifted = [
        shift_rows(masked, row_shift) * row_keep[row_shift][:, None]
        for row_shift in range(kernel.shape[1])
    ]
    summed = jnp.zeros_like(scores)
    for column in range(kernel.shape[2]):
        partial_sum = shifted[0] * kernel[:, 0, column][:, None, None]
        for row_shift in range(1, kernel.shape[1]):
            partial_sum = (
                partial_sum + shifted[row_shift] * kernel[:, row_shift, column][:, None, None]
            )
        summed = summed + shift_cols(partial_sum, column - centre)
    logits = jnp.where(allowed, summed, -1e30)
    largest = jnp.max(logits, axis=-1, keepdims=True)
    weights = jnp.exp(logits - largest)
    probability = weights / jnp.sum(weights, axis=-1, keepdims=True)
    return jnp.sum(mixing[:, :, None, None] * probability[None], axis=1)


def by_groups(matrix):
    seq_len = matrix.shape[0]
    return matrix.reshape(seq_len, HEADS // 2, 2, HEAD_DIM).transpose(1, 2, 0, 3)


def from_groups(blocks):
    return blocks.transpose(2, 0, 1, 3).reshape(blocks.shape[2], HEADS * HEAD_DIM)


def project(operand, weight):
    return jnp.dot(
        operand,
        lax.all_gather(weight, "fsdp", axis=0, tiled=True),
        preferred_element_type=jnp.float32,
    )


def project_back(upstream, weight):
    return lax.dot_general(
        upstream,
        lax.all_gather(weight, "fsdp", axis=0, tiled=True),
        (((1,), (1,)), ((), ())),
        preferred_element_type=jnp.float32,
    )


def weight_grad(operand, upstream):
    return lax.psum_scatter(
        lax.dot_general(
            operand, upstream, (((0,), (0,)), ((), ())), preferred_element_type=jnp.float32
        ).astype(jnp.bfloat16),
        "fsdp",
        scatter_dimension=0,
        tiled=True,
    ).astype(jnp.float32)


def attend_forward(query, keys, values, conv_kernel, head_mixing, allowed, row_keep):
    score_scale = 1.0 / math.sqrt(HEAD_DIM)

    def one_group(operands):
        q_group, k_group, v_group, k_conv, m_group = operands
        scores = (
            jnp.einsum("hid,hjd->hij", q_group, k_group, preferred_element_type=jnp.float32)
            * score_scale
        )
        probability = score_mix(scores, k_conv, m_group, allowed, row_keep).astype(jnp.bfloat16)
        return jnp.einsum("hij,hjd->hid", probability, v_group, preferred_element_type=jnp.float32)

    blocks = lax.map(
        one_group,
        (
            by_groups(query),
            by_groups(keys),
            by_groups(values),
            conv_kernel.reshape(HEADS // 2, 2, CQ, CK),
            head_mixing,
        ),
    )
    return from_groups(blocks)


def attend_backward(query, keys, values, upstream, conv_kernel, head_mixing, allowed, row_keep):
    score_scale = 1.0 / math.sqrt(HEAD_DIM)

    def one_group(operands):
        q_group, k_group, v_group, d_group, k_conv, m_group = operands
        scores = (
            jnp.einsum("hid,hjd->hij", q_group, k_group, preferred_element_type=jnp.float32)
            * score_scale
        )

        def mixing_piece(score_arg, kernel_arg, mixing_arg):
            return score_mix(score_arg, kernel_arg, mixing_arg, allowed, row_keep)

        probability, pull = jax.vjp(mixing_piece, scores, k_conv, m_group)
        rounded = probability.astype(jnp.bfloat16)
        d_prob = jnp.einsum("hid,hjd->hij", d_group, v_group, preferred_element_type=jnp.float32)
        d_values = jnp.einsum("hij,hid->hjd", rounded, d_group, preferred_element_type=jnp.float32)
        d_scores, d_kernel, d_mixing = pull(d_prob)
        d_rounded = d_scores.astype(jnp.bfloat16)
        d_query = (
            jnp.einsum("hij,hjd->hid", d_rounded, k_group, preferred_element_type=jnp.float32)
            * score_scale
        )
        d_keys = (
            jnp.einsum("hij,hid->hjd", d_rounded, q_group, preferred_element_type=jnp.float32)
            * score_scale
        )
        return (d_query, d_keys, d_values, d_kernel, d_mixing)

    results = lax.map(
        one_group,
        (
            by_groups(query),
            by_groups(keys),
            by_groups(values),
            by_groups(upstream),
            conv_kernel.reshape(HEADS // 2, 2, CQ, CK),
            head_mixing,
        ),
    )
    return (
        from_groups(results[0]),
        from_groups(results[1]),
        from_groups(results[2]),
        results[3].reshape(HEADS, CQ, CK),
        results[4],
    )


def body(
    layer_input,
    first_gain,
    qkv_weight,
    conv_kernel,
    head_mixing,
    group_gain,
    out_weight,
    second_gain,
    inner_weight,
    down_weight,
    doc_lengths,
    cotangent,
):
    width = layer_input.shape[1]
    seq_len = layer_input.shape[0]
    inputs = layer_input.astype(jnp.float32)
    allowed, row_keep = mask_tables(doc_lengths[0], seq_len, CQ)
    normed_value, first_pull = jax.vjp(rms_norm, inputs, first_gain)
    normed = normed_value.astype(jnp.bfloat16)
    projected = project(normed, qkv_weight).astype(jnp.bfloat16)
    query = projected[:, :width]
    keys = projected[:, width : 2 * width]
    values = projected[:, 2 * width :]
    attended = attend_forward(query, keys, values, conv_kernel, head_mixing, allowed, row_keep)
    grouped_value, group_pull = jax.vjp(group_norm, attended, group_gain)
    grouped = grouped_value.astype(jnp.bfloat16)
    middle = inputs + project(grouped, out_weight)
    second_value, second_pull = jax.vjp(rms_norm, middle, second_gain)
    second = second_value.astype(jnp.bfloat16)
    gate_up = project(second, inner_weight)
    hidden_value, swiglu_pull = jax.vjp(swiglu, gate_up)
    hidden = hidden_value.astype(jnp.bfloat16)
    layer_output = (middle + project(hidden, down_weight)).astype(jnp.bfloat16)
    upstream = cotangent.astype(jnp.float32)
    grad_down = weight_grad(hidden, cotangent)
    d_hidden = project_back(cotangent, down_weight)
    d_gate_up = swiglu_pull(d_hidden)[0].astype(jnp.bfloat16)
    grad_inner = weight_grad(second, d_gate_up)
    d_second = project_back(d_gate_up, inner_weight)
    d_middle, grad_second = second_pull(d_second)
    d_middle = upstream + d_middle
    d_branch = d_middle.astype(jnp.bfloat16)
    grad_proj = weight_grad(grouped, d_branch)
    d_grouped = project_back(d_branch, out_weight)
    d_attended, grad_group = group_pull(d_grouped)
    d_query, d_keys, d_values, grad_kernel, grad_mixing = attend_backward(
        query,
        keys,
        values,
        d_attended.astype(jnp.bfloat16),
        conv_kernel,
        head_mixing,
        allowed,
        row_keep,
    )
    d_projected = jnp.concatenate([d_query, d_keys, d_values], axis=1).astype(jnp.bfloat16)
    grad_qkv = weight_grad(normed, d_projected)
    d_normed = project_back(d_projected, qkv_weight)
    d_inputs, grad_first = first_pull(d_normed)
    grad_input = d_middle + d_inputs
    small = lax.psum(
        (grad_first, grad_kernel, grad_mixing, grad_group, grad_second), ("rep", "fsdp")
    )
    shards = (grad_qkv, grad_proj, grad_inner, grad_down)
    shards = (
        lax.psum(shards[0].astype(jnp.bfloat16), "rep").astype(jnp.float32),
        lax.psum(shards[1].astype(jnp.bfloat16), "rep").astype(jnp.float32),
        lax.psum(shards[2].astype(jnp.bfloat16), "rep").astype(jnp.float32),
        lax.psum(shards[3].astype(jnp.bfloat16), "rep").astype(jnp.float32),
    )
    return (
        layer_output,
        grad_input,
        small[0],
        shards[0],
        small[1],
        small[2],
        small[3],
        shards[1],
        small[4],
        shards[2],
        shards[3],
    )


def solution(mesh):
    placed = (
        P(("rep", "fsdp"), None),
        P(),
        P("fsdp", None),
        P(),
        P(),
        P(),
        P("fsdp", None),
        P(),
        P("fsdp", None),
        P("fsdp", None),
        P(("rep", "fsdp"), None),
        P(("rep", "fsdp"), None),
    )
    return jax.shard_map(
        body,
        mesh=mesh,
        in_specs=placed,
        out_specs=(
            P(("rep", "fsdp"), None),
            P(("rep", "fsdp"), None),
            P(),
            P("fsdp", None),
            P(),
            P(),
            P(),
            P("fsdp", None),
            P(),
            P("fsdp", None),
            P("fsdp", None),
        ),
        check_vma=False,
    )
```

profile of v0, /device:TPU:0, one launch (start us, length us, event | category | flops | bytes accessed | tf_op | source)
XLA Modules:
  0.0 3170.1 jit_solution(17603402515182418209)
XLA Ops:
  13.0 195.5 %all-gather.5.cloned.1.call-done = bf16[1536,4608]{1,0:T(8,128)(2,1)} async-done(((bf16[192,4608]{1,0:T(8,128)(2,1)}), bf16[1536,4608]{1,0:T(8,128)(2,1)}) %all-gather.5.cloned.1.call-update) | async-done | bytes 14155792 | tf_op jit(solution)/shard_map/all_gather | solution.py:100
  208.6 10.9 convolution_convert_fusion.4
  226.9 393.8 %while.32 = (s32[]{:T(128)}, f32[8,2,512,96]{2,3,1,0:T(8,128)}, f32[8,2,2]{2,1,0:T(2,128)S(1)}, bf16[8,2,512,96]{2,3,1,0:T(8,128)(2,1)}, bf16[8,2,512,96]{2,3,1,...) while((s32[]{:T(128)}, f32[8,2,512,96]{2,3,1,0:T(8,128)}, ...), condition=%wide.region_7.8_spmd.clone.clone, body=%wide.region_3.7_spmd.clone.sunk.clone | while | flops 278321664 | bytes 220977904 | solution.py:137
  653.4 115.6 %all-gather.9.cloned.1.call-done = bf16[1536,8192]{1,0:T(8,128)(2,1)} async-done(((bf16[192,8192]{1,0:T(8,128)(2,1)}), bf16[1536,8192]{1,0:T(8,128)(2,1)}) %all-gather.9.cloned.1.call-update) | async-done | bytes 25165840 | tf_op jit(solution)/shard_map/all_gather | solution.py:100
  769.0 22.2 fusion.209
  791.2 156.3 %all-gather.11.cloned.1.call-done = bf16[4096,1536]{1,0:T(8,128)(2,1)} async-done(((bf16[512,1536]{1,0:T(8,128)(2,1)}), bf16[4096,1536]{1,0:T(8,128)(2,1)}) %all-gather.11.cloned.1.call-update) | async-done | bytes 12582928 | tf_op jit(solution)/shard_map/all_gather | solution.py:100
  947.5 23.0 fusion.192
  970.5 27.7 multiply_reduce_fusion.71
  1011.6 9.5 multiply_reduce_fusion.72
  1048.0 11.9 convolution_convert_fusion.2
  1060.6 1307.8 %while.33 = (s32[]{:T(128)}, bf16[8,2,512,96]{2,3,1,0:T(8,128)(2,1)}, bf16[8,2,512,96]{2,3,1,0:T(8,128)(2,1)}, bf16[8,2,512,96]{2,3,1,0:T(8,128)(2,1)}, f32[8,2,...) while((s32[]{:T(128)}, ...), condition=%wide.region_89.90_spmd.clone.clone, body=%wide.region_14.89_spmd.clone.sunk.clone | while | flops 738697472 | bytes 735251840 | solution.py:179
  1097.4 8.8 fusion.385
  1186.6 10.6 select_convert_fusion.3
  1211.9 10.4 multiply_reduce_fusion.90
  1260.6 8.7 fusion.385
  1349.2 10.4 select_convert_fusion.3
  1365.7 8.5 multiply_reduce_fusion.89
  1374.3 10.4 multiply_reduce_fusion.90
  1423.0 8.7 fusion.385
  1511.5 10.4 select_convert_fusion.3
  1527.9 8.5 multiply_reduce_fusion.89
  1536.5 10.4 multiply_reduce_fusion.90
  1585.2 8.7 fusion.385
  1673.8 10.4 select_convert_fusion.3
  1698.8 10.4 multiply_reduce_fusion.90
  1747.5 8.7 fusion.385
  1836.0 10.4 select_convert_fusion.3
  1852.5 8.5 multiply_reduce_fusion.89
  1861.1 10.4 multiply_reduce_fusion.90
  1909.8 8.7 fusion.385
  1998.3 10.4 select_convert_fusion.3
  2014.8 8.5 multiply_reduce_fusion.89
  2023.4 10.4 multiply_reduce_fusion.90
  2072.1 8.7 fusion.385
  2160.6 10.4 select_convert_fusion.3
  2185.7 10.4 multiply_reduce_fusion.90
  2234.4 8.7 fusion.385
  2322.9 10.4 select_convert_fusion.3
  2339.4 8.5 multiply_reduce_fusion.89
  2348.0 10.4 multiply_reduce_fusion.90
  2368.4 13.8 convolution_convert_fusion.1
  2384.1 24.0 convolution_convert_fusion
  2408.2 201.6 %reduce-scatter.5.cloned.1.call-done = bf16[192,4608]{1,0:T(8,128)(2,1)} async-done(((bf16[1536,4608]{1,0:T(8,128)(2,1)}), bf16[192,4608]{1,0:T(8,128)(2,1)}) %reduce-scatter.5.cloned.1.call-update) | async-done | bytes 1769488 | tf_op jit(solution)/shard_map/reduce_scatter | solution.py:115
  2609.8 406.8 %reduce-scatter.9.cloned.1.call-done = bf16[192,8192]{1,0:T(8,128)(2,1)} async-done(((bf16[1536,8192]{1,0:T(8,128)(2,1)}), bf16[192,8192]{1,0:T(8,128)(2,1)}) %reduce-scatter.9.cloned.1.call-update) | async-done | bytes 3145744 | tf_op jit(solution)/shard_map/reduce_scatter | solution.py:115
  3018.5 15.2 fusion.179
  3033.8 42.1 %all-reduce.114 = (f32[1536]{0:T(1024)}, f32[16,6,11]{2,0,1:T(8,128)S(1)}, f32[8,2,2]{0,2,1:T(2,128)}, f32[1536]{0:T(1024)}, f32[1536]{0:T(1024)}) all-reduce(f32[1536]{0:T(1024)S(1)} %get-tuple-element.353, f32[16,6,11]{2,0,1:T(8,128)S(1)} %bitcast.958, f32[8,2,2]{0,2,1:T(2,128)S(1)} %copy.86, ...), channel_id=1, replica_groups=mesh['rep'=4,'fsdp'=8] {'rep','fsdp'}, use_global_device_ids=true, to_apply=%region_92.93 | all-reduce | flops 5696 | bytes 45568 | tf_op jit(solution)/shard_map/psum | solution.py:260
  3082.3 10.6 fusion.189
  3092.9 59.8 %all-reduce.118.cloned.1.call-done = (bf16[192,4608]{1,0:T(8,128)(2,1)}, bf16[192,1536]{1,0:T(8,128)(2,1)}, bf16[192,8192]{1,0:T(8,128)(2,1)}, bf16[512,1536]{1,0:T(8,128)(2,1)}) async-done(((bf16[192,4608]{1,0:T(8,128)(2,1)}, bf16[192,1536]{1,0:T(8,128)(2,1)}, bf16[192,8192]{1,0:T(8,128)(2,1)}, bf16[512,1536]{1,0:T(8,128)(2,1)}), (bf16[192,4608]{1,0:T(8,128)(2,1)}, bf16[192,1536]{1,0:T(8,128)(2,1)}, ...) | async-done | bytes 7077904 | tf_op jit(solution)/shard_map/psum | solution.py:265
  (2490 shorter events, 1502.3 us)
Async XLA Ops:
  7.2 201.4 %all-gather.5.cloned.1.call-start = ((), (), s32[]{:S(2)}) async-start(), calls=%async_computation.4 | async-start | bytes 15925248 | tf_op jit(solution)/shard_map/all_gather | solution.py:100
  7.9 637.3 %all-gather.7.cloned.1.call-start = ((), (), s32[]{:S(2)}) async-start(), calls=%async_computation.5 | async-start | bytes 5308416 | tf_op jit(solution)/shard_map/all_gather | solution.py:100
  8.7 760.3 %all-gather.9.cloned.1.call-start = ((), (), s32[]{:S(2)}) async-start(), calls=%async_computation.6 | async-start | bytes 28311552 | tf_op jit(solution)/shard_map/all_gather | solution.py:100
  9.4 199.1 %copy-start.132 = (f32[1536]{0:T(1024)S(1)}, f32[1536]{0:T(1024)}, u32[]{:S(2)}) copy-start(f32[1536]{0:T(1024)} %param.17) | copy-start | bytes 18436
  9.4 938.0 %all-gather.11.cloned.1.call-start = ((), (), s32[]{:S(2)}) async-start(), calls=%async_computation.7 | async-start | bytes 14155776 | tf_op jit(solution)/shard_map/all_gather | solution.py:100
  10.0 2398.1 %reduce-scatter.7.cloned.1.call-start = ((), (), s32[]{:S(2)}) async-start(), calls=%async_computation.9 | async-start | bytes 5308416 | tf_op jit(solution)/shard_map/reduce_scatter | solution.py:115
  10.6 208.9 %copy-start.123 = (f32[512]{0:T(512)}, f32[512]{0:T(512)S(1)}, u32[]{:S(2)}) copy-start(f32[512]{0:T(512)S(1)} %fusion.203) | copy-start | bytes 6148
  645.2 123.8 %copy-start.130 = (f32[1536]{0:T(1024)S(1)}, f32[1536]{0:T(1024)}, u32[]{:S(2)}) copy-start(f32[1536]{0:T(1024)} %param.23) | copy-start | bytes 18436
  653.4 344.9 %copy-start.125 = (f32[512]{0:T(512)}, f32[512]{0:T(512)S(1)}, u32[]{:S(2)}) copy-start(f32[512]{0:T(512)S(1)} %fusion.204) | copy-start | bytes 6148
  1008.6 1399.6 %reduce-scatter.11.cloned.1.call-start = ((), (), s32[]{:S(2)}) async-start(), calls=%async_computation.11 | async-start | bytes 14155776 | tf_op jit(solution)/shard_map/reduce_scatter | solution.py:115
  1059.9 1549.9 %reduce-scatter.5.cloned.1.call-start = ((), (), s32[]{:S(2)}) async-start(), calls=%async_computation.8 | async-start | bytes 15925248 | tf_op jit(solution)/shard_map/reduce_scatter | solution.py:115
  1126.5 49.7 %copy-start.15 = (f32[2,512,507]{1,2,0:T(8,128)}, f32[2,512,507]{1,2,0:T(8,128)S(1)}, u32[]{:S(2)}) copy-start(f32[2,512,507]{1,2,0:T(8,128)S(1)} %get-tuple-element.1486) | copy-start | bytes 6230020 | tf_op jit(solution)/shard_map/while
  1126.5 52.7 %copy-start.16 = (f32[2,512,507]{1,2,0:T(8,128)}, f32[2,512,507]{1,2,0:T(8,128)S(1)}, u32[]{:S(2)}) copy-start(f32[2,512,507]{1,2,0:T(8,128)S(1)} %get-tuple-element.1476) | copy-start | bytes 6230020 | tf_op jit(solution)/shard_map/while
  1126.9 52.4 %copy-start.17 = (f32[2,512,508]{1,2,0:T(8,128)}, f32[2,512,508]{1,2,0:T(8,128)S(1)}, u32[]{:S(2)}) copy-start(f32[2,512,508]{1,2,0:T(8,128)S(1)} %get-tuple-element.1477) | copy-start | bytes 6242308 | tf_op jit(solution)/shard_map/while
  1127.9 48.3 %copy-start.10 = (f32[2,512,510]{1,2,0:T(8,128)}, f32[2,512,510]{1,2,0:T(8,128)S(1)}, u32[]{:S(2)}) copy-start(f32[2,512,510]{1,2,0:T(8,128)S(1)} %get-tuple-element.1483) | copy-start | bytes 6266884 | tf_op jit(solution)/shard_map/while
  1127.9 51.4 %copy-start.12 = (f32[2,512,510]{1,2,0:T(8,128)}, f32[2,512,510]{1,2,0:T(8,128)S(1)}, u32[]{:S(2)}) copy-start(f32[2,512,510]{1,2,0:T(8,128)S(1)} %get-tuple-element.1479) | copy-start | bytes 6266884 | tf_op jit(solution)/shard_map/while
  1289.4 49.4 %copy-start.15 = (f32[2,512,507]{1,2,0:T(8,128)}, f32[2,512,507]{1,2,0:T(8,128)S(1)}, u32[]{:S(2)}) copy-start(f32[2,512,507]{1,2,0:T(8,128)S(1)} %get-tuple-element.1486) | copy-start | bytes 6230020 | tf_op jit(solution)/shard_map/while
  1289.4 52.5 %copy-start.16 = (f32[2,512,507]{1,2,0:T(8,128)}, f32[2,512,507]{1,2,0:T(8,128)S(1)}, u32[]{:S(2)}) copy-start(f32[2,512,507]{1,2,0:T(8,128)S(1)} %get-tuple-element.1476) | copy-start | bytes 6230020 | tf_op jit(solution)/shard_map/while
  1289.8 52.1 %copy-start.17 = (f32[2,512,508]{1,2,0:T(8,128)}, f32[2,512,508]{1,2,0:T(8,128)S(1)}, u32[]{:S(2)}) copy-start(f32[2,512,508]{1,2,0:T(8,128)S(1)} %get-tuple-element.1477) | copy-start | bytes 6242308 | tf_op jit(solution)/shard_map/while
  1290.8 48.1 %copy-start.10 = (f32[2,512,510]{1,2,0:T(8,128)}, f32[2,512,510]{1,2,0:T(8,128)S(1)}, u32[]{:S(2)}) copy-start(f32[2,512,510]{1,2,0:T(8,128)S(1)} %get-tuple-element.1483) | copy-start | bytes 6266884 | tf_op jit(solution)/shard_map/while
  1290.8 51.1 %copy-start.12 = (f32[2,512,510]{1,2,0:T(8,128)}, f32[2,512,510]{1,2,0:T(8,128)S(1)}, u32[]{:S(2)}) copy-start(f32[2,512,510]{1,2,0:T(8,128)S(1)} %get-tuple-element.1479) | copy-start | bytes 6266884 | tf_op jit(solution)/shard_map/while
  1451.7 49.4 %copy-start.15 = (f32[2,512,507]{1,2,0:T(8,128)}, f32[2,512,507]{1,2,0:T(8,128)S(1)}, u32[]{:S(2)}) copy-start(f32[2,512,507]{1,2,0:T(8,128)S(1)} %get-tuple-element.1486) | copy-start | bytes 6230020 | tf_op jit(solution)/shard_map/while
  1451.7 52.5 %copy-start.16 = (f32[2,512,507]{1,2,0:T(8,128)}, f32[2,512,507]{1,2,0:T(8,128)S(1)}, u32[]{:S(2)}) copy-start(f32[2,512,507]{1,2,0:T(8,128)S(1)} %get-tuple-element.1476) | copy-start | bytes 6230020 | tf_op jit(solution)/shard_map/while
  1452.1 52.1 %copy-start.17 = (f32[2,512,508]{1,2,0:T(8,128)}, f32[2,512,508]{1,2,0:T(8,128)S(1)}, u32[]{:S(2)}) copy-start(f32[2,512,508]{1,2,0:T(8,128)S(1)} %get-tuple-element.1477) | copy-start | bytes 6242308 | tf_op jit(solution)/shard_map/while
  1453.1 51.1 %copy-start.12 = (f32[2,512,510]{1,2,0:T(8,128)}, f32[2,512,510]{1,2,0:T(8,128)S(1)}, u32[]{:S(2)}) copy-start(f32[2,512,510]{1,2,0:T(8,128)S(1)} %get-tuple-element.1479) | copy-start | bytes 6266884 | tf_op jit(solution)/shard_map/while
  1614.0 49.4 %copy-start.15 = (f32[2,512,507]{1,2,0:T(8,128)}, f32[2,512,507]{1,2,0:T(8,128)S(1)}, u32[]{:S(2)}) copy-start(f32[2,512,507]{1,2,0:T(8,128)S(1)} %get-tuple-element.1486) | copy-start | bytes 6230020 | tf_op jit(solution)/shard_map/while
  1614.0 52.5 %copy-start.16 = (f32[2,512,507]{1,2,0:T(8,128)}, f32[2,512,507]{1,2,0:T(8,128)S(1)}, u32[]{:S(2)}) copy-start(f32[2,512,507]{1,2,0:T(8,128)S(1)} %get-tuple-element.1476) | copy-start | bytes 6230020 | tf_op jit(solution)/shard_map/while
  1614.3 52.1 %copy-start.17 = (f32[2,512,508]{1,2,0:T(8,128)}, f32[2,512,508]{1,2,0:T(8,128)S(1)}, u32[]{:S(2)}) copy-start(f32[2,512,508]{1,2,0:T(8,128)S(1)} %get-tuple-element.1477) | copy-start | bytes 6242308 | tf_op jit(solution)/shard_map/while
  1615.4 51.1 %copy-start.12 = (f32[2,512,510]{1,2,0:T(8,128)}, f32[2,512,510]{1,2,0:T(8,128)S(1)}, u32[]{:S(2)}) copy-start(f32[2,512,510]{1,2,0:T(8,128)S(1)} %get-tuple-element.1479) | copy-start | bytes 6266884 | tf_op jit(solution)/shard_map/while
  1776.3 49.4 %copy-start.15 = (f32[2,512,507]{1,2,0:T(8,128)}, f32[2,512,507]{1,2,0:T(8,128)S(1)}, u32[]{:S(2)}) copy-start(f32[2,512,507]{1,2,0:T(8,128)S(1)} %get-tuple-element.1486) | copy-start | bytes 6230020 | tf_op jit(solution)/shard_map/while
  1776.3 52.5 %copy-start.16 = (f32[2,512,507]{1,2,0:T(8,128)}, f32[2,512,507]{1,2,0:T(8,128)S(1)}, u32[]{:S(2)}) copy-start(f32[2,512,507]{1,2,0:T(8,128)S(1)} %get-tuple-element.1476) | copy-start | bytes 6230020 | tf_op jit(solution)/shard_map/while
  1776.6 52.1 %copy-start.17 = (f32[2,512,508]{1,2,0:T(8,128)}, f32[2,512,508]{1,2,0:T(8,128)S(1)}, u32[]{:S(2)}) copy-start(f32[2,512,508]{1,2,0:T(8,128)S(1)} %get-tuple-element.1477) | copy-start | bytes 6242308 | tf_op jit(solution)/shard_map/while
  1777.6 51.1 %copy-start.12 = (f32[2,512,510]{1,2,0:T(8,128)}, f32[2,512,510]{1,2,0:T(8,128)S(1)}, u32[]{:S(2)}) copy-start(f32[2,512,510]{1,2,0:T(8,128)S(1)} %get-tuple-element.1479) | copy-start | bytes 6266884 | tf_op jit(solution)/shard_map/while
  1938.6 49.4 %copy-start.15 = (f32[2,512,507]{1,2,0:T(8,128)}, f32[2,512,507]{1,2,0:T(8,128)S(1)}, u32[]{:S(2)}) copy-start(f32[2,512,507]{1,2,0:T(8,128)S(1)} %get-tuple-element.1486) | copy-start | bytes 6230020 | tf_op jit(solution)/shard_map/while
  1938.6 52.5 %copy-start.16 = (f32[2,512,507]{1,2,0:T(8,128)}, f32[2,512,507]{1,2,0:T(8,128)S(1)}, u32[]{:S(2)}) copy-start(f32[2,512,507]{1,2,0:T(8,128)S(1)} %get-tuple-element.1476) | copy-start | bytes 6230020 | tf_op jit(solution)/shard_map/while
  1938.9 52.1 %copy-start.17 = (f32[2,512,508]{1,2,0:T(8,128)}, f32[2,512,508]{1,2,0:T(8,128)S(1)}, u32[]{:S(2)}) copy-start(f32[2,512,508]{1,2,0:T(8,128)S(1)} %get-tuple-element.1477) | copy-start | bytes 6242308 | tf_op jit(solution)/shard_map/while
  1940.0 51.1 %copy-start.12 = (f32[2,512,510]{1,2,0:T(8,128)}, f32[2,512,510]{1,2,0:T(8,128)S(1)}, u32[]{:S(2)}) copy-start(f32[2,512,510]{1,2,0:T(8,128)S(1)} %get-tuple-element.1479) | copy-start | bytes 6266884 | tf_op jit(solution)/shard_map/while
  2100.8 49.4 %copy-start.15 = (f32[2,512,507]{1,2,0:T(8,128)}, f32[2,512,507]{1,2,0:T(8,128)S(1)}, u32[]{:S(2)}) copy-start(f32[2,512,507]{1,2,0:T(8,128)S(1)} %get-tuple-element.1486) | copy-start | bytes 6230020 | tf_op jit(solution)/shard_map/while
  2100.8 52.5 %copy-start.16 = (f32[2,512,507]{1,2,0:T(8,128)}, f32[2,512,507]{1,2,0:T(8,128)S(1)}, u32[]{:S(2)}) copy-start(f32[2,512,507]{1,2,0:T(8,128)S(1)} %get-tuple-element.1476) | copy-start | bytes 6230020 | tf_op jit(solution)/shard_map/while
  2101.2 52.1 %copy-start.17 = (f32[2,512,508]{1,2,0:T(8,128)}, f32[2,512,508]{1,2,0:T(8,128)S(1)}, u32[]{:S(2)}) copy-start(f32[2,512,508]{1,2,0:T(8,128)S(1)} %get-tuple-element.1477) | copy-start | bytes 6242308 | tf_op jit(solution)/shard_map/while
  2102.2 51.1 %copy-start.12 = (f32[2,512,510]{1,2,0:T(8,128)}, f32[2,512,510]{1,2,0:T(8,128)S(1)}, u32[]{:S(2)}) copy-start(f32[2,512,510]{1,2,0:T(8,128)S(1)} %get-tuple-element.1479) | copy-start | bytes 6266884 | tf_op jit(solution)/shard_map/while
  2263.1 49.4 %copy-start.15 = (f32[2,512,507]{1,2,0:T(8,128)}, f32[2,512,507]{1,2,0:T(8,128)S(1)}, u32[]{:S(2)}) copy-start(f32[2,512,507]{1,2,0:T(8,128)S(1)} %get-tuple-element.1486) | copy-start | bytes 6230020 | tf_op jit(solution)/shard_map/while
  2263.1 52.5 %copy-start.16 = (f32[2,512,507]{1,2,0:T(8,128)}, f32[2,512,507]{1,2,0:T(8,128)S(1)}, u32[]{:S(2)}) copy-start(f32[2,512,507]{1,2,0:T(8,128)S(1)} %get-tuple-element.1476) | copy-start | bytes 6230020 | tf_op jit(solution)/shard_map/while
  2263.5 52.1 %copy-start.17 = (f32[2,512,508]{1,2,0:T(8,128)}, f32[2,512,508]{1,2,0:T(8,128)S(1)}, u32[]{:S(2)}) copy-start(f32[2,512,508]{1,2,0:T(8,128)S(1)} %get-tuple-element.1477) | copy-start | bytes 6242308 | tf_op jit(solution)/shard_map/while
  2264.5 51.1 %copy-start.12 = (f32[2,512,510]{1,2,0:T(8,128)}, f32[2,512,510]{1,2,0:T(8,128)S(1)}, u32[]{:S(2)}) copy-start(f32[2,512,510]{1,2,0:T(8,128)S(1)} %get-tuple-element.1479) | copy-start | bytes 6266884 | tf_op jit(solution)/shard_map/while
  2382.2 634.3 %reduce-scatter.9.cloned.1.call-start = ((), (), s32[]{:S(2)}) async-start(), calls=%async_computation.10 | async-start | bytes 28311552 | tf_op jit(solution)/shard_map/reduce_scatter | solution.py:115
  2408.1 744.5 %all-reduce.118.cloned.1.call-start = ((), (), s32[]{:S(2)}) async-start(), calls=%async_computation.12 | async-start | bytes 14155776 | tf_op jit(solution)/shard_map/psum | solution.py:265
  3018.5 58.1 %copy-start.122 = (f32[512]{0:T(512)S(1)}, f32[512]{0:T(512)}, u32[]{:S(2)}) copy-start(f32[512]{0:T(512)} %copy-done.121) | copy-start | bytes 6148
  (806 other events, 5978.5 us)
Sparse Core Ops, SparseCore 0:
  10.2 198.3 all-gather.4
  210.7 78.0 all-gather.6
  290.4 478.5 all-gather.8
  771.0 176.3 all-gather.10
  1008.7 93.4 reduce-scatter.6
  1105.6 207.0 reduce-scatter.10
  2382.4 227.3 reduce-scatter.4
  2613.7 402.8 reduce-scatter.8
  3019.2 133.4 all-reduce.117
where the time goes:
time: 3180 us; the launch traced here: 3170 us
  other arithmetic  1470 us (46%)
  waiting for transfers between devices  1140 us (36%)
  matrix products  286 us (9%)
  local copies, waits for them, and re-layouts  192 us (6%)
  blocking collectives  42.1 us (1%)
    reduce_scatter x4, waiting for transfers between devices, weight_grad(): lax.psum_scatter(lax.dot_general(operand, upstream, (((0,), (0,)), ((), (...  608 us
    all_gather x4, waiting for transfers between devices, project(): lax.all_gather(weight, 'fsdp', axis=0, tiled=True)  467 us
    add x160, other arithmetic, score_mix(): partial_sum + shifted[row_shift] * kernel[:, row_shift, column][:, None,...  455 us
    mul x88, other arithmetic, score_mix(): shift_rows(masked, row_shift) * row_keep[row_shift][:, None]  341 us
    reduce_sum x16, other arithmetic, score_mix(): shifted[row_shift] * kernel[:, row_shift, column][:, None, None]  151 us
    add_any x40, other arithmetic, score_mix(): shifted[row_shift] * kernel[:, row_shift, column][:, None, None]  120 us
    convert_element_type x8, other arithmetic, one_group(): d_rounded = d_scores.astype(jnp.bfloat16)  83.2 us
    dot_general x4, matrix products, project_back(): lax.dot_general(upstream, lax.all_gather(weight, 'fsdp', axis=0, tiled=Tr...  75.5 us
  transfers between devices with their start and end apart: 9, of which 6 were waited for; matrix products, arithmetic and copies ran while one was open for 58% of the time, Pallas kernels for 0%

commit v1 on v0

v1 whole, which is shorter than its diff:
```python
import functools, math
import jax, jax.numpy as jnp
from jax import lax
from jax.experimental import pallas as pl
from jax.experimental.pallas import tpu as pltpu
from jax.sharding import PartitionSpec as P

HEADS = 16
HEAD_DIM = 96
CQ = 6
CK = 11
EPSILON = 1e-05
LANE = 128
QUAD = 4
SCALE = 1.0 / math.sqrt(HEAD_DIM)
F32 = jnp.float32
BF16 = jnp.bfloat16


def row_sets(seq):
    return [
        (r, min(r + LANE, 3 * LANE), max(0, r - 2 * LANE)) for r in range(0, seq, LANE)
    ]


def nt(a, b):
    return lax.dot_general(a, b, (((1,), (1,)), ((), ())), preferred_element_type=F32)


def nn(a, b):
    return jnp.dot(a, b, preferred_element_type=F32)


def fill_masks(docs_ref, masks, seq):
    ends = []
    total = jnp.int32(0)
    for d in range(docs_ref.shape[1] - 1):
        total = total + docs_ref[0, d]
        ends.append(total)
    for r0, width, c0 in row_sets(seq):
        rows = r0 + lax.broadcasted_iota(jnp.int32, (LANE, 1), 0)
        cols = c0 + lax.broadcasted_iota(jnp.int32, (1, width), 1)
        row_doc = sum((rows >= e).astype(jnp.int32) for e in ends)
        col_doc = sum((cols >= e).astype(jnp.int32) for e in ends)
        same = row_doc == col_doc
        for a in range(CQ):
            masks[a, r0 : r0 + LANE, :width] = jnp.where(
                same & (rows - cols >= a), 1.0, 0.0
            ).astype(BF16)


def circulant_masks():
    gap = lax.broadcasted_iota(jnp.int32, (LANE, LANE), 1) - lax.broadcasted_iota(
        jnp.int32, (LANE, LANE), 0
    )
    half = CK // 2
    return (jnp.abs(gap) <= half, gap <= half - LANE, gap >= LANE - half)


def circulant(taps):
    wide = jnp.broadcast_to(taps, (LANE, LANE))
    return pltpu.roll(wide, 0, axis=1, stride=1, stride_axis=0)


def fill_toeplitz(taps_ref, head, band, blocks):
    near, after, before = circulant_masks()
    for a in range(CQ):
        whole = circulant(taps_ref[head, a : a + 1, :])
        parts = {
            0: jnp.where(near, whole, 0.0).astype(BF16),
            1: jnp.where(after, whole, 0.0).astype(BF16),
            -1: jnp.where(before, whole, 0.0).astype(BF16),
        }
        for r in range(blocks):
            for c in range(blocks):
                part = parts.get(c - r)
                if part is not None:
                    yield a, r, c, part


def fill_forward_band(taps_ref, head, band):
    for a, r, c, part in fill_toeplitz(taps_ref, head, band, 3):
        at = (r * CQ + a) * LANE
        band[at : at + LANE, c * LANE : (c + 1) * LANE] = part


def fill_backward_band(taps_ref, head, band):
    for a, r, c, part in fill_toeplitz(taps_ref, head, band, 3):
        at = (c * CQ + a) * LANE
        band[r * LANE : (r + 1) * LANE, at : at + LANE] = part


def shifted_rows(query):
    wide = query.astype(F32)
    return [query] + [pltpu.roll(wide, a, axis=0).astype(BF16) for a in range(1, CQ)]


def masked_scores(shifted, keys, masks, r0, width, c0):
    left = jnp.concatenate([shifted[a, r0 : r0 + LANE] for a in range(CQ)], axis=0)
    scores = nt(left, keys[c0 : c0 + width]).astype(BF16)
    return left, [
        scores[a * LANE : (a + 1) * LANE] * masks[a, r0 : r0 + LANE, :width]
        for a in range(CQ)
    ]


def by_window(parts, width):
    return jnp.concatenate(
        [
            parts[a][:, b * LANE : (b + 1) * LANE]
            for b in range(width // LANE)
            for a in range(CQ)
        ],
        axis=1,
    )


def forward_kernel(
    docs_ref, mix_ref, taps_ref, gain_ref, q_ref, k_ref, v_ref,
    grouped_ref, attended_ref, soft_ref,
    masks, band, qs, ks, vs, shifted, outs, normed,
):
    seq = q_ref.shape[0]
    quad = pl.program_id(0)

    @pl.when(quad == 0)
    def _():
        fill_masks(docs_ref, masks, seq)
        band[...] = jnp.zeros_like(band)

    for h in range(QUAD):
        at = slice(h * HEAD_DIM, (h + 1) * HEAD_DIM)
        qs[h] = q_ref[:, at]
        ks[h] = k_ref[:, at]
        vs[h] = v_ref[:, at]

    sets = row_sets(seq)

    def pair(p, carry):
        group = quad * 2 + p
        for r in range(2):
            h = 2 * p + r
            fill_forward_band(taps_ref, quad * QUAD + h, band)
            for a, rows in enumerate(shifted_rows(qs[h])):
                shifted[a] = rows
            keys = ks[h]
            lefts = []
            for r0, width, c0 in sets:
                _, parts = masked_scores(shifted, keys, masks, r0, width, c0)
                lefts.append((width, by_window(parts, width)))
            convs = []
            i = 0
            while i < len(sets):
                width = sets[i][1]
                n = 1
                while i + n < len(sets) and sets[i + n][1] == width:
                    n += 1
                left = jnp.concatenate([lefts[i + m][1] for m in range(n)], axis=0)
                conv = nn(left, band[: width * CQ, :width])
                convs += [conv[m * LANE : (m + 1) * LANE] for m in range(n)]
                i += n
            for (r0, width, c0), conv in zip(sets, convs):
                logits = jnp.where(
                    masks[0, r0 : r0 + LANE, :width].astype(F32) > 0, conv, -1e30
                )
                weights = jnp.exp(logits - jnp.max(logits, axis=1, keepdims=True))
                soft = weights * (1.0 / jnp.sum(weights, axis=1, keepdims=True))
                soft_ref[h, r0 : r0 + LANE, :width] = soft.astype(BF16)
        for r in range(2):
            h = 2 * p + r
            values = vs[h]
            for r0, width, c0 in sets:
                mixed = (
                    mix_ref[group, 2 * r] * soft_ref[2 * p, r0 : r0 + LANE, :width].astype(F32)
                    + mix_ref[group, 2 * r + 1] * soft_ref[2 * p + 1, r0 : r0 + LANE, :width].astype(F32)
                ).astype(BF16)
                outs[h, r0 : r0 + LANE] = nn(mixed, values[c0 : c0 + width])
        return carry

    lax.fori_loop(0, 2, pair, 0)
    wholes, grouped = [], []
    for h in range(QUAD):
        attended = outs[h]
        centred = attended - jnp.mean(attended, axis=1, keepdims=True)
        var = jnp.mean(centred * centred, axis=1, keepdims=True)
        wholes.append(attended)
        grouped.append(centred * lax.rsqrt(var + EPSILON))
    attended_ref[...] = jnp.concatenate(wholes, axis=1)
    grouped_ref[...] = (jnp.concatenate(grouped, axis=1) * gain_ref[...]).astype(BF16)


def pad_taps(kernel):
    padded = jnp.pad(kernel * SCALE, ((0, 0), (0, 2), (0, LANE - CK)))
    return jnp.roll(padded, -(CK // 2), axis=2)


def attend_forward(projected, conv_kernel, head_mixing, docs, gain):
    seq = projected.shape[0]
    width = projected.shape[1] // 3
    block = QUAD * HEAD_DIM
    quads = HEADS // QUAD
    whole = pl.BlockSpec(memory_space=pltpu.VMEM)
    smem = pl.BlockSpec(memory_space=pltpu.SMEM)

    def columns(first):
        return pl.BlockSpec((seq, block), lambda i: (0, first * quads + i))

    return pl.pallas_call(
        forward_kernel,
        grid=(quads,),
        out_shape=[
            jax.ShapeDtypeStruct((seq, width), BF16),
            jax.ShapeDtypeStruct((seq, width), F32),
            jax.ShapeDtypeStruct((HEADS, seq, 3 * LANE), BF16),
        ],
        in_specs=[
            smem, smem, whole,
            pl.BlockSpec((1, block), lambda i: (0, i)),
            columns(0), columns(1), columns(2),
        ],
        out_specs=[
            columns(0), columns(0),
            pl.BlockSpec((QUAD, seq, 3 * LANE), lambda i: (i, 0, 0)),
        ],
        scratch_shapes=[
            pltpu.VMEM((CQ, seq, 3 * LANE), BF16),
            pltpu.VMEM((3 * LANE * CQ, 3 * LANE), BF16),
            pltpu.VMEM((QUAD, seq, HEAD_DIM), BF16),
            pltpu.VMEM((QUAD, seq, HEAD_DIM), BF16),
            pltpu.VMEM((QUAD, seq, HEAD_DIM), BF16),
            pltpu.VMEM((CQ, seq, HEAD_DIM), BF16),
            pltpu.VMEM((QUAD, seq, HEAD_DIM), F32),
            pltpu.VMEM((8, LANE), F32),
        ],
        compiler_params=pltpu.CompilerParams(vmem_limit_bytes=48 * 1024 * 1024),
    )(
        docs, head_mixing.reshape(HEADS // 2, 4), pad_taps(conv_kernel), gain.reshape(1, width),
        projected, projected, projected,
    )


def backward_kernel(
    docs_ref, mix_ref, taps_ref, gain_ref, q_ref, k_ref, v_ref, attended_ref, d_grouped_ref, soft_ref,
    dq_ref, dk_ref, dv_ref, grad_gain_ref, grad_taps_ref, grad_mix_ref,
    masks, band, qs, ks, vs, ds, shifted, d_heads, d_rows, d_cols, diagonal,
):
    seq = q_ref.shape[0]
    quad = pl.program_id(0)

    @pl.when(quad == 0)
    def _():
        fill_masks(docs_ref, masks, seq)
        band[...] = jnp.zeros_like(band)

    gains = []
    for h in range(QUAD):
        at = slice(h * HEAD_DIM, (h + 1) * HEAD_DIM)
        qs[h] = q_ref[:, at]
        ks[h] = k_ref[:, at]
        vs[h] = v_ref[:, at]
        attended = attended_ref[:, at]
        d_grouped = d_grouped_ref[:, at]
        centred = attended - jnp.mean(attended, axis=1, keepdims=True)
        var = jnp.mean(centred * centred, axis=1, keepdims=True)
        scale = lax.rsqrt(var + EPSILON)
        unit = centred * scale
        gains.append(jnp.sum(d_grouped * unit, axis=0, keepdims=True))
        w = d_grouped * gain_ref[:, at]
        d_attended = scale * (
            w
            - jnp.mean(w, axis=1, keepdims=True)
            - unit * jnp.mean(w * unit, axis=1, keepdims=True)
        )
        ds[h] = d_attended.astype(BF16)
    grad_gain_ref[...] = jnp.concatenate(gains, axis=1)

    sets = row_sets(seq)
    up = lax.broadcasted_iota(jnp.int32, (LANE, LANE), 0)
    across = lax.broadcasted_iota(jnp.int32, (LANE, LANE), 1)
    flip = jnp.where(up + across == LANE - 1, 1.0, 0.0).astype(BF16)
    gap = up + across - (LANE - 1)
    keeps = {0: jnp.abs(gap) <= CK // 2, 1: gap <= CK // 2 - LANE, -1: gap >= LANE - CK // 2}

    def pair(p, carry):
        group = quad * 2 + p
        mix = [[mix_ref[group, 2 * r + s] for s in range(2)] for r in range(2)]
        upstream_t = [ds[2 * p + r].T for r in range(2)]
        grad_mix = [[jnp.zeros((1, 1), F32) for _ in range(2)] for _ in range(2)]
        for r in range(2):
            d_cols[r] = jnp.zeros_like(d_cols[r])
        for r0, width, c0 in sets:
            rows = slice(r0, r0 + LANE)
            soft = [soft_ref[2 * p + s, rows, :width].astype(F32) for s in range(2)]
            d_prob, sums = [], []
            for r in range(2):
                dp = nt(ds[2 * p + r, rows], vs[2 * p + r, c0 : c0 + width])
                d_prob.append(dp)
                sums.append([jnp.sum(dp * soft[s], axis=1, keepdims=True) for s in range(2)])
                for s in range(2):
                    grad_mix[r][s] += jnp.sum(sums[r][s], axis=0, keepdims=True)
                mixed = (mix[r][0] * soft[0] + mix[r][1] * soft[1]).astype(BF16)
                d_cols[r, :, c0 : c0 + width] += nn(upstream_t[r][:, r0 : r0 + LANE], mixed)
            for s in range(2):
                d_soft = mix[0][s] * d_prob[0] + mix[1][s] * d_prob[1]
                inner = mix[0][s] * sums[0][s] + mix[1][s] * sums[1][s]
                d_conv = soft[s] * (d_soft - inner)
                d_rows[s, rows, :width] = d_conv.astype(BF16)
        lane = lax.broadcasted_iota(jnp.int32, (1, LANE), 1)
        line = jnp.zeros((1, LANE), F32)
        for r in range(2):
            for s in range(2):
                line = line + jnp.where(lane == 2 * r + s, grad_mix[r][s], 0.0)
        grad_mix_ref[0, pl.ds(p, 1), :] = line
        for r in range(2):
            d_heads[2, 2 * p + r] = d_cols[r].T

        for r in range(2):
            h = 2 * p + r
            fill_backward_band(taps_ref, quad * QUAD + h, band)
            for a, moved in enumerate(shifted_rows(qs[h])):
                shifted[a] = moved
            keys = ks[h]
            d_cols[0] = jnp.zeros_like(d_cols[0])
            diagonal[...] = jnp.zeros_like(diagonal)
            d_query = []
            for r0, width, c0 in sets:
                rows = slice(r0, r0 + LANE)
                left, parts = masked_scores(shifted, keys, masks, r0, width, c0)
                d_conv = d_rows[r, rows, :width]
                blocks = width // LANE
                flipped = jnp.concatenate(
                    [
                        nt(flip, d_conv[:, b * LANE : (b + 1) * LANE]).astype(BF16)
                        for b in range(blocks)
                    ],
                    axis=0,
                )
                taken = nn(flipped, by_window(parts, width))
                for a in range(CQ):
                    total = diagonal[a]
                    for jb in range(blocks):
                        for qb in range(blocks):
                            if abs(jb - qb) > 1:
                                continue
                            at = (qb * CQ + a) * LANE
                            one = taken[jb * LANE : (jb + 1) * LANE, at : at + LANE]
                            total = total + jnp.where(keeps[qb - jb], one, 0.0)
                    diagonal[a] = total
                spread = nn(d_conv, band[:width, : width * CQ]).astype(BF16)
                stacked = jnp.concatenate(
                    [
                        jnp.concatenate(
                            [
                                spread[:, (b * CQ + a) * LANE : (b * CQ + a + 1) * LANE]
                                for b in range(blocks)
                            ],
                            axis=1,
                        )
                        * masks[a, rows, :width]
                        for a in range(CQ)
                    ],
                    axis=0,
                )
                d_query.append(nn(stacked, keys[c0 : c0 + width]))
                d_cols[0, :, c0 : c0 + width] += nn(left.T, stacked)
            total = None
            for a in range(CQ):
                whole = jnp.concatenate([d[a * LANE : (a + 1) * LANE] for d in d_query], axis=0)
                if a:
                    whole = pltpu.roll(whole, seq - a, axis=0)
                total = whole if total is None else total + whole
            d_heads[0, h] = total
            d_heads[1, h] = d_cols[0].T
            for a in range(CQ):
                aligned = pltpu.roll(diagonal[a], 0, axis=1, stride=1, stride_axis=0)
                grad_taps_ref[h, a : a + 1, :] = jnp.sum(aligned, axis=0, keepdims=True)
        return carry

    lax.fori_loop(0, 2, pair, 0)
    for out, n in ((dq_ref, 0), (dk_ref, 1), (dv_ref, 2)):
        out[...] = jnp.concatenate([d_heads[n, h] for h in range(QUAD)], axis=1).astype(BF16)


def attend_backward(projected, conv_kernel, head_mixing, docs, gain, attended, d_grouped, soft):
    seq = projected.shape[0]
    width = projected.shape[1] // 3
    block = QUAD * HEAD_DIM
    quads = HEADS // QUAD
    whole = pl.BlockSpec(memory_space=pltpu.VMEM)
    smem = pl.BlockSpec(memory_space=pltpu.SMEM)

    def columns(first):
        return pl.BlockSpec((seq, block), lambda i: (0, first * quads + i))

    dq, dk, dv, grad_gain, grad_taps, grad_mix = pl.pallas_call(
        backward_kernel,
        grid=(quads,),
        out_shape=[
            jax.ShapeDtypeStruct((seq, width), BF16),
            jax.ShapeDtypeStruct((seq, width), BF16),
            jax.ShapeDtypeStruct((seq, width), BF16),
            jax.ShapeDtypeStruct((1, width), F32),
            jax.ShapeDtypeStruct((HEADS, 8, LANE), F32),
            jax.ShapeDtypeStruct((quads, 8, LANE), F32),
        ],
        in_specs=[
            smem, smem, whole,
            pl.BlockSpec((1, block), lambda i: (0, i)),
            columns(0), columns(1), columns(2), columns(0), columns(0),
            pl.BlockSpec((QUAD, seq, 3 * LANE), lambda i: (i, 0, 0)),
        ],
        out_specs=[
            columns(0), columns(0), columns(0),
            pl.BlockSpec((1, block), lambda i: (0, i)),
            pl.BlockSpec((QUAD, 8, LANE), lambda i: (i, 0, 0)),
            pl.BlockSpec((1, 8, LANE), lambda i: (i, 0, 0)),
        ],
        scratch_shapes=[
            pltpu.VMEM((CQ, seq, 3 * LANE), BF16),
            pltpu.VMEM((3 * LANE, 3 * LANE * CQ), BF16),
            pltpu.VMEM((QUAD, seq, HEAD_DIM), BF16),
            pltpu.VMEM((QUAD, seq, HEAD_DIM), BF16),
            pltpu.VMEM((QUAD, seq, HEAD_DIM), BF16),
            pltpu.VMEM((QUAD, seq, HEAD_DIM), BF16),
            pltpu.VMEM((CQ, seq, HEAD_DIM), BF16),
            pltpu.VMEM((3, QUAD, seq, HEAD_DIM), F32),
            pltpu.VMEM((2, seq, 3 * LANE), BF16),
            pltpu.VMEM((2, HEAD_DIM, seq), F32),
            pltpu.VMEM((CQ, LANE, LANE), F32),
        ],
        compiler_params=pltpu.CompilerParams(vmem_limit_bytes=56 * 1024 * 1024),
    )(
        docs, head_mixing.reshape(HEADS // 2, 4), pad_taps(conv_kernel[:, :, ::-1]), gain.reshape(1, width),
        projected, projected, projected, attended, d_grouped, soft,
    )
    return (
        dq, dk, dv, grad_gain.reshape(width),
        jnp.roll(grad_taps, CK // 2 + 1, axis=2)[:, :CQ, :CK][:, :, ::-1] * SCALE,
        grad_mix[:, :2, :4].reshape(HEADS // 2, 2, 2),
    )


def rms_norm(values, gains):
    return values * lax.rsqrt(jnp.mean(values * values, axis=-1, keepdims=True) + EPSILON) * gains


def swiglu(gate_up):
    middle_col = gate_up.shape[1] // 2
    return jax.nn.silu(gate_up[:, :middle_col]) * gate_up[:, middle_col:]


def project(operand, weight):
    return jnp.dot(
        operand,
        lax.all_gather(weight, "fsdp", axis=0, tiled=True),
        preferred_element_type=jnp.float32,
    )


def project_back(upstream, weight):
    return lax.dot_general(
        upstream,
        lax.all_gather(weight, "fsdp", axis=0, tiled=True),
        (((1,), (1,)), ((), ())),
        preferred_element_type=jnp.float32,
    )


def weight_grad(operand, upstream):
    return lax.psum_scatter(
        lax.dot_general(
            operand, upstream, (((0,), (0,)), ((), ())), preferred_element_type=jnp.float32
        ).astype(jnp.bfloat16),
        "fsdp",
        scatter_dimension=0,
        tiled=True,
    ).astype(jnp.float32)


def body(
    layer_input,
    first_gain,
    qkv_weight,
    conv_kernel,
    head_mixing,
    group_gain,
    out_weight,
    second_gain,
    inner_weight,
    down_weight,
    doc_lengths,
    cotangent,
):
    inputs = layer_input.astype(jnp.float32)
    normed_value, first_pull = jax.vjp(rms_norm, inputs, first_gain)
    normed = normed_value.astype(jnp.bfloat16)
    projected = project(normed, qkv_weight).astype(jnp.bfloat16)
    grouped, attended, soft = attend_forward(
        projected, conv_kernel, head_mixing, doc_lengths, group_gain
    )
    middle = inputs + project(grouped, out_weight)
    second_value, second_pull = jax.vjp(rms_norm, middle, second_gain)
    second = second_value.astype(jnp.bfloat16)
    gate_up = project(second, inner_weight)
    hidden_value, swiglu_pull = jax.vjp(swiglu, gate_up)
    hidden = hidden_value.astype(jnp.bfloat16)
    layer_output = (middle + project(hidden, down_weight)).astype(jnp.bfloat16)
    upstream = cotangent.astype(jnp.float32)
    grad_down = weight_grad(hidden, cotangent)
    d_hidden = project_back(cotangent, down_weight)
    d_gate_up = swiglu_pull(d_hidden)[0].astype(jnp.bfloat16)
    grad_inner = weight_grad(second, d_gate_up)
    d_second = project_back(d_gate_up, inner_weight)
    d_middle, grad_second = second_pull(d_second)
    d_middle = upstream + d_middle
    d_branch = d_middle.astype(jnp.bfloat16)
    grad_proj = weight_grad(grouped, d_branch)
    d_grouped = project_back(d_branch, out_weight)
    d_query, d_keys, d_values, grad_group, grad_kernel, grad_mixing = attend_backward(
        projected, conv_kernel, head_mixing, doc_lengths, group_gain, attended, d_grouped, soft
    )
    d_projected = jnp.concatenate([d_query, d_keys, d_values], axis=1)
    grad_qkv = weight_grad(normed, d_projected)
    d_normed = project_back(d_projected, qkv_weight)
    d_inputs, grad_first = first_pull(d_normed)
    grad_input = d_middle + d_inputs
    small = lax.psum(
        (grad_first, grad_kernel, grad_mixing, grad_group, grad_second), ("rep", "fsdp")
    )
    shards = (grad_qkv, grad_proj, grad_inner, grad_down)
    shards = (
        lax.psum(shards[0].astype(jnp.bfloat16), "rep").astype(jnp.float32),
        lax.psum(shards[1].astype(jnp.bfloat16), "rep").astype(jnp.float32),
        lax.psum(shards[2].astype(jnp.bfloat16), "rep").astype(jnp.float32),
        lax.psum(shards[3].astype(jnp.bfloat16), "rep").astype(jnp.float32),
    )
    return (
        layer_output,
        grad_input,
        small[0],
        shards[0],
        small[1],
        small[2],
        small[3],
        shards[1],
        small[4],
        shards[2],
        shards[3],
    )


def solution(mesh):
    placed = (
        P(("rep", "fsdp"), None),
        P(),
        P("fsdp", None),
        P(),
        P(),
        P(),
        P("fsdp", None),
        P(),
        P("fsdp", None),
        P("fsdp", None),
        P(("rep", "fsdp"), None),
        P(("rep", "fsdp"), None),
    )
    return jax.shard_map(
        body,
        mesh=mesh,
        in_specs=placed,
        out_specs=(
            P(("rep", "fsdp"), None),
            P(("rep", "fsdp"), None),
            P(),
            P("fsdp", None),
            P(),
            P(),
            P(),
            P("fsdp", None),
            P(),
            P("fsdp", None),
            P("fsdp", None),
        ),
        check_vma=False,
    )
```

time: 3180 us -> 2110 us (0.66)
  other arithmetic: 1470 us -> 21.6 us
  waiting for transfers between devices: 1140 us -> 1690 us
  local copies, waits for them, and re-layouts: 192 us -> 13 us
  Pallas kernels: 0 us -> 147 us
  matrix products: 286 us -> 173 us
    add x161 -> x0, other arithmetic: 455 us -> none  [the longest x160 455 us: score_mix(): partial_sum + shifted[row_shift] * kernel[:, row_shift, column][:, None,...]
    mul x97 -> x3, other arithmetic: 389 us -> 0.03 us  [the longest x2 0.02 us: pad_taps(): padded = jnp.pad(kernel * SCALE, ((0, 0), (0, 2), (0, LANE - CK)))]
    all_gather x4, waiting for transfers between devices: 467 us -> 852 us  [project(): lax.all_gather(weight, 'fsdp', axis=0, tiled=True)]
    reduce_sum x61 -> x0, other arithmetic: 233 us -> none  [the longest x16 151 us: score_mix(): shifted[row_shift] * kernel[:, row_shift, column][:, None, None]]
    reduce_scatter x4, waiting for transfers between devices: 608 us -> 776 us  [weight_grad(): lax.psum_scatter(lax.dot_general(operand, upstream, (((0,), (0,)), ((), (...]
    pallas_call x0 -> x2, Pallas kernels: none -> 147 us  [the longest x1 107 us: attend_backward(): pl.pallas_call(backward_kernel, grid=(quads,), out_shape=[jax.ShapeDtypeS...]
    add_any x40 -> x0, other arithmetic: 120 us -> none  [score_mix(): shifted[row_shift] * kernel[:, row_shift, column][:, None, None]]
    dot_general x56 -> x0, matrix products: 105 us -> none  [the longest x16 26.4 us: one_group(): jnp.einsum('hid,hjd->hij', q_group, k_group, preferred_element_type=jnp.f...]
  transfers between devices with their start and end apart: 9 -> 9, of which waited for: 6 -> 8; matrix products, arithmetic and copies ran while one was open for 58% -> 6% of each run, Pallas kernels for 0% -> 7%
where the time goes in v1:
time: 2110 us; the launch traced here: 2100 us
  waiting for transfers between devices  1690 us (80%)
  matrix products  173 us (8%)
  Pallas kernels  147 us (7%)
  blocking collectives  42.1 us (2%)
  other arithmetic  21.6 us (1%)
    all_gather x4, waiting for transfers between devices, project(): lax.all_gather(weight, 'fsdp', axis=0, tiled=True)  852 us
    reduce_scatter x4, waiting for transfers between devices, weight_grad(): lax.psum_scatter(lax.dot_general(operand, upstream, (((0,), (0,)), ((), (...  776 us
    pallas_call x1, Pallas kernels, attend_backward(): pl.pallas_call(backward_kernel, grid=(quads,), out_shape=[jax.ShapeDtypeS...  107 us
    dot_general x4, matrix products, project_back(): lax.dot_general(upstream, lax.all_gather(weight, 'fsdp', axis=0, tiled=Tr...  68.7 us
    psum x1, waiting for transfers between devices, body(): lax.psum(shards[0].astype(jnp.bfloat16), 'rep').astype(jnp.float32)  62 us
    dot_general x4, matrix products, project(): jnp.dot(operand, lax.all_gather(weight, 'fsdp', axis=0, tiled=True), pref...  54.1 us
    dot_general x4, matrix products, weight_grad(): lax.dot_general(operand, upstream, (((0,), (0,)), ((), ())), preferred_el...  50.1 us
  transfers between devices with their start and end apart: 9, of which 8 were waited for; matrix products, arithmetic and copies ran while one was open for 6% of the time, Pallas kernels for 7%

profile of v1, /device:TPU:0, one launch (start us, length us, event | category | flops | bytes accessed | tf_op | source)
XLA Modules:
  0.0 2103.7 jit_solution(12010346595390996070)
XLA Ops:
  7.3 0.7 all-gather.5.cloned.1.call-update
  8.0 0.7 all-gather.7.cloned.1.call-update
  8.8 0.7 all-gather.9.cloned.1.call-update
  9.5 0.5 all-gather.11.cloned.1.call-update
  10.2 0.1 copy.29
  10.5 0.4 fusion.9
  10.9 0.5 copy-done.17
  11.5 197.1 %all-gather.5.cloned.1.call-done = bf16[1536,4608]{1,0:T(8,128)(2,1)} async-done(((bf16[192,4608]{1,0:T(8,128)(2,1)}), bf16[1536,4608]{1,0:T(8,128)(2,1)}) %all-gather.5.cloned.1.call-update) | async-done | bytes 14155792 | tf_op jit(solution)/shard_map/all_gather | solution.py:455
  208.6 14.2 convolution_convert_fusion.4.q_ref.k_ref.v_ref
  222.8 39.3 %shard_map.203 = (bf16[512,1536]{1,0:T(8,128)(2,1)S(1)}, f32[512,1536]{1,0:T(8,128)S(1)}, bf16[16,512,384]{2,1,0:T(8,128)(2,1)}) custom-call(s32[1,4]{1,0:T(1,128)S(1)} %copy-done.3, f32[8,4]{1,0:T(8,128)S(1)} %copy.30.mix_ref, f32[16,8,128]{2,1,0:T(8,128)S(1)} %pad_maximum_fusion.1.taps_ref, f32[1,1536]{1,0:T(1,128)S(1)} %reshape.77.gain_ref, ...), custom_call_target="tpu_custom_call" | custom-call | tf_op jit(solution)/shard_map/pallas_call | solution.py:208
  262.2 1.7 copy-done
  263.8 25.0 %all-gather.7.cloned.1.call-done = bf16[1536,1536]{1,0:T(8,128)(2,1)} async-done(((bf16[192,1536]{1,0:T(8,128)(2,1)}), bf16[1536,1536]{1,0:T(8,128)(2,1)}) %all-gather.7.cloned.1.call-update) | async-done | bytes 4718608 | tf_op jit(solution)/shard_map/all_gather | solution.py:455
  288.9 6.6 multiply_reduce_fusion.2
  295.5 473.5 %all-gather.9.cloned.1.call-done = bf16[1536,8192]{1,0:T(8,128)(2,1)} async-done(((bf16[192,8192]{1,0:T(8,128)(2,1)}), bf16[1536,8192]{1,0:T(8,128)(2,1)}) %all-gather.9.cloned.1.call-update) | async-done | bytes 25165840 | tf_op jit(solution)/shard_map/all_gather | solution.py:455
  769.0 22.5 %fusion.23 = f32[512,8192]{1,0:T(8,128)} fusion(bf16[1536,8192]{1,0:T(8,128)(2,1)} %all-gather.9.cloned.1.call-done, f32[512,1536]{1,0:T(8,128)} %get-tuple-element.68, f32[1536]{0:T(1024)S(1)} %copy-done.20, f32[512]{0:T(512)S(1)} %fusion.20), kind=kOutput, calls=%fused_computation.59 | convolution fusion | flops 12887261184 | bytes 45096960 | tf_op jit(solution)/shard_map/dot_general | solution.py:453
  791.5 156.0 %all-gather.11.cloned.1.call-done = bf16[4096,1536]{1,0:T(8,128)(2,1)} async-done(((bf16[512,1536]{1,0:T(8,128)(2,1)}), bf16[4096,1536]{1,0:T(8,128)(2,1)}) %all-gather.11.cloned.1.call-update) | async-done | bytes 12582928 | tf_op jit(solution)/shard_map/all_gather | solution.py:455
  947.5 21.1 %fusion.13 = (f32[512,4096]{1,0:T(8,128)}, f32[512,4096]{1,0:T(8,128)}, bf16[512,4096]{1,0:T(8,128)(2,1)}) fusion(f32[512,8192]{1,0:T(8,128)} %fusion.23, bf16[512,1536]{1,0:T(8,128)(2,1)S(1)} %copy-done.13, bf16[4096,1536]{1,0:T(8,128)(2,1)} %all-gather.11.cloned.1.call-done), kind=kOutput, calls=%fused_computation.34 | convolution fusion | flops 6471811072 | bytes 51904512 | tf_op jit(solution)/shard_map/dot_general | solution.py:461
  968.6 27.1 %multiply_reduce_fusion = (f32[1536]{0:T(1024)S(1)}, f32[512]{0:T(512)S(1)}, f32[512,1536]{1,0:T(8,128)}) fusion(f32[512,1536]{1,0:T(8,128)} %get-tuple-element.68, f32[512]{0:T(512)S(1)} %fusion.20, f32[1536]{0:T(1024)S(1)} %copy-done.20, bf16[1536,8192]{1,0:T(8,128)(2,1)} %all-gather.9.cloned.1.call-done, f32[512,4096]{1,0:T(8,128)} %get-tuple-element.65, ...), kind=kOutput, calls=%fused_computation.28 | convolution fusion | flops 12898007040 | bytes 48250880 | tf_op jit(solution)/shard_map/dot_general | solution.py:461
  995.7 3.6 fusion.7
  999.4 1.7 copy-done.4
  1001.0 4.3 convolution_convert_fusion.3
  1005.4 12.1 convolution_convert_fusion.2
  1017.7 0.7 pad_maximum_fusion.2.taps_ref
  1018.4 0.9 copy-done.5
  1019.4 6.7 fusion.15.d_grouped_ref
  1026.0 107.5 %shard_map.204 = (bf16[512,1536]{1,0:T(8,128)(2,1)}, bf16[512,1536]{1,0:T(8,128)(2,1)}, bf16[512,1536]{1,0:T(8,128)(2,1)}, f32[1,1536]{1,0:T(1,128)}, f32[16,8,128]{2,1,0:T(8,128)}, /*index=5*/f32[4,8,128]{2,1,0:T(8,128)}) custom-call(s32[1,4]{1,0:T(1,128)} %docs_ref.3, f32[8,4]{1,0:T(8,128)} %copy-done.2, f32[16,8,128]{2,1,0:T(8,128)} %pad_maximum_fusion.2.taps_ref, ...), custom_call_target="tpu_custom_call" | custom-call | tf_op jit(solution)/shard_map/pallas_call | solution.py:395
  1133.6 1.7 constant_dynamic-update-slice_fusion.2
  1135.2 0.2 copy-done.11
  1135.5 0.4 copy-done.10
  1136.1 2.2 copy-done.14
  1138.3 10.4 convolution_convert_fusion.1
  1148.8 23.3 %convolution_convert_fusion = bf16[1536,8192]{1,0:T(8,128)(2,1)} fusion(f32[512,4096]{1,0:T(8,128)} %get-tuple-element.65, f32[512,4096]{1,0:T(8,128)} %get-tuple-element.64, f32[512,1536]{1,0:T(8,128)} %get-tuple-element.68, f32[1536]{0:T(1024)S(1)} %copy-done.20, f32[512]{0:T(512)S(1)} %fusion.20), kind=kOutput, calls=%fused_computation | convolution fusion | flops 12908232704 | bytes 45096960 | tf_op jit(solution)/shard_map/dot_general | solution.py:471
  1172.2 137.3 %reduce-scatter.11.cloned.1.call-done = bf16[512,1536]{1,0:T(8,128)(2,1)} async-done(((bf16[4096,1536]{1,0:T(8,128)(2,1)}), bf16[512,1536]{1,0:T(8,128)(2,1)}) %reduce-scatter.11.cloned.1.call-update) | async-done | bytes 1572880 | tf_op jit(solution)/shard_map/reduce_scatter | solution.py:470
  1309.5 231.9 %reduce-scatter.5.cloned.1.call-done = bf16[192,4608]{1,0:T(8,128)(2,1)} async-done(((bf16[1536,4608]{1,0:T(8,128)(2,1)}), bf16[192,4608]{1,0:T(8,128)(2,1)}) %reduce-scatter.5.cloned.1.call-update) | async-done | bytes 1769488 | tf_op jit(solution)/shard_map/reduce_scatter | solution.py:470
  1541.4 406.8 %reduce-scatter.9.cloned.1.call-done = bf16[192,8192]{1,0:T(8,128)(2,1)} async-done(((bf16[1536,8192]{1,0:T(8,128)(2,1)}), bf16[192,8192]{1,0:T(8,128)(2,1)}) %reduce-scatter.9.cloned.1.call-update) | async-done | bytes 3145744 | tf_op jit(solution)/shard_map/reduce_scatter | solution.py:470
  1948.3 13.8 fusion.6
  1962.0 0.7 slice.43
  1963.3 42.1 %all-reduce.4 = (f32[1536]{0:T(1024)}, f32[16,6,11]{2,1,0:T(8,128)S(1)}, f32[8,2,2]{0,2,1:T(2,128)}, f32[1536]{0:T(1024)}, f32[1536]{0:T(1024)}) all-reduce(f32[1536]{0:T(1024)S(1)} %get-tuple-element.53, f32[16,6,11]{2,1,0:T(8,128)S(1)} %broadcast_multiply_fusion, ...), channel_id=1, replica_groups=mesh['rep'=4,'fsdp'=8] {'rep','fsdp'}, use_global_device_ids=true, to_apply=%region_5.6 | all-reduce | flops 5696 | bytes 45568 | tf_op jit(solution)/shard_map/psum | solution.py:527
  2005.4 0.7 copy.34
  2006.2 5.1 fusion.8
  2011.3 0.3 copy-done.24
  2011.5 10.7 fusion.11
  2022.3 62.0 %all-reduce.8.cloned.1.call-done = (bf16[192,4608]{1,0:T(8,128)(2,1)}, bf16[192,1536]{1,0:T(8,128)(2,1)}, bf16[192,8192]{1,0:T(8,128)(2,1)}, bf16[512,1536]{1,0:T(8,128)(2,1)}) async-done(((bf16[192,4608]{1,0:T(8,128)(2,1)}, bf16[192,1536]{1,0:T(8,128)(2,1)}, bf16[192,8192]{1,0:T(8,128)(2,1)}, bf16[512,1536]{1,0:T(8,128)(2,1)}), (bf16[192,4608]{1,0:T(8,128)(2,1)}, bf16[192,1536]{1,0:T(8,128)(2,1)}, ...) | async-done | bytes 7077904 | tf_op jit(solution)/shard_map/psum | solution.py:532
  2084.3 2.3 convert_element_type.74
  2086.6 3.7 convert_element_type.72
  2090.3 2.1 convert_element_type.78
  2092.3 0.9 copy-done.9
  2093.3 3.4 convert_element_type.76
  (79 shorter events, 1.7 us)
Async XLA Ops:
  7.2 2.9 copy-start.23
  7.2 3.0 copy-start.19
  7.2 3.0 copy-start.16
  7.2 201.4 %all-gather.5.cloned.1.call-start = ((), (), s32[]{:S(2)}) async-start(), calls=%async_computation.4 | async-start | bytes 15925248 | tf_op jit(solution)/shard_map/all_gather | solution.py:455
  7.9 2.6 copy-start.6
  8.0 280.9 %all-gather.7.cloned.1.call-start = ((), (), s32[]{:S(2)}) async-start(), calls=%async_computation.5 | async-start | bytes 5308416 | tf_op jit(solution)/shard_map/all_gather | solution.py:455
  8.7 199.9 %copy-start.21 = (f32[1536]{0:T(1024)S(1)}, f32[1536]{0:T(1024)}, u32[]{:S(2)}) copy-start(f32[1536]{0:T(1024)} %param.13) | copy-start | bytes 18436
  8.7 760.3 %all-gather.9.cloned.1.call-start = ((), (), s32[]{:S(2)}) async-start(), calls=%async_computation.6 | async-start | bytes 28311552 | tf_op jit(solution)/shard_map/all_gather | solution.py:455
  9.4 938.0 %all-gather.11.cloned.1.call-start = ((), (), s32[]{:S(2)}) async-start(), calls=%async_computation.7 | async-start | bytes 14155776 | tf_op jit(solution)/shard_map/all_gather | solution.py:455
  10.0 1162.2 %reduce-scatter.7.cloned.1.call-start = ((), (), s32[]{:S(2)}) async-start(), calls=%async_computation.9 | async-start | bytes 5308416 | tf_op jit(solution)/shard_map/reduce_scatter | solution.py:470
  10.2 212.6 %copy-start.2 = (f32[8,4]{1,0:T(8,128)}, f32[8,4]{1,0:T(8,128)S(1)}, u32[]{:S(2)}) copy-start(f32[8,4]{1,0:T(8,128)S(1)} %copy.30.mix_ref) | copy-start | bytes 388
  10.2 212.6 %copy-start.1 = (f32[1,1536]{1,0:T(1,128)}, f32[1,1536]{1,0:T(1,128)S(1)}, u32[]{:S(2)}) copy-start(f32[1,1536]{1,0:T(1,128)S(1)} %reshape.77.gain_ref) | copy-start | bytes 18436
  10.9 0.5 copy-start.17
  11.5 211.3 %copy-start.3 = (s32[1,4]{1,0:T(1,128)S(1)}, s32[1,4]{1,0:T(1,128)}, u32[]{:S(2)}) copy-start(s32[1,4]{1,0:T(1,128)} %docs_ref.3) | copy-start | bytes 52
  262.1 1.7 copy-start
  288.9 480.2 %copy-start.20 = (f32[1536]{0:T(1024)S(1)}, f32[1536]{0:T(1024)}, u32[]{:S(2)}) copy-start(f32[1536]{0:T(1024)} %param.19) | copy-start | bytes 18436
  769.0 178.5 %copy-start.13 = (bf16[512,1536]{1,0:T(8,128)(2,1)S(1)}, bf16[512,1536]{1,0:T(8,128)(2,1)}, u32[]{:S(2)}) copy-start(bf16[512,1536]{1,0:T(8,128)(2,1)} %param.23) | copy-start | bytes 4718596
  999.4 1.7 copy-start.4
  1005.3 304.2 %reduce-scatter.11.cloned.1.call-start = ((), (), s32[]{:S(2)}) async-start(), calls=%async_computation.11 | async-start | bytes 14155776 | tf_op jit(solution)/shard_map/reduce_scatter | solution.py:470
  1017.4 1.9 copy-start.5
  1017.5 524.0 %reduce-scatter.5.cloned.1.call-start = ((), (), s32[]{:S(2)}) async-start(), calls=%async_computation.8 | async-start | bytes 15925248 | tf_op jit(solution)/shard_map/reduce_scatter | solution.py:470
  1133.5 1.9 copy-start.11
  1133.5 2.4 copy-start.10
  1135.4 2.8 copy-start.7
  1136.1 2.2 copy-start.14
  1148.7 799.5 %reduce-scatter.9.cloned.1.call-start = ((), (), s32[]{:S(2)}) async-start(), calls=%async_computation.10 | async-start | bytes 28311552 | tf_op jit(solution)/shard_map/reduce_scatter | solution.py:470
  1172.1 912.2 %all-reduce.8.cloned.1.call-start = ((), (), s32[]{:S(2)}) async-start(), calls=%async_computation.12 | async-start | bytes 14155776 | tf_op jit(solution)/shard_map/psum | solution.py:532
  1948.2 14.7 copy-start.15
  1948.2 15.0 copy-start.22
  1948.2 57.9 %copy-start.18 = (f32[512]{0:T(512)S(1)}, f32[512]{0:T(512)}, u32[]{:S(2)}) copy-start(f32[512]{0:T(512)} %copy-done.17) | copy-start | bytes 6148
  2006.2 5.1 copy-start.8
  2006.2 5.4 copy-start.24
  2084.3 6.0 copy-start.12
  2090.3 3.0 copy-start.9
Sparse Core Ops, SparseCore 0:
  10.2 198.3 all-gather.4
  210.8 78.0 all-gather.6
  290.4 478.5 all-gather.8
  771.1 176.3 all-gather.10
  1005.5 93.6 reduce-scatter.6
  1102.6 206.9 reduce-scatter.10
  1313.1 228.2 reduce-scatter.4
  1545.3 402.8 reduce-scatter.8
  1950.8 133.4 all-reduce.7

commit v2 on v1

--- a/solution.py
+++ b/solution.py
@@ -12,6 +12,7 @@
 EPSILON = 1e-05
 LANE = 128
 QUAD = 4
+LAG = 1
 SCALE = 1.0 / math.sqrt(HEAD_DIM)
 F32 = jnp.float32
 BF16 = jnp.bfloat16
@@ -440,6 +441,394 @@
     )
 
 
+MESH = pl.DeviceIdType.MESH
+
+
+def ring_index(place, n):
+    place = lax.rem(place + 2 * n, n)
+    return jnp.where(place < n // 2, 2 * place, 2 * (n - 1 - place) + 1)
+
+
+def ring_place(index, n):
+    half = lax.div(index, 2)
+    return jnp.where(lax.rem(index, 2) == 0, half, n - 1 - half)
+
+
+class Ring:
+    def __init__(self, n):
+        self.n = n
+        rep = lax.axis_index("rep")
+        self.x, self.core = lax.div(rep, 2), lax.rem(rep, 2)
+        index = lax.axis_index("fsdp")
+        self.index = index
+        self.place = ring_place(index, n)
+        self.right = (rep, ring_index(self.place + 1, n))
+        self.left = (rep, ring_index(self.place - 1, n))
+        self.sibling = (self.x * 2 + 1 - self.core, index)
+        self.across = ((1 - self.x) * 2 + self.core, index)
+
+    def meet(self):
+        barrier = pltpu.get_barrier_semaphore()
+        for other in (self.right, self.left, self.sibling, self.across):
+            pl.semaphore_signal(barrier, inc=1, device_id=other, device_id_type=MESH)
+        pl.semaphore_wait(barrier, 4)
+
+
+def send(src, dst, send_sem, recv_sem, device):
+    return pltpu.make_async_remote_copy(
+        src_ref=src, dst_ref=dst, send_sem=send_sem, recv_sem=recv_sem,
+        device_id=device, device_id_type=MESH,
+    )
+
+
+def cols(start, size):
+    return pl.ds(pl.multiple_of(start, LANE), size)
+
+
+class Gather:
+    def __init__(self, ring, weights, fulls, widths, sems):
+        self.ring, self.weights, self.fulls = ring, weights, fulls
+        self.axes, self.widths = zip(*widths)
+        (self.own, self.ring_send, self.ring_recv, self.core_send, self.core_recv, self.x_send, self.x_recv) = sems
+
+    def windows(self, i):
+        ring = self.ring
+        half = self.weights[i].shape[self.axes[i]] // 2
+        w = self.widths[i]
+        base = ring.core * half
+        part = half - 2 * w
+        first = base + jnp.where(ring.x == 0, 0, half - w)
+        second = base + jnp.where(ring.x == 0, w, half - 2 * w)
+        give = base + jnp.where(ring.x == 0, 0, half - part)
+        take = base + jnp.where(ring.x == 0, half - part, 0)
+        return w, part, first, second, give, take
+
+    def block(self, i, index, start, width):
+        rows = self.weights[i].shape[0]
+        if self.axes[i] == 0:
+            return self.fulls[i].at[pl.ds(pl.multiple_of(index * rows + start, 16), width), :]
+        return self.fulls[i].at[pl.ds(pl.multiple_of(index * rows, 16), rows), cols(start, width)]
+
+    def piece(self, i, start, width):
+        if self.axes[i] == 0:
+            return self.weights[i].at[pl.ds(pl.multiple_of(start, 16), width), :]
+        return self.weights[i].at[:, cols(start, width)]
+
+    def ring_copy(self, i, d, k, source):
+        ring = self.ring
+        w, _, first, second, _, _ = self.windows(i)
+        start = second if d else first
+        index = ring_index(ring.place + (k if d else -k), ring.n)
+        there = self.block(i, index, start, w)
+        src = self.piece(i, start, w) if source else there
+        return send(src, there, self.ring_send.at[i, d, k], self.ring_recv.at[i, d, k], ring.left if d else ring.right)
+
+    def core_copy(self, i, d, k):
+        ring = self.ring
+        w, part, first, second, _, take = self.windows(i)
+        start, width = ((first, w), (second, w), (take, part))[d]
+        index = ring_index(ring.place + (k + 1 if d == 1 else -k - 1), ring.n)
+        there = self.block(i, index, start, width)
+        return send(there, there, self.core_send.at[i, d, k], self.core_recv.at[i, d, k], ring.sibling)
+
+    def x_copy(self, i, k):
+        ring = self.ring
+        _, part, _, _, give, _ = self.windows(i)
+        there = self.block(i, ring_index(ring.place - k - 1, ring.n), give, part)
+        return send(there, there, self.x_send.at[i, k], self.x_recv.at[i, k], ring.across)
+
+    def own_copy(self, i):
+        rows = self.weights[i].shape[0]
+        there = self.fulls[i].at[pl.ds(pl.multiple_of(self.ring.index * rows, 16), rows), :]
+        return send(self.weights[i], there, self.own.at[0, i], self.own.at[1, i], self.ring.sibling)
+
+    def has_part(self, i):
+        return self.weights[i].shape[self.axes[i]] // 2 > 2 * self.widths[i]
+
+    def start(self):
+        for i in range(len(self.weights)):
+            for d in range(2):
+                self.ring_copy(i, d, 0, True).start()
+        for i in range(len(self.weights)):
+            self.own_copy(i).start()
+
+    def step(self, k):
+        last = self.ring.n - 2
+        for i in range(len(self.weights)):
+            for d in range(2):
+                self.ring_copy(i, d, k, False).wait_recv()
+
+                @pl.when(k < last)
+                def _():
+                    self.ring_copy(i, d, k + 1, False).start()
+
+                if d == 0 and self.has_part(i):
+                    self.x_copy(i, k).start()
+                self.core_copy(i, d, k).start()
+
+            if self.has_part(i):
+                @pl.when(k >= LAG)
+                def _():
+                    self.pass_on(i, k - LAG)
+
+    def pass_on(self, i, k):
+        self.x_copy(i, k).wait_recv()
+        self.core_copy(i, 2, k).start()
+
+    def finish(self):
+        last = self.ring.n - 2
+        for k in range(max(0, last + 1 - LAG), last + 1):
+            for i in range(len(self.weights)):
+                if self.has_part(i):
+                    self.pass_on(i, k)
+
+        def settle(k, carry):
+            for i in range(len(self.weights)):
+                for d in range(2):
+                    self.ring_copy(i, d, k, False).wait_send()
+                    self.core_copy(i, d, k).wait()
+                if self.has_part(i):
+                    self.x_copy(i, k).wait_send()
+                    self.core_copy(i, 2, k).wait()
+            return carry
+
+        lax.fori_loop(0, self.ring.n - 1, settle, 0)
+        for i in range(len(self.weights)):
+            self.own_copy(i).wait()
+
+    @staticmethod
+    def scratch(count, n):
+        dma = pltpu.SemaphoreType.DMA
+        return [
+            dma((2, count)), dma((count, 2, n - 1)), dma((count, 2, n - 1)),
+            dma((count, 3, n - 1)), dma((count, 3, n - 1)), dma((count, n - 1)), dma((count, n - 1)),
+        ]
+
+
+def gather_kernel(n, count, widths, *refs):
+    ring = Ring(n)
+    gather = Gather(ring, refs[:count], refs[count : 2 * count], widths, refs[2 * count :])
+    ring.meet()
+    gather.start()
+
+    def one(k, carry):
+        gather.step(k)
+        return carry
+
+    lax.fori_loop(0, n - 1, one, 0)
+    gather.finish()
+
+
+def share(shape):
+    rows, columns = shape
+    axis, unit = (0, 16) if rows % 64 == 0 else (1, LANE)
+    units = (rows, columns)[axis] // 2 // unit
+    return axis, -(-units // 3) * unit
+
+
+def gather_all(weights, n, collective):
+    count = len(weights)
+    widths = [share(w.shape) for w in weights]
+    anywhere = pl.BlockSpec(memory_space=pl.ANY)
+    return pl.pallas_call(
+        functools.partial(gather_kernel, n, count, widths),
+        out_shape=[jax.ShapeDtypeStruct((n * w.shape[0], w.shape[1]), w.dtype) for w in weights],
+        in_specs=[anywhere] * count,
+        out_specs=[anywhere] * count,
+        scratch_shapes=Gather.scratch(count, n),
+        compiler_params=pltpu.CompilerParams(collective_id=collective, has_side_effects=True),
+    )(*weights)
+
+
+class Reduce:
+    def __init__(self, ring, grads, totals, others, shapes, scratch):
+        self.ring, self.grads, self.totals, self.others, self.shapes = ring, grads, totals, others, shapes
+        count = len(grads)
+        pairs = 2 * count
+        self.slots = [scratch[2 * i : 2 * i + 2] for i in range(count)]
+        scratch = scratch[pairs:]
+        self.mine = [scratch[2 * i : 2 * i + 2] for i in range(count)]
+        scratch = scratch[pairs:]
+        self.twin = [scratch[2 * i : 2 * i + 2] for i in range(count)]
+        scratch = scratch[pairs:]
+        self.plane = [scratch[2 * i : 2 * i + 2] for i in range(count)]
+        scratch = scratch[pairs:]
+        (self.load, self.ring_send, self.ring_recv, self.core_send, self.core_recv,
+         self.end_send, self.end_recv, self.keep) = scratch
+
+    def owner(self, d, j):
+        ring = self.ring
+        return ring_index(ring.place + (j + 1 if d else -j - 1), ring.n)
+
+    def window(self, i, d, core):
+        rows, columns = self.shapes[i]
+        w = columns // 4
+        return core * 2 * w + d * w, w
+
+    def rows(self, i, index):
+        rows = self.shapes[i][0]
+        return pl.ds(pl.multiple_of(index * rows, 16), rows)
+
+    def core_copy(self, i, d, j):
+        ring = self.ring
+        start, w = self.window(i, d, 1 - ring.core)
+        rows = self.rows(i, self.owner(d, j))
+        return send(
+            self.grads[i].at[rows, cols(start, w)], self.others[i].at[rows, d * w : (d + 1) * w],
+            self.core_send.at[i, d, j], self.core_recv.at[i, d, j], ring.sibling,
+        )
+
+    def loads(self, i, d, j):
+        start, w = self.window(i, d, self.ring.core)
+        rows = self.rows(i, self.owner(d, j))
+        return (
+            pltpu.make_async_copy(self.grads[i].at[rows, cols(start, w)], self.mine[i][d], self.load.at[i, d, 0]),
+            pltpu.make_async_copy(self.others[i].at[rows, d * w : (d + 1) * w], self.twin[i][d], self.load.at[i, d, 1]),
+        )
+
+    def ring_copy(self, i, d, j):
+        ring = self.ring
+        return send(
+            self.slots[i][d].at[j], self.slots[i][d].at[j + 1],
+            self.ring_send.at[i, d, j], self.ring_recv.at[i, d, j + 1], ring.left if d else ring.right,
+        )
+
+    def arrived(self, i, d, j):
+        ring = self.ring
+        return send(
+            self.slots[i][d].at[j], self.slots[i][d].at[j],
+            self.ring_send.at[i, d, j], self.ring_recv.at[i, d, j], ring.left if d else ring.right,
+        )
+
+    def across_copy(self, i, d):
+        return send(
+            self.slots[i][d].at[self.ring.n - 1], self.plane[i][d],
+            self.end_send.at[i, d, 0], self.end_recv.at[i, d, 0], self.ring.across,
+        )
+
+    def final_copies(self, i, d):
+        start, w = self.window(i, d, self.ring.core)
+        there = self.totals[i].at[:, cols(start, w)]
+        return (
+            send(self.mine[i][d], there, self.end_send.at[i, d, 1], self.end_recv.at[i, d, 1], self.ring.sibling),
+            pltpu.make_async_copy(self.mine[i][d], there, self.keep.at[i, d]),
+        )
+
+    def each(self):
+        return [(i, d) for i in range(len(self.grads)) for d in range(2)]
+
+    def start(self):
+        def give(j, carry):
+            for i, d in self.each():
+                self.core_copy(i, d, j).start()
+            return carry
+
+        lax.fori_loop(0, self.ring.n, give, 0)
+        for i, d in self.each():
+            self.fetch(i, d, 0)
+
+    def fetch(self, i, d, j):
+        own, other = self.loads(i, d, j)
+        own.start()
+        self.core_copy(i, d, j).wait_recv()
+        other.start()
+
+    def item(self, j):
+        last = self.ring.n - 1
+        for i, d in self.each():
+            for copy in self.loads(i, d, j):
+                copy.wait()
+            slot = self.slots[i][d]
+            both = self.mine[i][d][...].astype(F32) + self.twin[i][d][...].astype(F32)
+
+            @pl.when(j == 0)
+            def _():
+                slot[j] = both.astype(BF16)
+
+            @pl.when(j > 0)
+            def _():
+                self.arrived(i, d, j).wait_recv()
+                slot[j] = (slot[j].astype(F32) + both).astype(BF16)
+
+            @pl.when(j < last)
+            def _():
+                self.ring_copy(i, d, j).start()
+                self.fetch(i, d, j + 1)
+
+    def finish(self):
+        last = self.ring.n - 1
+        for i, d in self.each():
+            self.across_copy(i, d).start()
+        for i, d in self.each():
+            self.across_copy(i, d).wait()
+            both = self.slots[i][d][last].astype(F32) + self.plane[i][d][...].astype(F32)
+            self.mine[i][d][...] = both.astype(BF16)
+            for copy in self.final_copies(i, d):
+                copy.start()
+        for i, d in self.each():
+            for copy in self.final_copies(i, d):
+                copy.wait()
+
+        def settle(j, carry):
+            for i, d in self.each():
+                self.core_copy(i, d, j).wait_send()
+
+                @pl.when(j < last)
+                def _():
+                    self.ring_copy(i, d, j).wait_send()
+
+            return carry
+
+        lax.fori_loop(0, self.ring.n, settle, 0)
+
+    @staticmethod
+    def scratch(shapes, n):
+        dma = pltpu.SemaphoreType.DMA
+        count = len(shapes)
+        blocks = [(rows, columns // 4) for rows, columns in shapes for _ in range(2)]
+        return (
+            [pltpu.VMEM((n,) + b, BF16) for b in blocks]
+            + [pltpu.VMEM(b, BF16) for b in blocks] * 3
+            + [
+                dma((count, 2, 2)), dma((count, 2, n)), dma((count, 2, n)), dma((count, 2, n)), dma((count, 2, n)),
+                dma((count, 2, 2)), dma((count, 2, 2)), dma((count, 2)),
+            ]
+        )
+
+
+def reduce_kernel(n, shapes, *refs):
+    count = len(shapes)
+    ring = Ring(n)
+    reduce = Reduce(ring, refs[:count], refs[count : 2 * count], refs[2 * count : 3 * count], shapes, refs[3 * count :])
+    ring.meet()
+    reduce.start()
+
+    def one(j, carry):
+        reduce.item(j)
+        return carry
+
+    lax.fori_loop(0, n, one, 0)
+    reduce.finish()
+
+
+def reduce_all(grads, n, collective):
+    count = len(grads)
+    shapes = [(g.shape[0] // n, g.shape[1]) for g in grads]
+    anywhere = pl.BlockSpec(memory_space=pl.ANY)
+    results = pl.pallas_call(
+        functools.partial(reduce_kernel, n, shapes),
+        out_shape=[jax.ShapeDtypeStruct(s, BF16) for s in shapes]
+        + [jax.ShapeDtypeStruct((n * rows, columns // 2), BF16) for rows, columns in shapes],
+        in_specs=[anywhere] * count,
+        out_specs=[anywhere] * (2 * count),
+        scratch_shapes=Reduce.scratch(shapes, n),
+        compiler_params=pltpu.CompilerParams(
+            collective_id=collective, has_side_effects=True, vmem_limit_bytes=60 * 1024 * 1024
+        ),
+    )(*grads)
+    return results[:count]
+
+
 def rms_norm(values, gains):
     return values * lax.rsqrt(jnp.mean(values * values, axis=-1, keepdims=True) + EPSILON) * gains
 
@@ -450,31 +839,19 @@
 
 
 def project(operand, weight):
-    return jnp.dot(
-        operand,
-        lax.all_gather(weight, "fsdp", axis=0, tiled=True),
-        preferred_element_type=jnp.float32,
-    )
+    return jnp.dot(operand, weight, preferred_element_type=F32)
 
 
 def project_back(upstream, weight):
     return lax.dot_general(
-        upstream,
-        lax.all_gather(weight, "fsdp", axis=0, tiled=True),
-        (((1,), (1,)), ((), ())),
-        preferred_element_type=jnp.float32,
+        upstream, weight, (((1,), (1,)), ((), ())), preferred_element_type=F32
     )
 
 
 def weight_grad(operand, upstream):
-    return lax.psum_scatter(
-        lax.dot_general(
-            operand, upstream, (((0,), (0,)), ((), ())), preferred_element_type=jnp.float32
-        ).astype(jnp.bfloat16),
-        "fsdp",
-        scatter_dimension=0,
-        tiled=True,
-    ).astype(jnp.float32)
+    return lax.dot_general(
+        operand, upstream, (((0,), (0,)), ((), ())), preferred_element_type=F32
+    ).astype(BF16)
 
 
 def body(
@@ -491,6 +868,9 @@
     doc_lengths,
     cotangent,
 ):
+    n = lax.axis_size("fsdp")
+    (qkv_weight,) = gather_all([qkv_weight], n, 0)
+    out_weight, inner_weight, down_weight = gather_all([out_weight, inner_weight, down_weight], n, 1)
     inputs = layer_input.astype(jnp.float32)
     normed_value, first_pull = jax.vjp(rms_norm, inputs, first_gain)
     normed = normed_value.astype(jnp.bfloat16)
@@ -527,13 +907,8 @@
     small = lax.psum(
         (grad_first, grad_kernel, grad_mixing, grad_group, grad_second), ("rep", "fsdp")
     )
-    shards = (grad_qkv, grad_proj, grad_inner, grad_down)
-    shards = (
-        lax.psum(shards[0].astype(jnp.bfloat16), "rep").astype(jnp.float32),
-        lax.psum(shards[1].astype(jnp.bfloat16), "rep").astype(jnp.float32),
-        lax.psum(shards[2].astype(jnp.bfloat16), "rep").astype(jnp.float32),
-        lax.psum(shards[3].astype(jnp.bfloat16), "rep").astype(jnp.float32),
-    )
+    shards = reduce_all([grad_down, grad_inner, grad_proj, grad_qkv], n, 2)
+    shards = [shards[i].astype(F32) for i in (3, 2, 1, 0)]
     return (
         layer_output,
         grad_input,

time: 2110 us -> 987 us (0.47)
  waiting for transfers between devices: 1690 us -> 0 us
  Pallas kernels: 147 us -> 727 us
    all_gather x4 -> x0, waiting for transfers between devices: 852 us -> none  [project(): lax.all_gather(weight, 'fsdp', axis=0, tiled=True)]
    reduce_scatter x4 -> x0, waiting for transfers between devices: 776 us -> none  [weight_grad(): lax.psum_scatter(lax.dot_general(operand, upstream, (((0,), (0,)), ((), (...]
    pallas_call x0 -> x3, Pallas kernels: none -> 580 us  [the longest x1 360 us: reduce_all(): pl.pallas_call(functools.partial(reduce_kernel, n, shapes), out_shape=[ja...]
    psum x1 -> x0, waiting for transfers between devices: 62 us -> none  [body(): lax.psum(shards[0].astype(jnp.bfloat16), 'rep').astype(jnp.float32)]
  transfers between devices with their start and end apart: 9 -> 0, of which waited for: 8 -> 0; matrix products, arithmetic and copies ran while one was open for 6% -> 0% of each run, Pallas kernels for 7% -> 0%
where the time goes in v2:
time: 987 us; the launch traced here: 979 us
  Pallas kernels  727 us (74%)
  matrix products  171 us (17%)
  blocking collectives  42.5 us (4%)
  other arithmetic  22.4 us (2%)
  local copies, waits for them, and re-layouts  14.3 us (1%)
    pallas_call x1, Pallas kernels, reduce_all(): pl.pallas_call(functools.partial(reduce_kernel, n, shapes), out_shape=[ja...  360 us
    pallas_call x2, Pallas kernels, gather_all(): pl.pallas_call(functools.partial(gather_kernel, n, count, widths), out_sh...  220 us
    pallas_call x1, Pallas kernels, attend_backward(): pl.pallas_call(backward_kernel, grid=(quads,), out_shape=[jax.ShapeDtypeS...  108 us
    dot_general x4, matrix products, project_back(): lax.dot_general(upstream, weight, (((1,), (1,)), ((), ())), preferred_ele...  66.6 us
    dot_general x4, matrix products, project(): return jnp.dot(operand, weight, preferred_element_type=F32)  52.8 us
    dot_general x4, matrix products, weight_grad(): lax.dot_general(operand, upstream, (((0,), (0,)), ((), ())), preferred_el...  52.1 us
    psum x1, blocking collectives, body(): lax.psum((grad_first, grad_kernel, grad_mixing, grad_group, grad_second),...  42.5 us
    pallas_call x1, Pallas kernels, attend_forward(): pl.pallas_call(forward_kernel, grid=(quads,), out_shape=[jax.ShapeDtypeSt...  39.3 us

profile of v2, /device:TPU:0, one launch (start us, length us, event | category | flops | bytes accessed | tf_op | source)
XLA Modules:
  0.0 978.6 jit_solution(2022212254262410168)
XLA Ops:
  0.6 1.8 fusion.9
  2.4 0.6 copy-done.14
  3.0 0.8 copy.31.mix_ref
  3.8 0.7 reshape.77.gain_ref
  4.5 0.9 copy.30
  5.5 0.1 pad_slice_fusion.1
  5.6 0.7 pad_maximum_fusion.2.taps_ref
  6.4 0.1 pad_maximum_fusion.1.taps_ref
  6.5 65.7 %shard_map.203 = bf16[1536,4608]{1,0:T(8,128)(2,1)} custom-call(bf16[192,4608]{1,0:T(8,128)(2,1)} %refs_0_.2), custom_call_target="tpu_custom_call" | custom-call | tf_op jit(solution)/shard_map/pallas_call | solution.py:633
  72.3 14.3 %convolution_convert_fusion.4.q_ref.k_ref.v_ref = bf16[512,4608]{1,0:T(8,128)(2,1)} fusion(bf16[1536,4608]{1,0:T(8,128)(2,1)} %shard_map.203, bf16[512,1536]{1,0:T(8,128)(2,1)S(1)} %copy-done.6, f32[1536]{0:T(1024)S(1)} %copy-done.17, f32[512]{0:T(512)S(1)} %fusion.18), kind=kOutput, calls=%fused_computation.13 | convolution fusion | flops 7253262336 | bytes 20455424 | tf_op jit(solution)/shard_map/dot_general | solution.py:842
  86.6 39.3 %shard_map.204 = (bf16[512,1536]{1,0:T(8,128)(2,1)S(1)}, f32[512,1536]{1,0:T(8,128)S(1)}, bf16[16,512,384]{2,1,0:T(8,128)(2,1)}) custom-call(s32[1,4]{1,0:T(1,128)S(1)} %copy-done.3, f32[8,4]{1,0:T(8,128)S(1)} %copy.31.mix_ref, f32[16,8,128]{2,1,0:T(8,128)S(1)} %pad_maximum_fusion.1.taps_ref, f32[1,1536]{1,0:T(1,128)S(1)} %reshape.77.gain_ref, ...), custom_call_target="tpu_custom_call" | custom-call | tf_op jit(solution)/shard_map/pallas_call | solution.py:209
  126.0 1.7 copy-done
  127.6 154.5 %shard_map.205 = (bf16[1536,1536]{1,0:T(8,128)(2,1)}, bf16[1536,8192]{1,0:T(8,128)(2,1)}, bf16[4096,1536]{1,0:T(8,128)(2,1)}) custom-call(bf16[192,1536]{1,0:T(8,128)(2,1)} %refs_0_.3, bf16[192,8192]{1,0:T(8,128)(2,1)} %refs_1_.1, bf16[512,1536]{1,0:T(8,128)(2,1)} %refs_2_.1), custom_call_target="tpu_custom_call" | custom-call | tf_op jit(solution)/shard_map/pallas_call | solution.py:633
  282.1 4.6 multiply_reduce_fusion.2
  286.8 1.6 copy-done.7
  288.5 21.6 %fusion.22 = f32[512,8192]{1,0:T(8,128)} fusion(bf16[1536,8192]{1,0:T(8,128)(2,1)} %get-tuple-element.29, f32[512,1536]{1,0:T(8,128)S(1)} %get-tuple-element.78, f32[1536]{0:T(1024)S(1)} %copy-done.16, f32[512]{0:T(512)S(1)} %fusion.19), kind=kOutput, calls=%fused_computation.60 | convolution fusion | flops 12887261184 | bytes 45096960 | tf_op jit(solution)/shard_map/dot_general | solution.py:842
  310.0 20.3 %bitcast_multiply_fusion.1 = (f32[512,4096]{1,0:T(8,128)}, f32[512,4096]{1,0:T(8,128)}, bf16[512,4096]{1,0:T(8,128)(2,1)}) fusion(f32[512,8192]{1,0:T(8,128)} %fusion.22, bf16[4096,1536]{1,0:T(8,128)(2,1)} %get-tuple-element.30, bf16[512,1536]{1,0:T(8,128)(2,1)} %param.23), kind=kOutput, calls=%fused_computation.8 | convolution fusion | flops 6471811072 | bytes 51904512 | tf_op jit(solution)/shard_map/dot_general | solution.py:846
  330.3 12.3 %fusion.11 = bf16[512,1536]{1,0:T(8,128)(2,1)} fusion(f32[512,1536]{1,0:T(8,128)} %copy-done.7, bf16[512,4096]{1,0:T(8,128)(2,1)} %get-tuple-element.76, bf16[4096,1536]{1,0:T(8,128)(2,1)} %get-tuple-element.30), kind=kOutput, calls=%fused_computation.34 | convolution fusion | flops 6444023808 | bytes 21495808 | tf_op jit(solution)/shard_map/dot_general | solution.py:842
  342.6 27.1 %multiply_reduce_fusion = (f32[1536]{0:T(1024)S(1)}, f32[512]{0:T(512)S(1)}, f32[512,1536]{1,0:T(8,128)}) fusion(f32[512,1536]{1,0:T(8,128)} %copy-done.7, f32[512]{0:T(512)S(1)} %fusion.19, f32[1536]{0:T(1024)S(1)} %copy-done.16, bf16[1536,8192]{1,0:T(8,128)(2,1)} %get-tuple-element.29, f32[512,4096]{1,0:T(8,128)} %get-tuple-element.75, ...), kind=kOutput, calls=%fused_computation.30 | convolution fusion | flops 12898007040 | bytes 48250880 | tf_op jit(solution)/shard_map/dot_general | solution.py:846
  369.7 4.1 fusion.7
  373.8 1.7 copy-done.4
  375.5 6.7 fusion.14.d_grouped_ref
  382.1 107.5 %shard_map.206 = (bf16[512,1536]{1,0:T(8,128)(2,1)}, bf16[512,1536]{1,0:T(8,128)(2,1)}, bf16[512,1536]{1,0:T(8,128)(2,1)}, f32[1,1536]{1,0:T(1,128)}, f32[16,8,128]{2,1,0:T(8,128)}, /*index=5*/f32[4,8,128]{2,1,0:T(8,128)}) custom-call(s32[1,4]{1,0:T(1,128)} %docs_ref.3, f32[8,4]{1,0:T(8,128)} %copy-done.2, f32[16,8,128]{2,1,0:T(8,128)} %pad_maximum_fusion.2.taps_ref, ...), custom_call_target="tpu_custom_call" | custom-call | tf_op jit(solution)/shard_map/pallas_call | solution.py:396
  489.6 0.7 slice.43
  490.4 0.1 reshape.80
  490.5 0.1 copy.38
  490.6 0.7 reduce
  491.3 0.9 slice.40
  492.2 0.9 pad_maximum_fusion
  493.2 1.7 constant_dynamic-update-slice_fusion.2
  494.9 0.2 copy-done.10
  495.1 0.1 constant_dynamic-update-slice_fusion.1
  495.2 0.4 copy-done.9
  495.6 0.1 constant_dynamic-update-slice_fusion
  495.7 12.5 %fusion.6 = (f32[1536]{0:T(1024)S(1)}, f32[512]{0:T(512)S(1)}, f32[512,1536]{1,0:T(8,128)S(1)}) fusion(bf16[512,1536]{1,0:T(8,128)(2,1)S(1)} %copy-done.6, f32[512]{0:T(512)S(1)} %fusion.18, f32[1536]{0:T(1024)S(1)} %copy-done.17, bf16[512,4608]{1,0:T(8,128)(2,1)S(1)} %constant_dynamic-update-slice_fusion, bf16[1536,4608]{1,0:T(8,128)(2,1)} %shard_map.203), kind=kOutput, calls=%fused_computation.25 | convolution fusion | flops 7253260288 | bytes 23609344 | tf_op jit(solution)/shard_map/dot_general | solution.py:846
  508.3 2.4 fusion.8
  510.7 4.3 convolution_convert_fusion.3.refs_2_
  515.1 42.5 %all-reduce.4 = (f32[1536]{0:T(1024)}, f32[16,6,11]{2,1,0:T(8,128)S(1)}, f32[8,2,2]{0,2,1:T(2,128)}, f32[1536]{0:T(1024)}, f32[1536]{0:T(1024)}) all-reduce(f32[1536]{0:T(1024)S(1)} %get-tuple-element.67, f32[16,6,11]{2,1,0:T(8,128)S(1)} %broadcast_multiply_fusion, ...), channel_id=1, replica_groups=mesh['rep'=4,'fsdp'=8] {'rep','fsdp'}, use_global_device_ids=true, to_apply=%region_5.6 | all-reduce | flops 5696 | bytes 45568 | tf_op jit(solution)/shard_map/psum | solution.py:907
  557.6 0.7 copy.36
  558.3 23.0 %convolution_convert_fusion.refs_1_ = bf16[1536,8192]{1,0:T(8,128)(2,1)} fusion(f32[512,4096]{1,0:T(8,128)} %get-tuple-element.75, f32[512,4096]{1,0:T(8,128)} %get-tuple-element.74, f32[512,1536]{1,0:T(8,128)} %copy-done.7, f32[1536]{0:T(1024)S(1)} %copy-done.16, f32[512]{0:T(512)S(1)} %fusion.19), kind=kOutput, calls=%fused_computation | convolution fusion | flops 12908232704 | bytes 45096960 | tf_op jit(solution)/shard_map/dot_general | solution.py:852
  581.4 12.0 %convolution_convert_fusion.2.refs_0_ = bf16[4096,1536]{1,0:T(8,128)(2,1)} fusion(bf16[512,4096]{1,0:T(8,128)(2,1)} %get-tuple-element.76, bf16[512,1536]{1,0:T(8,128)(2,1)S(1)} %copy-done.12), kind=kOutput, calls=%fused_computation.3 | convolution fusion | flops 6448742400 | bytes 18350080 | tf_op jit(solution)/shard_map/dot_general | solution.py:852
  593.4 12.8 %convolution_convert_fusion.1.refs_3_ = bf16[1536,4608]{1,0:T(8,128)(2,1)} fusion(bf16[512,4608]{1,0:T(8,128)(2,1)} %copy-done.13, bf16[512,1536]{1,0:T(8,128)(2,1)S(1)} %copy-done.6, f32[1536]{0:T(1024)S(1)} %copy-done.17, f32[512]{0:T(512)S(1)} %fusion.18), kind=kOutput, calls=%fused_computation.1 | convolution fusion | flops 7257980928 | bytes 20455424 | tf_op jit(solution)/shard_map/dot_general | solution.py:852
  606.1 359.6 %shard_map.207 = (bf16[512,1536]{1,0:T(8,128)(2,1)}, bf16[192,8192]{1,0:T(8,128)(2,1)}, bf16[192,1536]{1,0:T(8,128)(2,1)}, bf16[192,4608]{1,0:T(8,128)(2,1)}, bf...) custom-call(bf16[4096,1536]{1,0:T(8,128)(2,1)} %convolution_convert_, ...), custom_call_target="tpu_custom_call" | custom-call | tf_op jit(solution)/shard_map/pallas_call | solution.py:818
  965.7 2.3 convert_element_type.68
  968.0 3.7 convert_element_type.67
  971.7 2.1 convert_element_type.70
  973.8 0.9 copy-done.8
  974.7 3.4 convert_element_type.69
  (41 shorter events, 0.4 us)
Async XLA Ops:
  2.4 0.6 copy-start.14
  3.8 82.8 %copy-start.2 = (f32[8,4]{1,0:T(8,128)}, f32[8,4]{1,0:T(8,128)S(1)}, u32[]{:S(2)}) copy-start(f32[8,4]{1,0:T(8,128)S(1)} %copy.31.mix_ref) | copy-start | bytes 388
  4.5 82.1 %copy-start.1 = (f32[1,1536]{1,0:T(1,128)}, f32[1,1536]{1,0:T(1,128)S(1)}, u32[]{:S(2)}) copy-start(f32[1,1536]{1,0:T(1,128)S(1)} %reshape.77.gain_ref) | copy-start | bytes 18436
  6.5 65.8 %copy-start.6 = (bf16[512,1536]{1,0:T(8,128)(2,1)S(1)}, bf16[512,1536]{1,0:T(8,128)(2,1)}, u32[]{:S(2)}) copy-start(bf16[512,1536]{1,0:T(8,128)(2,1)} %param.12) | copy-start | bytes 4718596
  6.5 65.8 %copy-start.17 = (f32[1536]{0:T(1024)S(1)}, f32[1536]{0:T(1024)}, u32[]{:S(2)}) copy-start(f32[1536]{0:T(1024)} %param.13) | copy-start | bytes 18436
  72.3 14.3 %copy-start.3 = (s32[1,4]{1,0:T(1,128)S(1)}, s32[1,4]{1,0:T(1,128)}, u32[]{:S(2)}) copy-start(s32[1,4]{1,0:T(1,128)} %docs_ref.3) | copy-start | bytes 52
  126.0 1.7 copy-start
  282.1 6.3 copy-start.16
  286.8 1.7 copy-start.7
  373.8 1.7 copy-start.4
  493.2 1.9 copy-start.10
  493.2 2.3 copy-start.9
  495.7 12.6 %copy-start.13 = (bf16[512,4608]{1,0:T(8,128)(2,1)}, bf16[512,4608]{1,0:T(8,128)(2,1)S(1)}, u32[]{:S(2)}) copy-start(bf16[512,4608]{1,0:T(8,128)(2,1)S(1)} %constant_dynamic-update-slice_fusion) | copy-start | bytes 14155780
  495.7 12.6 %copy-start.15 = (f32[512]{0:T(512)S(1)}, f32[512]{0:T(512)}, u32[]{:S(2)}) copy-start(f32[512]{0:T(512)} %copy-done.14) | copy-start | bytes 6148
  495.7 12.6 %copy-start.5 = (f32[512,1536]{1,0:T(8,128)S(1)}, f32[512,1536]{1,0:T(8,128)}, u32[]{:S(2)}) copy-start(f32[512,1536]{1,0:T(8,128)} %copy-done.4) | copy-start | bytes 9437188
  558.3 23.0 %copy-start.12 = (bf16[512,1536]{1,0:T(8,128)(2,1)S(1)}, bf16[512,1536]{1,0:T(8,128)(2,1)}, u32[]{:S(2)}) copy-start(bf16[512,1536]{1,0:T(8,128)(2,1)} %param.23) | copy-start | bytes 4718596
  965.7 6.0 copy-start.11
  971.7 3.0 copy-start.8

commit v3 on v2

--- a/solution.py
+++ b/solution.py
@@ -13,6 +13,7 @@
 LANE = 128
 QUAD = 4
 LAG = 1
+LEAD = 3
 SCALE = 1.0 / math.sqrt(HEAD_DIM)
 F32 = jnp.float32
 BF16 = jnp.bfloat16
@@ -117,23 +118,74 @@
 
 
 def forward_kernel(
-    docs_ref, mix_ref, taps_ref, gain_ref, q_ref, k_ref, v_ref,
-    grouped_ref, attended_ref, soft_ref,
-    masks, band, qs, ks, vs, shifted, outs, normed,
+    n, first_widths, rest_widths, docs_ref, mix_ref, taps_ref, gain_ref, input_ref, first_gain_ref, second_gain_ref, *refs
 ):
-    seq = q_ref.shape[0]
+    refs = list(refs)
+
+    def take(size):
+        taken = refs[:size]
+        del refs[:size]
+        return taken
+
+    first_count, rest_count = len(first_widths), len(rest_widths)
+    first_weights, rest_weights = take(first_count), take(rest_count)
+    grouped_ref, attended_ref, soft_ref, normed_ref, middle_ref, second_ref, projected = take(7)
+    first_fulls, rest_fulls = take(first_count), take(rest_count)
+    masks, band, qs, ks, vs, shifted, outs = take(7)
+    blocks, block_weight, every, out_weight, block_in, block_out, out_in = take(7)
+    ring = Ring(n)
+    sems = len(Gather.scratch(first_count, n))
+    first = Gather(ring, first_weights, first_fulls, first_widths, take(sems))
+    rest = Gather(ring, rest_weights, rest_fulls, rest_widths, take(sems))
+    seq = input_ref.shape[0]
     quad = pl.program_id(0)
+    quads = HEADS // QUAD
+    size = QUAD * HEAD_DIM
+    count = 3 * quads
+
+    def block_copy(t):
+        slot = lax.rem(t, 2)
+        return pltpu.make_async_copy(first_fulls[0].at[:, cols(t * size, size)], block_weight.at[slot], block_in.at[slot])
+
+    def block_save(t):
+        return pltpu.make_async_copy(blocks.at[t], projected.at[:, cols(t * size, size)], block_out.at[t])
+
+    out_copy = pltpu.make_async_copy(first_fulls[1], out_weight, out_in)
 
     @pl.when(quad == 0)
     def _():
+        ring.meet()
+        first.start()
         fill_masks(docs_ref, masks, seq)
         band[...] = jnp.zeros_like(band)
+        values = input_ref[...].astype(F32)
+        scale = lax.rsqrt(jnp.mean(values * values, axis=1, keepdims=True) + EPSILON)
+        normed_ref[...] = (values * scale * first_gain_ref[...]).astype(BF16)
+
+        def one(k, carry):
+            first.step(k)
+            pl.when(k == n - 3)(rest.start)
+            return carry
+
+        lax.fori_loop(0, n - 1, one, 0)
+        first.finish()
+        block_copy(0).start()
+        out_copy.start()
+
+        def project_block(t, carry):
+            pl.when(t < count - 1)(lambda: block_copy(t + 1).start())
+            block_copy(t).wait()
+            blocks[t] = nn(normed_ref[...], block_weight[lax.rem(t, 2)]).astype(BF16)
+            block_save(t).start()
+            return carry
+
+        lax.fori_loop(0, count, project_block, 0)
 
     for h in range(QUAD):
         at = slice(h * HEAD_DIM, (h + 1) * HEAD_DIM)
-        qs[h] = q_ref[:, at]
-        ks[h] = k_ref[:, at]
-        vs[h] = v_ref[:, at]
+        qs[h] = blocks[quad, :, at]
+        ks[h] = blocks[quads + quad, :, at]
+        vs[h] = blocks[2 * quads + quad, :, at]
 
     sets = row_sets(seq)
 
@@ -153,13 +205,13 @@
             i = 0
             while i < len(sets):
                 width = sets[i][1]
-                n = 1
-                while i + n < len(sets) and sets[i + n][1] == width:
-                    n += 1
-                left = jnp.concatenate([lefts[i + m][1] for m in range(n)], axis=0)
+                run = 1
+                while i + run < len(sets) and sets[i + run][1] == width:
+                    run += 1
+                left = jnp.concatenate([lefts[i + m][1] for m in range(run)], axis=0)
                 conv = nn(left, band[: width * CQ, :width])
-                convs += [conv[m * LANE : (m + 1) * LANE] for m in range(n)]
-                i += n
+                convs += [conv[m * LANE : (m + 1) * LANE] for m in range(run)]
+                i += run
             for (r0, width, c0), conv in zip(sets, convs):
                 logits = jnp.where(
                     masks[0, r0 : r0 + LANE, :width].astype(F32) > 0, conv, -1e30
@@ -176,6 +228,8 @@
                     + mix_ref[group, 2 * r + 1] * soft_ref[2 * p + 1, r0 : r0 + LANE, :width].astype(F32)
                 ).astype(BF16)
                 outs[h, r0 : r0 + LANE] = nn(mixed, values[c0 : c0 + width])
+        for k in in_turn(group, HEADS // 2, n - 1):
+            pl.when(k < n - 1)(functools.partial(rest.step, k))
         return carry
 
     lax.fori_loop(0, 2, pair, 0)
@@ -187,7 +241,24 @@
         wholes.append(attended)
         grouped.append(centred * lax.rsqrt(var + EPSILON))
     attended_ref[...] = jnp.concatenate(wholes, axis=1)
-    grouped_ref[...] = (jnp.concatenate(grouped, axis=1) * gain_ref[...]).astype(BF16)
+    every[quad] = (jnp.concatenate(grouped, axis=1) * gain_ref[...]).astype(BF16)
+    grouped_ref[...] = every[quad]
+
+    @pl.when(quad == quads - 1)
+    def _():
+        out_copy.wait()
+        branch = nn(jnp.concatenate([every[i] for i in range(quads)], axis=1), out_weight[...])
+        middle = input_ref[...].astype(F32) + branch
+        scale = lax.rsqrt(jnp.mean(middle * middle, axis=1, keepdims=True) + EPSILON)
+        middle_ref[...] = middle
+        second_ref[...] = (middle * scale * second_gain_ref[...]).astype(BF16)
+
+        def saved(t, carry):
+            block_save(t).wait()
+            return carry
+
+        lax.fori_loop(0, count, saved, 0)
+        rest.finish()
 
 
 def pad_taps(kernel):
@@ -195,34 +266,43 @@
     return jnp.roll(padded, -(CK // 2), axis=2)
 
 
-def attend_forward(projected, conv_kernel, head_mixing, docs, gain):
-    seq = projected.shape[0]
-    width = projected.shape[1] // 3
+def in_turn(turn, turns, steps):
+    each = -(-steps // turns)
+    return [turn * each + t for t in range(each)]
+
+
+def attend_forward(layer_input, conv_kernel, head_mixing, docs, gains, first, rest, n, collective):
+    seq, width = layer_input.shape
     block = QUAD * HEAD_DIM
     quads = HEADS // QUAD
+    first_widths, rest_widths = [share(w.shape) for w in first], [share(w.shape) for w in rest]
     whole = pl.BlockSpec(memory_space=pltpu.VMEM)
     smem = pl.BlockSpec(memory_space=pltpu.SMEM)
-
-    def columns(first):
-        return pl.BlockSpec((seq, block), lambda i: (0, first * quads + i))
-
-    return pl.pallas_call(
-        forward_kernel,
+    anywhere = pl.BlockSpec(memory_space=pl.ANY)
+    columns = pl.BlockSpec((seq, block), lambda i: (0, i))
+    dma = pltpu.SemaphoreType.DMA
+    first_gain, group_gain, second_gain = [g.reshape(1, width) for g in gains]
+    results = pl.pallas_call(
+        functools.partial(forward_kernel, n, first_widths, rest_widths),
         grid=(quads,),
         out_shape=[
             jax.ShapeDtypeStruct((seq, width), BF16),
             jax.ShapeDtypeStruct((seq, width), F32),
             jax.ShapeDtypeStruct((HEADS, seq, 3 * LANE), BF16),
-        ],
-        in_specs=[
-            smem, smem, whole,
-            pl.BlockSpec((1, block), lambda i: (0, i)),
-            columns(0), columns(1), columns(2),
-        ],
+            jax.ShapeDtypeStruct((seq, width), BF16),
+            jax.ShapeDtypeStruct((seq, width), F32),
+            jax.ShapeDtypeStruct((seq, width), BF16),
+            jax.ShapeDtypeStruct((seq, 3 * width), BF16),
+        ]
+        + [jax.ShapeDtypeStruct((n * w.shape[0], w.shape[1]), w.dtype) for w in first + rest],
+        in_specs=[smem, smem, whole, pl.BlockSpec((1, block), lambda i: (0, i)), whole, whole, whole]
+        + [anywhere] * len(first + rest),
         out_specs=[
-            columns(0), columns(0),
+            columns, columns,
             pl.BlockSpec((QUAD, seq, 3 * LANE), lambda i: (i, 0, 0)),
-        ],
+            whole, whole, whole,
+        ]
+        + [anywhere] * (1 + len(first + rest)),
         scratch_shapes=[
             pltpu.VMEM((CQ, seq, 3 * LANE), BF16),
             pltpu.VMEM((3 * LANE * CQ, 3 * LANE), BF16),
@@ -231,22 +311,41 @@
             pltpu.VMEM((QUAD, seq, HEAD_DIM), BF16),
             pltpu.VMEM((CQ, seq, HEAD_DIM), BF16),
             pltpu.VMEM((QUAD, seq, HEAD_DIM), F32),
-            pltpu.VMEM((8, LANE), F32),
-        ],
-        compiler_params=pltpu.CompilerParams(vmem_limit_bytes=48 * 1024 * 1024),
+            pltpu.VMEM((3 * quads, seq, block), BF16),
+            pltpu.VMEM((2, width, block), BF16),
+            pltpu.VMEM((quads, seq, block), BF16),
+            pltpu.VMEM((width, width), BF16),
+            dma((2,)), dma((3 * quads,)), dma,
+        ]
+        + Gather.scratch(len(first), n)
+        + Gather.scratch(len(rest), n),
+        compiler_params=pltpu.CompilerParams(
+            collective_id=collective, has_side_effects=True, vmem_limit_bytes=60 * 1024 * 1024
+        ),
     )(
-        docs, head_mixing.reshape(HEADS // 2, 4), pad_taps(conv_kernel), gain.reshape(1, width),
-        projected, projected, projected,
+        docs, head_mixing.reshape(HEADS // 2, 4), pad_taps(conv_kernel), group_gain, layer_input, first_gain, second_gain,
+        *first, *rest,
     )
+    return results[:7], results[7 : 7 + len(first)], results[7 + len(first) :]
 
 
 def backward_kernel(
-    docs_ref, mix_ref, taps_ref, gain_ref, q_ref, k_ref, v_ref, attended_ref, d_grouped_ref, soft_ref,
-    dq_ref, dk_ref, dv_ref, grad_gain_ref, grad_taps_ref, grad_mix_ref,
-    masks, band, qs, ks, vs, ds, shifted, d_heads, d_rows, d_cols, diagonal,
+    n, specs, docs_ref, mix_ref, taps_ref, gain_ref, q_ref, k_ref, v_ref, attended_ref, d_grouped_ref, soft_ref, *refs
 ):
+    count = len(specs)
+    grads, refs = refs[:count], refs[count:]
+    d_projected, grad_gain_ref, grad_taps_ref, grad_mix_ref = refs[:4]
+    sums, others, refs = refs[4 : 4 + count], refs[4 + count : 4 + 2 * count], refs[4 + 2 * count :]
+    masks, band, qs, ks, vs, ds, shifted, d_heads, d_rows, d_cols, diagonal, leaving, leave_sem = refs[:13]
+    reduce = Reduce(Ring(n), grads, sums, others, specs, refs[13:])
     seq = q_ref.shape[0]
     quad = pl.program_id(0)
+
+    @pl.when(quad == 0)
+    def _():
+        reduce.clear()
+        reduce.ring.meet()
+        reduce.start()
 
     @pl.when(quad == 0)
     def _():
@@ -274,6 +373,8 @@
         )
         ds[h] = d_attended.astype(BF16)
     grad_gain_ref[...] = jnp.concatenate(gains, axis=1)
+    grad_taps_ref[...] = jnp.zeros_like(grad_taps_ref)
+    grad_mix_ref[...] = jnp.zeros_like(grad_mix_ref)
 
     sets = row_sets(seq)
     up = lax.broadcasted_iota(jnp.int32, (LANE, LANE), 0)
@@ -375,47 +476,73 @@
             for a in range(CQ):
                 aligned = pltpu.roll(diagonal[a], 0, axis=1, stride=1, stride_axis=0)
                 grad_taps_ref[h, a : a + 1, :] = jnp.sum(aligned, axis=0, keepdims=True)
+            work = reduce.each()
+            middle = len(work) // 2
+            for j in in_turn(group, HEADS // 2, n):
+                pl.when(j < n)(functools.partial(reduce.item, j, work[middle:] if r else work[:middle]))
         return carry
 
     lax.fori_loop(0, 2, pair, 0)
-    for out, n in ((dq_ref, 0), (dk_ref, 1), (dv_ref, 2)):
-        out[...] = jnp.concatenate([d_heads[n, h] for h in range(QUAD)], axis=1).astype(BF16)
-
-
-def attend_backward(projected, conv_kernel, head_mixing, docs, gain, attended, d_grouped, soft):
+    quads = HEADS // QUAD
+    block = QUAD * HEAD_DIM
+
+    def leave(part):
+        there = d_projected.at[:, cols((part * quads + quad) * block, block)]
+        return pltpu.make_async_copy(leaving.at[part], there, leave_sem.at[part])
+
+    for part in range(3):
+        pl.when(quad > 0)(leave(part).wait)
+        leaving[part] = jnp.concatenate([d_heads[part, h] for h in range(QUAD)], axis=1).astype(BF16)
+        leave(part).start()
+
+    @pl.when(quad == quads - 1)
+    def _():
+        for part in range(3):
+            leave(part).wait()
+
+    @pl.when(quad == pl.num_programs(0) - 1)
+    def _():
+        reduce.finish()
+
+
+def attend_backward(projected, conv_kernel, head_mixing, docs, gain, attended, d_grouped, soft, grads, n, collective):
     seq = projected.shape[0]
     width = projected.shape[1] // 3
     block = QUAD * HEAD_DIM
     quads = HEADS // QUAD
+    count = len(grads)
+    specs = Reduce.specs_of(grads, n, True)
+    anywhere = pl.BlockSpec(memory_space=pl.ANY)
     whole = pl.BlockSpec(memory_space=pltpu.VMEM)
     smem = pl.BlockSpec(memory_space=pltpu.SMEM)
 
     def columns(first):
         return pl.BlockSpec((seq, block), lambda i: (0, first * quads + i))
 
-    dq, dk, dv, grad_gain, grad_taps, grad_mix = pl.pallas_call(
-        backward_kernel,
+    results = pl.pallas_call(
+        functools.partial(backward_kernel, n, specs),
         grid=(quads,),
         out_shape=[
-            jax.ShapeDtypeStruct((seq, width), BF16),
-            jax.ShapeDtypeStruct((seq, width), BF16),
-            jax.ShapeDtypeStruct((seq, width), BF16),
+            jax.ShapeDtypeStruct((seq, 3 * width), BF16),
             jax.ShapeDtypeStruct((1, width), F32),
             jax.ShapeDtypeStruct((HEADS, 8, LANE), F32),
             jax.ShapeDtypeStruct((quads, 8, LANE), F32),
-        ],
+        ]
+        + Reduce.results(specs, n),
         in_specs=[
             smem, smem, whole,
             pl.BlockSpec((1, block), lambda i: (0, i)),
             columns(0), columns(1), columns(2), columns(0), columns(0),
             pl.BlockSpec((QUAD, seq, 3 * LANE), lambda i: (i, 0, 0)),
-        ],
+        ]
+        + [anywhere] * count,
         out_specs=[
-            columns(0), columns(0), columns(0),
+            anywhere,
             pl.BlockSpec((1, block), lambda i: (0, i)),
             pl.BlockSpec((QUAD, 8, LANE), lambda i: (i, 0, 0)),
             pl.BlockSpec((1, 8, LANE), lambda i: (i, 0, 0)),
-        ],
+        ]
+        + [anywhere] * (2 * count),
         scratch_shapes=[
             pltpu.VMEM((CQ, seq, 3 * LANE), BF16),
             pltpu.VMEM((3 * LANE, 3 * LANE * CQ), BF16),
@@ -428,17 +555,21 @@
             pltpu.VMEM((2, seq, 3 * LANE), BF16),
             pltpu.VMEM((2, HEAD_DIM, seq), F32),
             pltpu.VMEM((CQ, LANE, LANE), F32),
-        ],
-        compiler_params=pltpu.CompilerParams(vmem_limit_bytes=56 * 1024 * 1024),
+            pltpu.VMEM((3, seq, block), BF16),
+            pltpu.SemaphoreType.DMA((3,)),
+        ]
+        + Reduce.scratch(specs, n),
+        compiler_params=pltpu.CompilerParams(
+            collective_id=collective, has_side_effects=True, vmem_limit_bytes=62 * 1024 * 1024
+        ),
     )(
         docs, head_mixing.reshape(HEADS // 2, 4), pad_taps(conv_kernel[:, :, ::-1]), gain.reshape(1, width),
-        projected, projected, projected, attended, d_grouped, soft,
+        projected, projected, projected, attended, d_grouped, soft, *grads,
     )
+    d_projected, grad_gain, grad_taps, grad_mix = results[:4]
     return (
-        dq, dk, dv, grad_gain.reshape(width),
-        jnp.roll(grad_taps, CK // 2 + 1, axis=2)[:, :CQ, :CK][:, :, ::-1] * SCALE,
-        grad_mix[:, :2, :4].reshape(HEADS // 2, 2, 2),
-    )
+        d_projected, grad_gain, grad_taps.reshape(-1, LANE), grad_mix.reshape(-1, LANE),
+    ), list(results[4 : 4 + count]), specs
 
 
 MESH = pl.DeviceIdType.MESH
@@ -605,20 +736,6 @@
         ]
 
 
-def gather_kernel(n, count, widths, *refs):
-    ring = Ring(n)
-    gather = Gather(ring, refs[:count], refs[count : 2 * count], widths, refs[2 * count :])
-    ring.meet()
-    gather.start()
-
-    def one(k, carry):
-        gather.step(k)
-        return carry
-
-    lax.fori_loop(0, n - 1, one, 0)
-    gather.finish()
-
-
 def share(shape):
     rows, columns = shape
     axis, unit = (0, 16) if rows % 64 == 0 else (1, LANE)
@@ -626,65 +743,76 @@
     return axis, -(-units // 3) * unit
 
 
-def gather_all(weights, n, collective):
-    count = len(weights)
-    widths = [share(w.shape) for w in weights]
-    anywhere = pl.BlockSpec(memory_space=pl.ANY)
-    return pl.pallas_call(
-        functools.partial(gather_kernel, n, count, widths),
-        out_shape=[jax.ShapeDtypeStruct((n * w.shape[0], w.shape[1]), w.dtype) for w in weights],
-        in_specs=[anywhere] * count,
-        out_specs=[anywhere] * count,
-        scratch_shapes=Gather.scratch(count, n),
-        compiler_params=pltpu.CompilerParams(collective_id=collective, has_side_effects=True),
-    )(*weights)
+def carried(columns, shared):
+    half = columns // 2
+    units = half // LANE
+    if not shared or units < 3:
+        return half // 2, 0
+    lanes = -(-units // 3) * LANE
+    return lanes, half - 2 * lanes
 
 
 class Reduce:
-    def __init__(self, ring, grads, totals, others, shapes, scratch):
-        self.ring, self.grads, self.totals, self.others, self.shapes = ring, grads, totals, others, shapes
+    def __init__(self, ring, grads, sums, others, specs, scratch):
+        self.ring, self.grads, self.sums, self.others, self.specs = ring, grads, sums, others, specs
         count = len(grads)
-        pairs = 2 * count
-        self.slots = [scratch[2 * i : 2 * i + 2] for i in range(count)]
-        scratch = scratch[pairs:]
-        self.mine = [scratch[2 * i : 2 * i + 2] for i in range(count)]
-        scratch = scratch[pairs:]
-        self.twin = [scratch[2 * i : 2 * i + 2] for i in range(count)]
-        scratch = scratch[pairs:]
-        self.plane = [scratch[2 * i : 2 * i + 2] for i in range(count)]
-        scratch = scratch[pairs:]
+        self.slots, self.mine, self.twin, self.x_slots, self.x_out = [], [], [], [], []
+        scratch = list(scratch)
+        for spec in specs:
+            part = carried(spec[1], spec[2])[1]
+            take = [scratch.pop(0) for _ in range(10 if part else 6)]
+            self.slots.append(take[:2])
+            self.mine.append(take[2:4] + take[6:7])
+            self.twin.append(take[4:6] + take[7:8])
+            self.x_slots.append(take[8] if part else None)
+            self.x_out.append(take[9] if part else None)
         (self.load, self.ring_send, self.ring_recv, self.core_send, self.core_recv,
-         self.end_send, self.end_recv, self.keep) = scratch
-
-    def owner(self, d, j):
+         self.x_send, self.x_recv, self.keep) = scratch
+
+    def owner(self, kind, j):
         ring = self.ring
-        return ring_index(ring.place + (j + 1 if d else -j - 1), ring.n)
-
-    def window(self, i, d, core):
-        rows, columns = self.shapes[i]
-        w = columns // 4
-        return core * 2 * w + d * w, w
+        return ring_index(ring.place + (j + 1 if kind == 1 else -j - 1), ring.n)
+
+    def span(self, i, kind):
+        columns, shared = self.specs[i][1:]
+        w, part = carried(columns, shared)
+        half = columns // 2
+        lower, upper = ((0, half - w), (w, half - 2 * w), (half - part, 0))[kind]
+        return jnp.where(self.ring.x == 0, lower, upper), part if kind == 2 else w
 
     def rows(self, i, index):
-        rows = self.shapes[i][0]
+        rows = self.specs[i][0]
         return pl.ds(pl.multiple_of(index * rows, 16), rows)
 
-    def core_copy(self, i, d, j):
+    def kinds(self, i):
+        return 3 if self.x_slots[i] is not None else 2
+
+    def core_copy(self, i, kind, j):
         ring = self.ring
-        start, w = self.window(i, d, 1 - ring.core)
-        rows = self.rows(i, self.owner(d, j))
+        start, width = self.span(i, kind)
+        rows = self.rows(i, self.owner(kind, j))
+        half = self.specs[i][1] // 2
         return send(
-            self.grads[i].at[rows, cols(start, w)], self.others[i].at[rows, d * w : (d + 1) * w],
-            self.core_send.at[i, d, j], self.core_recv.at[i, d, j], ring.sibling,
+            self.grads[i].at[rows, cols((1 - ring.core) * half + start, width)], self.others[i].at[rows, cols(start, width)],
+            self.core_send.at[i, kind, j], self.core_recv.at[i, kind, j], ring.sibling,
         )
 
-    def loads(self, i, d, j):
-        start, w = self.window(i, d, self.ring.core)
-        rows = self.rows(i, self.owner(d, j))
+    def loads(self, i, kind, j):
+        start, width = self.span(i, kind)
+        rows = self.rows(i, self.owner(kind, j))
+        base = self.ring.core * (self.specs[i][1] // 2)
         return (
-            pltpu.make_async_copy(self.grads[i].at[rows, cols(start, w)], self.mine[i][d], self.load.at[i, d, 0]),
-            pltpu.make_async_copy(self.others[i].at[rows, d * w : (d + 1) * w], self.twin[i][d], self.load.at[i, d, 1]),
+            pltpu.make_async_copy(
+                self.grads[i].at[rows, cols(base + start, width)], self.mine[i][kind], self.load.at[i, kind, 0]
+            ),
+            pltpu.make_async_copy(self.others[i].at[rows, cols(start, width)], self.twin[i][kind], self.load.at[i, kind, 1]),
         )
+
+    def fetch(self, i, kind, j):
+        own, other = self.loads(i, kind, j)
+        own.start()
+        self.core_copy(i, kind, j).wait_recv()
+        other.start()
 
     def ring_copy(self, i, d, j):
         ring = self.ring
@@ -693,53 +821,87 @@
             self.ring_send.at[i, d, j], self.ring_recv.at[i, d, j + 1], ring.left if d else ring.right,
         )
 
-    def arrived(self, i, d, j):
-        ring = self.ring
+    def gap(self, i):
+        w, part = carried(*self.specs[i][1:])
+        x = self.ring.x
+        return w - part, jnp.where(x == 0, part, 0), jnp.where(x == 0, w - part, 0), part
+
+    def x_copy(self, i, j):
+        _, _, at, part = self.gap(i)
         return send(
-            self.slots[i][d].at[j], self.slots[i][d].at[j],
-            self.ring_send.at[i, d, j], self.ring_recv.at[i, d, j], ring.left if d else ring.right,
+            self.x_out[i].at[lax.rem(j, 2)], self.x_slots[i].at[j, :, cols(at, part)],
+            self.x_send.at[i, j], self.x_recv.at[i, j], self.ring.across,
         )
 
-    def across_copy(self, i, d):
-        return send(
-            self.slots[i][d].at[self.ring.n - 1], self.plane[i][d],
-            self.end_send.at[i, d, 0], self.end_recv.at[i, d, 0], self.ring.across,
-        )
-
-    def final_copies(self, i, d):
-        start, w = self.window(i, d, self.ring.core)
-        there = self.totals[i].at[:, cols(start, w)]
-        return (
-            send(self.mine[i][d], there, self.end_send.at[i, d, 1], self.end_recv.at[i, d, 1], self.ring.sibling),
-            pltpu.make_async_copy(self.mine[i][d], there, self.keep.at[i, d]),
-        )
+    def give(self, i, j):
+        j = jnp.int32(j)
+        for copy in self.loads(i, 2, j):
+            copy.wait()
+
+        @pl.when(j >= 2)
+        def _():
+            self.x_copy(i, j - 2).wait_send()
+
+        self.x_out[i][lax.rem(j, 2)] = (self.mine[i][2][...].astype(F32) + self.twin[i][2][...].astype(F32)).astype(BF16)
+        self.x_copy(i, j).start()
+        self.hand_next(i, 2, j)
+
+        @pl.when(j < self.ring.n - 1)
+        def _():
+            self.fetch(i, 2, j + 1)
 
     def each(self):
-        return [(i, d) for i in range(len(self.grads)) for d in range(2)]
+        return [(i, d) for i in range(len(self.grads)) for d in (1, 0)]
+
+    def clear(self):
+        for i in range(len(self.grads)):
+            if self.kinds(i) == 3:
+                width, at, _, _ = self.gap(i)
+                if width:
+                    rows = self.specs[i][0]
+                    self.x_slots[i][:, :, cols(at, width)] = jnp.zeros((self.ring.n, rows, width), BF16)
+
+    def hand_over(self):
+        for j in range(min(LEAD, self.ring.n)):
+            for i in range(len(self.grads)):
+                for kind in reversed(range(self.kinds(i))):
+                    self.core_copy(i, kind, j).start()
+
+    def hand_next(self, i, kind, j):
+        pl.when(j + LEAD < self.ring.n)(lambda: self.core_copy(i, kind, j + LEAD).start())
+
+    def fetch_first(self):
+        for i in range(len(self.grads)):
+            for kind in reversed(range(self.kinds(i))):
+                self.fetch(i, kind, 0)
+
+    def give_all(self, j):
+        for i in range(len(self.grads)):
+            if self.kinds(i) == 3:
+                self.give(i, j)
+
+    def opening(self):
+        return [
+            self.hand_over, self.fetch_first,
+            functools.partial(self.give_all, 0), functools.partial(self.give_all, 1),
+        ]
 
     def start(self):
-        def give(j, carry):
-            for i, d in self.each():
-                self.core_copy(i, d, j).start()
-            return carry
-
-        lax.fori_loop(0, self.ring.n, give, 0)
-        for i, d in self.each():
-            self.fetch(i, d, 0)
-
-    def fetch(self, i, d, j):
-        own, other = self.loads(i, d, j)
-        own.start()
-        self.core_copy(i, d, j).wait_recv()
-        other.start()
-
-    def item(self, j):
+        for step in self.opening():
+            step()
+
+    def item(self, j, work):
         last = self.ring.n - 1
-        for i, d in self.each():
+        for i, d in work:
+            if d == 0 and self.kinds(i) == 3:
+                pl.when(j < last - 1)(functools.partial(self.give, i, j + 2))
             for copy in self.loads(i, d, j):
                 copy.wait()
             slot = self.slots[i][d]
             both = self.mine[i][d][...].astype(F32) + self.twin[i][d][...].astype(F32)
+            if d == 0 and self.kinds(i) == 3:
+                self.x_copy(i, j).wait_recv()
+                both = both + self.x_slots[i][j].astype(F32)
 
             @pl.when(j == 0)
             def _():
@@ -747,7 +909,7 @@
 
             @pl.when(j > 0)
             def _():
-                self.arrived(i, d, j).wait_recv()
+                self.ring_copy(i, d, j - 1).wait_recv()
                 slot[j] = (slot[j].astype(F32) + both).astype(BF16)
 
             @pl.when(j < last)
@@ -755,78 +917,530 @@
                 self.ring_copy(i, d, j).start()
                 self.fetch(i, d, j + 1)
 
+            self.hand_next(i, d, j)
+
+            @pl.when(j == last)
+            def _():
+                self.keep_copy(i, d).start()
+
+    def keep_copy(self, i, d):
+        w = carried(*self.specs[i][1:])[0]
+        at = jnp.where(self.ring.x == 0, d * w, (1 - d) * w)
+        return pltpu.make_async_copy(self.slots[i][d].at[self.ring.n - 1], self.sums[i].at[:, cols(at, w)], self.keep.at[i, d])
+
     def finish(self):
         last = self.ring.n - 1
         for i, d in self.each():
-            self.across_copy(i, d).start()
-        for i, d in self.each():
-            self.across_copy(i, d).wait()
-            both = self.slots[i][d][last].astype(F32) + self.plane[i][d][...].astype(F32)
-            self.mine[i][d][...] = both.astype(BF16)
-            for copy in self.final_copies(i, d):
+            self.keep_copy(i, d).wait()
+
+        def settle(j, carry):
+            for i in range(len(self.grads)):
+                for kind in range(self.kinds(i)):
+                    self.core_copy(i, kind, j).wait_send()
+                for d in range(2):
+                    pl.when(j < last)(lambda i=i, d=d: self.ring_copy(i, d, j).wait_send())
+                if self.kinds(i) == 3:
+                    pl.when(j >= last - 1)(lambda i=i: self.x_copy(i, j).wait_send())
+            return carry
+
+        lax.fori_loop(0, self.ring.n, settle, 0)
+
+    @staticmethod
+    def specs_of(grads, n, shared):
+        return [(g.shape[0] // n, g.shape[1], shared) for g in grads]
+
+    @staticmethod
+    def results(specs, n):
+        return [
+            jax.ShapeDtypeStruct((rows, 2 * carried(columns, shared)[0]), BF16) for rows, columns, shared in specs
+        ] + [jax.ShapeDtypeStruct((n * rows, columns // 2), BF16) for rows, columns, _ in specs]
+
+    @staticmethod
+    def scratch(specs, n):
+        dma = pltpu.SemaphoreType.DMA
+        count = len(specs)
+        buffers = []
+        for rows, columns, shared in specs:
+            w, part = carried(columns, shared)
+            buffers += [pltpu.VMEM((n, rows, w), BF16)] * 2 + [pltpu.VMEM((rows, w), BF16)] * 4
+            if part:
+                buffers += [pltpu.VMEM((rows, part), BF16)] * 2
+                buffers += [pltpu.VMEM((n, rows, w), BF16), pltpu.VMEM((2, rows, part), BF16)]
+        return buffers + [
+            dma((count, 3, 2)), dma((count, 2, n)), dma((count, 2, n)), dma((count, 3, n)), dma((count, 3, n)),
+            dma((count, n)), dma((count, n)), dma((count, 2)),
+        ]
+
+
+class FinalSum:
+    def __init__(self, ring, sums, totals, specs, scratch):
+        self.ring, self.sums, self.totals, self.specs = ring, sums, totals, specs
+        scratch = list(scratch)
+        self.mine, self.plane, self.own = [], [], []
+        for spec in specs:
+            self.mine.append(scratch.pop(0))
+            self.plane.append(scratch.pop(0))
+            self.own.append(scratch.pop(0) if carried(spec[1], spec[2])[1] else None)
+        self.local, self.remote_send, self.remote_recv = scratch
+
+    def spans(self, i):
+        columns, shared = self.specs[i][1:]
+        w, part = carried(columns, shared)
+        half, wide = columns // 2, 2 * w - part
+        base = self.ring.core * half
+        low = self.ring.x == 0
+        return (
+            (jnp.where(low, part, 0), base + part, wide),
+            (jnp.where(low, 0, wide), base + jnp.where(low, 0, half - part), part),
+            (0, base + jnp.where(low, half - part, 0), part),
+        )
+
+    def remote(self, i, at, src, dst, device):
+        return send(src, dst, self.remote_send.at[i, at], self.remote_recv.at[i, at], device)
+
+    def copy(self, i, name):
+        ring, sums, totals = self.ring, self.sums[i], self.totals[i]
+        (a, a_out, wide), (b, b_out, part), (_, c_out, _) = self.spans(i)
+        local = {"load": 0, "save": 1, "load done": 2, "save done": 3}
+        remote = {"across": 0, "sibling": 1, "done across": 2, "done sibling": 3, "pass on": 4}
+        if name in ("load", "save", "across", "sibling"):
+            src, dst, mid = sums.at[:, cols(a, wide)], totals.at[:, cols(a_out, wide)], self.mine[i]
+        elif name == "pass on":
+            src = dst = mid = totals.at[:, cols(c_out, part)]
+        else:
+            src, dst, mid = sums.at[:, cols(b, part)], totals.at[:, cols(b_out, part)], self.own[i]
+        if name in local:
+            ends = (src, mid) if name.startswith("load") else (mid, dst)
+            return pltpu.make_async_copy(*ends, self.local.at[i, local[name]])
+        ends = {"across": (src, self.plane[i]), "sibling": (mid, dst)}.get(name, (src, dst))
+        device = ring.across if "across" in name else ring.sibling
+        at = remote[name]
+        return send(*ends, self.remote_send.at[i, at], self.remote_recv.at[i, at], device)
+
+    def shares(self, i):
+        return carried(*self.specs[i][1:])[1] > 0
+
+    def start(self):
+        for i in range(len(self.specs)):
+            for name in ("across", "load"):
+                self.copy(i, name).start()
+            if self.shares(i):
+                for name in ("done across", "load done", "done sibling"):
+                    self.copy(i, name).start()
+
+    def add(self, i):
+        self.copy(i, "load").wait()
+        self.copy(i, "across").wait_recv()
+        self.mine[i][...] = (self.mine[i][...].astype(F32) + self.plane[i][...].astype(F32)).astype(BF16)
+        self.copy(i, "sibling").start()
+        self.copy(i, "save").start()
+        if self.shares(i):
+            self.copy(i, "load done").wait()
+            self.copy(i, "save done").start()
+            self.copy(i, "done across").wait_recv()
+            self.copy(i, "pass on").start()
+
+    def finish(self):
+        for i in range(len(self.specs)):
+            self.copy(i, "across").wait_send()
+            self.copy(i, "sibling").wait()
+            self.copy(i, "save").wait()
+            if self.shares(i):
+                self.copy(i, "done across").wait_send()
+                for name in ("done sibling", "save done", "pass on"):
+                    self.copy(i, name).wait()
+
+    @staticmethod
+    def scratch(specs):
+        dma = pltpu.SemaphoreType.DMA
+        count = len(specs)
+        buffers = []
+        for rows, columns, shared in specs:
+            w, part = carried(columns, shared)
+            buffers += [pltpu.VMEM((rows, 2 * w - part), BF16)] * 2
+            if part:
+                buffers += [pltpu.VMEM((rows, part), BF16)]
+        return buffers + [dma((count, 4)), dma((count, 5)), dma((count, 5))]
+
+
+class SmallSum:
+    def __init__(self, ring, given, total, scratch):
+        self.ring, self.given, self.total = ring, given, total
+        self.mine, self.twin, self.plane, self.slots, self.pair, self.ring_send, self.ring_recv = scratch
+
+    def copy(self, src, dst, at, device):
+        return send(src, dst, self.pair.at[0, at], self.pair.at[1, at], device)
+
+    def start(self):
+        ring = self.ring
+        copy = self.copy(self.given, self.twin, 0, ring.sibling)
+        copy.start()
+        copy.wait()
+        self.mine[...] = self.given[...] + self.twin[...]
+        copy = self.copy(self.mine, self.plane, 1, ring.across)
+        copy.start()
+        copy.wait()
+        self.slots[0] = self.mine[...] + self.plane[...]
+
+    def ring_copy(self, j):
+        return send(
+            self.slots.at[j], self.slots.at[j + 1], self.ring_send.at[j], self.ring_recv.at[j + 1], self.ring.right
+        )
+
+    def item(self, j):
+        @pl.when(j > 0)
+        def _():
+            self.ring_copy(j - 1).wait_recv()
+
+        @pl.when(j < self.ring.n - 1)
+        def _():
+            self.ring_copy(j).start()
+
+    def finish(self):
+        ring = self.ring
+        total = jnp.zeros(self.total.shape, F32)
+        for place in range(ring.n):
+            total = total + self.slots[lax.rem(ring.place - place + ring.n, ring.n)]
+        self.total[...] = total
+
+        def settle(j, carry):
+            self.ring_copy(j).wait_send()
+            return carry
+
+        lax.fori_loop(0, ring.n - 1, settle, 0)
+
+    @staticmethod
+    def scratch(rows, n):
+        dma = pltpu.SemaphoreType.DMA
+        block = pltpu.VMEM((rows, LANE), F32)
+        return [block, block, block, pltpu.VMEM((n, rows, LANE), F32), dma((2, 2)), dma((n,)), dma((n,))]
+
+
+SMALL_SCRATCH = 7
+
+
+NORM_ROUNDS = 3
+
+
+def pack(given, at, value):
+    if value.shape[0] == 1:
+        for r in range(value.shape[1] // LANE):
+            given[at + r : at + r + 1, :] = value[:, r * LANE : (r + 1) * LANE]
+        return at + value.shape[1] // LANE
+    given[at : at + value.shape[0], :] = value
+    return at + value.shape[0]
+
+
+def last_kernel(n, specs, early_specs, chunk, small_count, *refs):
+    count, early = len(specs), len(early_specs)
+    ring = Ring(n)
+    refs = list(refs)
+
+    def take(size):
+        taken = refs[:size]
+        del refs[:size]
+        return taken
+
+    small_refs = take(small_count)
+    input_ref, gain_ref, d_middle_ref, d_projected, weight = take(5)
+    grads, early_sums = take(count), take(early)
+    grad_input_ref, total_ref = take(2)
+    totals, early_totals, sums, others = take(count), take(early), take(count), take(count)
+    given, d_normed, in_left, in_right, in_sem = take(5)
+    small = SmallSum(ring, given, total_ref, take(SMALL_SCRATCH))
+    last_sum = FinalSum(ring, sums, totals, specs, take(len(FinalSum.scratch(specs))))
+    early_sum = FinalSum(ring, early_sums, early_totals, early_specs, take(len(FinalSum.scratch(early_specs))))
+    reduce = Reduce(ring, grads, sums, others, specs, refs)
+    chunks = d_projected.shape[1] // chunk
+    turns = -(-chunks // NORM_ROUNDS)
+
+    def arrive(t, slot):
+        at = cols(t * chunk, chunk)
+        return (
+            pltpu.make_async_copy(d_projected.at[:, at], in_left.at[slot], in_sem.at[slot, 0]),
+            pltpu.make_async_copy(weight.at[:, at], in_right.at[slot], in_sem.at[slot, 1]),
+        )
+
+    for copy in arrive(0, 0):
+        copy.start()
+    reduce.clear()
+    ring.meet()
+    d_normed[...] = jnp.zeros_like(d_normed)
+    given[...] = jnp.zeros_like(given)
+    reduce.start()
+
+    def turn(t):
+        slot = lax.rem(t, 2)
+        for copy in arrive(t, slot):
+            copy.wait()
+
+        @pl.when(t < chunks - 1)
+        def _():
+            for copy in arrive(t + 1, 1 - slot):
                 copy.start()
-        for i, d in self.each():
-            for copy in self.final_copies(i, d):
-                copy.wait()
-
-        def settle(j, carry):
-            for i, d in self.each():
-                self.core_copy(i, d, j).wait_send()
-
-                @pl.when(j < last)
-                def _():
-                    self.ring_copy(i, d, j).wait_send()
-
-            return carry
-
-        lax.fori_loop(0, self.ring.n, settle, 0)
-
-    @staticmethod
-    def scratch(shapes, n):
-        dma = pltpu.SemaphoreType.DMA
-        count = len(shapes)
-        blocks = [(rows, columns // 4) for rows, columns in shapes for _ in range(2)]
-        return (
-            [pltpu.VMEM((n,) + b, BF16) for b in blocks]
-            + [pltpu.VMEM(b, BF16) for b in blocks] * 3
-            + [
-                dma((count, 2, 2)), dma((count, 2, n)), dma((count, 2, n)), dma((count, 2, n)), dma((count, 2, n)),
-                dma((count, 2, 2)), dma((count, 2, 2)), dma((count, 2)),
-            ]
-        )
-
-
-def reduce_kernel(n, shapes, *refs):
-    count = len(shapes)
-    ring = Ring(n)
-    reduce = Reduce(ring, refs[:count], refs[count : 2 * count], refs[2 * count : 3 * count], shapes, refs[3 * count :])
-    ring.meet()
-    reduce.start()
-
-    def one(j, carry):
-        reduce.item(j)
+
+        d_normed[...] += nt(in_left[slot], in_right[slot])
+
+    def first(j, carry):
+        reduce.item(j, reduce.each())
+        for k in range(turns):
+            t = j * turns + k
+            pl.when(t < chunks)(functools.partial(turn, t))
         return carry
 
-    lax.fori_loop(0, n, one, 0)
+    lax.fori_loop(0, NORM_ROUNDS, first, 0)
+    values = input_ref[...].astype(F32)
+    scale = lax.rsqrt(jnp.mean(values * values, axis=1, keepdims=True) + EPSILON)
+    upstream = d_normed[...]
+    grad_gain = jnp.sum(upstream * (values * scale), axis=0, keepdims=True)
+    at = pack(given, 0, grad_gain)
+    for ref in small_refs:
+        at = pack(given, at, ref[...])
+    scaled = upstream * gain_ref[...]
+    inner = jnp.mean(scaled * values, axis=1, keepdims=True)
+    grad_input_ref[...] = d_middle_ref[...] + scale * scaled - values * (scale * scale * scale * inner)
+    small.start()
+    early_sum.start()
+    rounds = n - NORM_ROUNDS
+    hops = -(-n // rounds)
+
+    def rest(j, carry):
+        reduce.item(j, reduce.each())
+        for hop in range(hops):
+            at = (j - NORM_ROUNDS) * hops + hop
+            pl.when(at < n)(functools.partial(small.item, at))
+        for i in range(early):
+            pl.when(j == n - early + i)(functools.partial(early_sum.add, i))
+        return carry
+
+    lax.fori_loop(NORM_ROUNDS, n, rest, 0)
     reduce.finish()
-
-
-def reduce_all(grads, n, collective):
-    count = len(grads)
-    shapes = [(g.shape[0] // n, g.shape[1]) for g in grads]
+    last_sum.start()
+    small.finish()
+    for i in range(count):
+        last_sum.add(i)
+    early_sum.finish()
+    last_sum.finish()
+
+
+def last_step(
+    d_projected, qkv_weight, layer_input, first_gain, d_middle, grads, smalls, early_sums, early_specs, n, collective
+):
+    count, early = len(grads), len(early_specs)
+    seq, width = layer_input.shape
+    chunk = 512
+    specs = Reduce.specs_of(grads, n, False)
+    sizes = [v.size // LANE for v in [first_gain] + smalls]
+    rows = -(-sum(sizes) // 8) * 8
     anywhere = pl.BlockSpec(memory_space=pl.ANY)
+    whole = pl.BlockSpec(memory_space=pltpu.VMEM)
     results = pl.pallas_call(
-        functools.partial(reduce_kernel, n, shapes),
-        out_shape=[jax.ShapeDtypeStruct(s, BF16) for s in shapes]
-        + [jax.ShapeDtypeStruct((n * rows, columns // 2), BF16) for rows, columns in shapes],
-        in_specs=[anywhere] * count,
-        out_specs=[anywhere] * (2 * count),
-        scratch_shapes=Reduce.scratch(shapes, n),
+        functools.partial(last_kernel, n, specs, early_specs, chunk, len(smalls)),
+        out_shape=[jax.ShapeDtypeStruct((seq, width), F32), jax.ShapeDtypeStruct((rows, LANE), F32)]
+        + [jax.ShapeDtypeStruct(spec[:2], BF16) for spec in specs + early_specs]
+        + Reduce.results(specs, n),
+        in_specs=[whole] * (len(smalls) + 3) + [anywhere] * (2 + count + early),
+        out_specs=[whole] * 2 + [anywhere] * (3 * count + early),
+        scratch_shapes=[
+            pltpu.VMEM((rows, LANE), F32),
+            pltpu.VMEM((seq, width), F32),
+            pltpu.VMEM((2, seq, chunk), BF16),
+            pltpu.VMEM((2, width, chunk), BF16),
+            pltpu.SemaphoreType.DMA((2, 2)),
+        ]
+        + SmallSum.scratch(rows, n)
+        + FinalSum.scratch(specs)
+        + FinalSum.scratch(early_specs)
+        + Reduce.scratch(specs, n),
         compiler_params=pltpu.CompilerParams(
             collective_id=collective, has_side_effects=True, vmem_limit_bytes=60 * 1024 * 1024
         ),
-    )(*grads)
-    return results[:count]
+    )(*smalls, layer_input, first_gain.reshape(1, width), d_middle, d_projected, qkv_weight, *grads, *early_sums)
+    out, at = [], 0
+    for size in sizes:
+        out.append(results[1][at : at + size])
+        at += size
+    return results[0], results[2 : 2 + count + early], out
+
+
+TILES = 8
+EARLY_TILES = 3
+
+
+def mlp_kernel(n, specs, tile, *refs):
+    refs = list(refs)
+
+    def take(size):
+        taken = refs[:size]
+        del refs[:size]
+        return taken
+
+    second_ref, upstream_ref, middle, inner, down = take(5)
+    out_ref, d_second_ref = take(2)
+    (early, late, grad_down), sums, others = take(3), take(1), take(1)
+    turned, out_sum, in_gate, in_up, in_down, to_gate, to_up, to_down = take(8)
+    middle_sem, in_sem, to_sem = take(3)
+    reduce = Reduce(Ring(n), [early], sums, others, specs, refs)
+    hidden_size = down.shape[0]
+    tiles = hidden_size // tile
+    begun = EARLY_TILES
+    each = -(-n // (tiles - begun - 1))
+    due = -(-each // 2)
+
+    def arrive(t, slot):
+        at = pl.multiple_of(t * tile, tile)
+        return (
+            pltpu.make_async_copy(inner.at[:, pl.ds(at, tile)], in_gate.at[slot], in_sem.at[slot, 0]),
+            pltpu.make_async_copy(
+                inner.at[:, pl.ds(pl.multiple_of(hidden_size + at, tile), tile)], in_up.at[slot], in_sem.at[slot, 1]
+            ),
+            pltpu.make_async_copy(down.at[pl.ds(at, tile), :], in_down.at[slot], in_sem.at[slot, 2]),
+        )
+
+    def leave(grad, t, slot, first, count):
+        at = pl.multiple_of((t - first) * tile, tile)
+        return (
+            pltpu.make_async_copy(to_gate.at[slot], grad.at[:, pl.ds(at, tile)], to_sem.at[slot, 0]),
+            pltpu.make_async_copy(
+                to_up.at[slot], grad.at[:, pl.ds(pl.multiple_of(count * tile + at, tile), tile)], to_sem.at[slot, 1]
+            ),
+            pltpu.make_async_copy(
+                to_down.at[slot], grad_down.at[pl.ds(pl.multiple_of(t * tile, tile), tile), :], to_sem.at[slot, 2]
+            ),
+        )
+
+    def leave_early(t):
+        return leave(early, t, lax.rem(t, 2), 0, begun)
+
+    def leave_late(t):
+        return leave(late, t, lax.rem(t, 2), begun, tiles - begun)
+
+    first = pltpu.make_async_copy(middle, out_sum, middle_sem)
+    first.start()
+    for copy in arrive(0, 0):
+        copy.start()
+    reduce.clear()
+    reduce.ring.meet()
+    turned[...] = second_ref[...].T
+    d_second_ref[...] = jnp.zeros_like(d_second_ref)
+    first.wait()
+
+    def serve(t, point):
+        @pl.when(t == begun)
+        def _():
+            if point == 0:
+                for back in (2, 1):
+                    for copy in leave_early(t - back):
+                        copy.wait()
+            reduce.opening()[point]()
+
+        for step in range(due):
+            if point // 2 * due + step < each:
+                j = (t - begun - 1) * each + point // 2 * due + step
+                pl.when((t > begun) & (j < n))(functools.partial(reduce.item, j, [(0, 1 - point % 2)]))
+
+    def one(t, carry):
+        slot = lax.rem(t, 2)
+        for copy in arrive(t, slot):
+            copy.wait()
+
+        @pl.when(t < tiles - 1)
+        def _():
+            for copy in arrive(t + 1, 1 - slot):
+                copy.start()
+
+        second, upstream = second_ref[...], upstream_ref[...]
+        gate = nn(second, in_gate[slot])
+        up = nn(second, in_up[slot])
+        sigmoid = jax.nn.sigmoid(gate)
+        silu = gate * sigmoid
+        hidden = (silu * up).astype(BF16)
+        serve(t, 0)
+        d_hidden = nt(upstream, in_down[slot])
+        out_sum[...] += nn(hidden, in_down[slot])
+
+        @pl.when((t >= 2) & (t < begun))
+        def _():
+            for copy in leave_early(t - 2):
+                copy.wait()
+
+        @pl.when(t >= begun + 2)
+        def _():
+            for copy in leave_late(t - 2):
+                copy.wait()
+
+        to_down[slot] = nn(hidden.T, upstream).astype(BF16)
+        d_gate = (d_hidden * up * sigmoid * (1.0 + gate * (1.0 - sigmoid))).astype(BF16)
+        d_up = (d_hidden * silu).astype(BF16)
+        serve(t, 1)
+        d_second_ref[...] += nt(d_gate, in_gate[slot])
+        to_gate[slot] = nn(turned[...], d_gate).astype(BF16)
+        serve(t, 2)
+        d_second_ref[...] += nt(d_up, in_up[slot])
+        to_up[slot] = nn(turned[...], d_up).astype(BF16)
+        serve(t, 3)
+
+        @pl.when(t < begun)
+        def _():
+            for copy in leave_early(t):
+                copy.start()
+
+        @pl.when(t >= begun)
+        def _():
+            for copy in leave_late(t):
+                copy.start()
+
+        return carry
+
+    lax.fori_loop(0, tiles, one, 0)
+    out_ref[...] = out_sum[...].astype(BF16)
+    for t in (tiles - 2, tiles - 1):
+        for copy in leave_late(t):
+            copy.wait()
+    reduce.finish()
+
+
+def feed_forward(second, upstream, middle, inner, down, n, collective):
+    seq, width = second.shape
+    hidden_size = down.shape[0]
+    tile = hidden_size // TILES
+    early = EARLY_TILES * tile
+    specs = [(width // n, 2 * early, True)]
+    whole = pl.BlockSpec(memory_space=pltpu.VMEM)
+    anywhere = pl.BlockSpec(memory_space=pl.ANY)
+    dma = pltpu.SemaphoreType.DMA
+    results = pl.pallas_call(
+        functools.partial(mlp_kernel, n, specs, tile),
+        out_shape=[
+            jax.ShapeDtypeStruct((seq, width), BF16),
+            jax.ShapeDtypeStruct((seq, width), F32),
+        ]
+        + [
+            jax.ShapeDtypeStruct((width, 2 * early), BF16),
+            jax.ShapeDtypeStruct((width, 2 * (hidden_size - early)), BF16),
+            jax.ShapeDtypeStruct((hidden_size, width), BF16),
+        ]
+        + Reduce.results(specs, n),
+        in_specs=[whole, whole, anywhere, anywhere, anywhere],
+        out_specs=[whole, whole] + [anywhere] * 5,
+        scratch_shapes=[
+            pltpu.VMEM((width, seq), BF16),
+            pltpu.VMEM((seq, width), F32),
+            pltpu.VMEM((2, width, tile), BF16),
+            pltpu.VMEM((2, width, tile), BF16),
+            pltpu.VMEM((2, tile, width), BF16),
+            pltpu.VMEM((2, width, tile), BF16),
+            pltpu.VMEM((2, width, tile), BF16),
+            pltpu.VMEM((2, tile, width), BF16),
+            dma, dma((2, 3)), dma((2, 3)),
+        ]
+        + Reduce.scratch(specs, n),
+        compiler_params=pltpu.CompilerParams(
+            collective_id=collective, has_side_effects=True, vmem_limit_bytes=62 * 1024 * 1024
+        ),
+    )(second, upstream, middle, inner, down)
+    out, d_second, _, late, grad_down, sums, _ = results
+    return out, d_second, late, grad_down, [sums], specs
 
 
 def rms_norm(values, gains):
@@ -869,58 +1483,40 @@
     cotangent,
 ):
     n = lax.axis_size("fsdp")
-    (qkv_weight,) = gather_all([qkv_weight], n, 0)
-    out_weight, inner_weight, down_weight = gather_all([out_weight, inner_weight, down_weight], n, 1)
-    inputs = layer_input.astype(jnp.float32)
-    normed_value, first_pull = jax.vjp(rms_norm, inputs, first_gain)
-    normed = normed_value.astype(jnp.bfloat16)
-    projected = project(normed, qkv_weight).astype(jnp.bfloat16)
-    grouped, attended, soft = attend_forward(
-        projected, conv_kernel, head_mixing, doc_lengths, group_gain
+    kept, (qkv_weight, out_weight), (inner_weight, down_weight) = attend_forward(
+        layer_input, conv_kernel, head_mixing, doc_lengths, (first_gain, group_gain, second_gain),
+        [qkv_weight, out_weight], [inner_weight, down_weight], n, 0,
     )
-    middle = inputs + project(grouped, out_weight)
-    second_value, second_pull = jax.vjp(rms_norm, middle, second_gain)
-    second = second_value.astype(jnp.bfloat16)
-    gate_up = project(second, inner_weight)
-    hidden_value, swiglu_pull = jax.vjp(swiglu, gate_up)
-    hidden = hidden_value.astype(jnp.bfloat16)
-    layer_output = (middle + project(hidden, down_weight)).astype(jnp.bfloat16)
-    upstream = cotangent.astype(jnp.float32)
-    grad_down = weight_grad(hidden, cotangent)
-    d_hidden = project_back(cotangent, down_weight)
-    d_gate_up = swiglu_pull(d_hidden)[0].astype(jnp.bfloat16)
-    grad_inner = weight_grad(second, d_gate_up)
-    d_second = project_back(d_gate_up, inner_weight)
+    grouped, attended, soft, normed, middle, second, projected = kept
+    second_pull = jax.vjp(rms_norm, middle, second_gain)[1]
+    layer_output, d_second, late_inner, grad_down, early_sums, early_specs = feed_forward(
+        second, cotangent, middle, inner_weight, down_weight, n, 2
+    )
     d_middle, grad_second = second_pull(d_second)
-    d_middle = upstream + d_middle
+    d_middle = cotangent.astype(F32) + d_middle
     d_branch = d_middle.astype(jnp.bfloat16)
     grad_proj = weight_grad(grouped, d_branch)
     d_grouped = project_back(d_branch, out_weight)
-    d_query, d_keys, d_values, grad_group, grad_kernel, grad_mixing = attend_backward(
-        projected, conv_kernel, head_mixing, doc_lengths, group_gain, attended, d_grouped, soft
+    (d_projected, grad_group, grad_kernel, grad_mixing), sums, specs = attend_backward(
+        projected, conv_kernel, head_mixing, doc_lengths, group_gain, attended, d_grouped, soft,
+        [late_inner, grad_down, grad_proj], n, 3,
     )
-    d_projected = jnp.concatenate([d_query, d_keys, d_values], axis=1)
     grad_qkv = weight_grad(normed, d_projected)
-    d_normed = project_back(d_projected, qkv_weight)
-    d_inputs, grad_first = first_pull(d_normed)
-    grad_input = d_middle + d_inputs
-    small = lax.psum(
-        (grad_first, grad_kernel, grad_mixing, grad_group, grad_second), ("rep", "fsdp")
+    grad_input, shards, small = last_step(
+        d_projected, qkv_weight, layer_input, first_gain, d_middle, [grad_qkv],
+        [grad_group, grad_second.reshape(1, -1), grad_kernel, grad_mixing], early_sums + sums, early_specs + specs, n, 4,
     )
-    shards = reduce_all([grad_down, grad_inner, grad_proj, grad_qkv], n, 2)
-    shards = [shards[i].astype(F32) for i in (3, 2, 1, 0)]
+    grad_first, grad_group, grad_second = [g.reshape(-1) for g in small[:3]]
+    grad_kernel = jnp.roll(small[3].reshape(HEADS, 8, LANE), CK // 2 + 1, axis=2)[:, :CQ, :CK][:, :, ::-1] * SCALE
+    grad_mixing = small[4].reshape(-1, 8, LANE)[:, :2, :4].reshape(HEADS // 2, 2, 2)
+    early_half, late_half = shards[1].shape[1] // 2, shards[2].shape[1] // 2
+    grad_inner = jnp.concatenate(
+        [shards[1][:, :early_half], shards[2][:, :late_half], shards[1][:, early_half:], shards[2][:, late_half:]], axis=1
+    )
+    shards = [g.astype(F32) for g in (shards[0], shards[4], grad_inner, shards[3])]
     return (
-        layer_output,
-        grad_input,
-        small[0],
-        shards[0],
-        small[1],
-        small[2],
-        small[3],
-        shards[1],
-        small[4],
-        shards[2],
-        shards[3],
+        layer_output, grad_input, grad_first, shards[0], grad_kernel, grad_mixing, grad_group, shards[1], grad_second,
+        shards[2], shards[3],
     )
 
 

time: 987 us -> 660 us (0.67)
  matrix products: 171 us -> 21.1 us
  Pallas kernels: 727 us -> 594 us
  blocking collectives: 42.5 us -> 0 us
    pallas_call x5 -> x4, Pallas kernels: 727 us -> 594 us  [the longest x1 224 us: attend_forward(): pl.pallas_call(functools.partial(forward_kernel, n, first_widths, rest_wi...]
    dot_general x4 -> x1, matrix products: 66.6 us -> 4.3 us  [project_back(): lax.dot_general(upstream, weight, (((1,), (1,)), ((), ())), preferred_ele...]
    dot_general x4 -> x0, matrix products: 52.8 us -> none  [project(): return jnp.dot(operand, weight, preferred_element_type=F32)]
    psum x1 -> x0, blocking collectives: 42.5 us -> none  [body(): lax.psum((grad_first, grad_kernel, grad_mixing, grad_group, grad_second),...]
    dot_general x4 -> x2, matrix products: 52.1 us -> 16.8 us  [weight_grad(): lax.dot_general(operand, upstream, (((0,), (0,)), ((), ())), preferred_el...]
where the time goes in v3:
time: 660 us; the launch traced here: 652 us
  Pallas kernels  594 us (90%)
  matrix products  21.1 us (3%)
  local copies, waits for them, and re-layouts  18.7 us (3%)
  other arithmetic  16.1 us (2%)
    pallas_call x1, Pallas kernels, attend_forward(): pl.pallas_call(functools.partial(forward_kernel, n, first_widths, rest_wi...  224 us
    pallas_call x1, Pallas kernels, attend_backward(): pl.pallas_call(functools.partial(backward_kernel, n, specs), grid=(quads,...  150 us
    pallas_call x1, Pallas kernels, last_step(): pl.pallas_call(functools.partial(last_kernel, n, specs, early_specs, chun...  125 us
    pallas_call x1, Pallas kernels, feed_forward(): pl.pallas_call(functools.partial(mlp_kernel, n, specs, tile), out_shape=[...  95.1 us
    dot_general x2, matrix products, weight_grad(): lax.dot_general(operand, upstream, (((0,), (0,)), ((), ())), preferred_el...  16.8 us

profile of v3, /device:TPU:0, one launch (start us, length us, event | category | flops | bytes accessed | tf_op | source)
XLA Modules:
  0.0 651.5 jit_solution(13027951156128236940)
XLA Ops:
  0.6 0.9 copy.29
  1.6 0.1 pad_slice_fusion.3
  1.7 0.7 pad_maximum_fusion.1.taps_ref
  2.4 1.3 reshape.85.gain_ref
  3.7 1.3 reshape.86.first_gain_ref.refs_5_
  5.0 1.3 copy.30.mix_ref
  6.3 1.3 reshape.87.second_gain_ref
  7.6 223.5 %shard_map.203 = (bf16[512,1536]{1,0:T(8,128)(2,1)}, f32[512,1536]{1,0:T(8,128)}, bf16[16,512,384]{2,1,0:T(8,128)(2,1)}, bf16[512,1536]{1,0:T(8,128)(2,1)}, f32[...) custom-call(s32[1,4]{1,0:T(1,128)} %docs_ref.3, ...), custom_call_target="tpu_custom_call" | custom-call | tf_op jit(solution)/shard_map/pallas_call | solution.py:285
  231.2 0.0 copy-start.10
  231.2 95.1 %shard_map.204 = (bf16[512,1536]{1,0:T(8,128)(2,1)}, f32[512,1536]{1,0:T(8,128)}, bf16[1536,3072]{1,0:T(8,128)(2,1)}, bf16[1536,5120]{1,0:T(8,128)(2,1)}, bf16[4...) custom-call(bf16[512,1536]{1,0:T(8,128)(2,1)} %get-tuple-element.41.refs_0_, ...), custom_call_target="tpu_custom_call" | custom-call | tf_op jit(solution)/shard_map/pallas_call | solution.py:1412
  326.3 0.0 copy-start
  326.3 2.3 multiply_reduce_fusion.2
  328.6 0.0 copy-done.10
  328.6 0.5 copy-done
  329.1 3.0 multiply_reduce_fusion
  332.1 0.0 copy-done.2
  332.1 0.3 copy-done.3
  332.4 0.8 fusion.refs_6_
  333.2 0.0 copy-start.1
  333.2 0.6 copy-done.12
  333.8 4.3 convolution_convert_fusion.1.refs_2_
  338.1 0.0 copy-done.1
  338.1 4.3 fusion.2.d_grouped_ref
  342.4 0.1 rev.6
  342.5 0.1 pad_slice_fusion.1
  342.6 0.7 pad_maximum_fusion.2.taps_ref
  343.3 150.4 %shard_map.205 = (bf16[512,4608]{1,0:T(8,128)(2,1)}, f32[1,1536]{1,0:T(1,128)}, f32[16,8,128]{2,1,0:T(8,128)}, f32[4,8,128]{2,1,0:T(8,128)}, bf16[192,1792]{1,0:...) custom-call(s32[1,4]{1,0:T(1,128)} %docs_ref.3, ...), custom_call_target="tpu_custom_call" | custom-call | tf_op jit(solution)/shard_map/pallas_call | solution.py:522
  493.8 12.6 %convolution_convert_fusion.refs_9_ = bf16[1536,4608]{1,0:T(8,128)(2,1)} fusion(bf16[512,1536]{1,0:T(8,128)(2,1)S(1)} %copy-done.11, bf16[512,4608]{1,0:T(8,128)(2,1)} %get-tuple-element.57.refs_7_), kind=kOutput, calls=%fused_computation | convolution fusion | flops 7254835200 | bytes 20447232 | tf_op jit(solution)/shard_map/dot_general | solution.py:1466
  506.3 0.6 reshape.88.refs_1_
  506.9 125.4 %shard_map.206 = (f32[512,1536]{1,0:T(8,128)}, f32[200,128]{1,0:T(8,128)}, bf16[192,4608]{1,0:T(8,128)(2,1)}, bf16[192,3072]{1,0:T(8,128)(2,1)}, bf16[192,5120]{...) custom-call(f32[1,1536]{1,0:T(1,128)} %get-tuple-element.54.refs_0_,, ...), custom_call_target="tpu_custom_call" | custom-call | tf_op jit(solution)/shard_map/pallas_call | solution.py:1237
  632.3 1.7 fusion.5
  634.0 0.1 copy-done.7
  634.2 0.1 fusion.6
  634.3 3.0 maximum_convert_fusion
  637.3 0.1 slice.72
  637.4 0.1 pad_maximum_fusion
  637.5 0.1 rev.7
  637.6 0.7 copy.34
  638.3 2.2 convert_element_type.31
  640.5 0.0 copy-done.6
  640.5 2.1 convert_element_type.34
  642.6 1.1 convert_element_type.32
  643.7 1.0 slice_bitcast_fusion.1
  644.7 0.1 reshape.97
  644.8 0.7 copy.36
  645.4 1.4 slice_bitcast_fusion.2
  646.8 2.7 copy.39
  649.5 1.7 copy.40
  (29 shorter events, 0.1 us)
Async XLA Ops:
  231.2 97.4 %copy-start.10 = (f32[1536]{0:T(1024)S(1)}, f32[1536]{0:T(1024)}, u32[]{:S(2)}) copy-start(f32[1536]{0:T(1024)} %param.19) | copy-start | bytes 18436
  326.3 2.8 copy-start
  329.1 3.0 copy-start.2
  329.1 3.3 copy-start.3
  332.4 1.4 copy-start.12
  332.4 5.7 slice-start
  333.2 4.9 copy-start.1
  333.8 4.3 slice-start.1
  343.3 150.4 %copy-start.11 = (bf16[512,1536]{1,0:T(8,128)(2,1)S(1)}, bf16[512,1536]{1,0:T(8,128)(2,1)}, u32[]{:S(2)}) copy-start(bf16[512,1536]{1,0:T(8,128)(2,1)} %get-tuple-element.59) | copy-start | bytes 4718596
  632.3 1.9 copy-start.7
  634.2 3.0 copy-start.9
  634.3 4.1 copy-start.5
  637.3 3.2 copy-start.6
  640.5 2.1 copy-start.8
  642.6 6.9 %copy-start.4 = (f32[512,1536]{1,0:T(8,128)S(1)}, f32[512,1536]{1,0:T(8,128)}, u32[]{:S(2)}) copy-start(f32[512,1536]{1,0:T(8,128)} %get-tuple-element.114) | copy-start | bytes 9437188

commit v4 on v3

--- a/solution.py
+++ b/solution.py
@@ -118,7 +118,7 @@
 
 
 def forward_kernel(
-    n, first_widths, rest_widths, docs_ref, mix_ref, taps_ref, gain_ref, input_ref, first_gain_ref, second_gain_ref, *refs
+    n, first_widths, rest_widths, docs_ref, mix_ref, taps_ref, gain_ref, input_ref, gains_ref, *refs
 ):
     refs = list(refs)
 
@@ -160,7 +160,7 @@
         band[...] = jnp.zeros_like(band)
         values = input_ref[...].astype(F32)
         scale = lax.rsqrt(jnp.mean(values * values, axis=1, keepdims=True) + EPSILON)
-        normed_ref[...] = (values * scale * first_gain_ref[...]).astype(BF16)
+        normed_ref[...] = (values * scale * gains_ref[0:1, :]).astype(BF16)
 
         def one(k, carry):
             first.step(k)
@@ -224,8 +224,8 @@
             values = vs[h]
             for r0, width, c0 in sets:
                 mixed = (
-                    mix_ref[group, 2 * r] * soft_ref[2 * p, r0 : r0 + LANE, :width].astype(F32)
-                    + mix_ref[group, 2 * r + 1] * soft_ref[2 * p + 1, r0 : r0 + LANE, :width].astype(F32)
+                    mix_ref[group, r, 0] * soft_ref[2 * p, r0 : r0 + LANE, :width].astype(F32)
+                    + mix_ref[group, r, 1] * soft_ref[2 * p + 1, r0 : r0 + LANE, :width].astype(F32)
                 ).astype(BF16)
                 outs[h, r0 : r0 + LANE] = nn(mixed, values[c0 : c0 + width])
         for k in in_turn(group, HEADS // 2, n - 1):
@@ -241,7 +241,7 @@
         wholes.append(attended)
         grouped.append(centred * lax.rsqrt(var + EPSILON))
     attended_ref[...] = jnp.concatenate(wholes, axis=1)
-    every[quad] = (jnp.concatenate(grouped, axis=1) * gain_ref[...]).astype(BF16)
+    every[quad] = (jnp.concatenate(grouped, axis=1) * gain_ref[1:2, :]).astype(BF16)
     grouped_ref[...] = every[quad]
 
     @pl.when(quad == quads - 1)
@@ -251,7 +251,7 @@
         middle = input_ref[...].astype(F32) + branch
         scale = lax.rsqrt(jnp.mean(middle * middle, axis=1, keepdims=True) + EPSILON)
         middle_ref[...] = middle
-        second_ref[...] = (middle * scale * second_gain_ref[...]).astype(BF16)
+        second_ref[...] = (middle * scale * gains_ref[2:3, :]).astype(BF16)
 
         def saved(t, carry):
             block_save(t).wait()
@@ -281,7 +281,7 @@
     anywhere = pl.BlockSpec(memory_space=pl.ANY)
     columns = pl.BlockSpec((seq, block), lambda i: (0, i))
     dma = pltpu.SemaphoreType.DMA
-    first_gain, group_gain, second_gain = [g.reshape(1, width) for g in gains]
+    gains = jnp.stack(gains)
     results = pl.pallas_call(
         functools.partial(forward_kernel, n, first_widths, rest_widths),
         grid=(quads,),
@@ -295,7 +295,7 @@
             jax.ShapeDtypeStruct((seq, 3 * width), BF16),
         ]
         + [jax.ShapeDtypeStruct((n * w.shape[0], w.shape[1]), w.dtype) for w in first + rest],
-        in_specs=[smem, smem, whole, pl.BlockSpec((1, block), lambda i: (0, i)), whole, whole, whole]
+        in_specs=[smem, smem, whole, pl.BlockSpec((3, block), lambda i: (0, i)), whole, whole]
         + [anywhere] * len(first + rest),
         out_specs=[
             columns, columns,
@@ -323,21 +323,24 @@
             collective_id=collective, has_side_effects=True, vmem_limit_bytes=60 * 1024 * 1024
         ),
     )(
-        docs, head_mixing.reshape(HEADS // 2, 4), pad_taps(conv_kernel), group_gain, layer_input, first_gain, second_gain,
+        docs, head_mixing, pad_taps(conv_kernel), gains, layer_input, gains,
         *first, *rest,
     )
     return results[:7], results[7 : 7 + len(first)], results[7 + len(first) :]
 
 
 def backward_kernel(
-    n, specs, docs_ref, mix_ref, taps_ref, gain_ref, q_ref, k_ref, v_ref, attended_ref, d_grouped_ref, soft_ref, *refs
+    n, specs, done_specs, docs_ref, mix_ref, taps_ref, gain_ref, q_ref, k_ref, v_ref, attended_ref, d_grouped_ref, soft_ref, *refs
 ):
-    count = len(specs)
-    grads, refs = refs[:count], refs[count:]
+    count, done = len(specs), len(done_specs)
+    grads, done_sums, refs = refs[:count], refs[count : count + done], refs[count + done :]
     d_projected, grad_gain_ref, grad_taps_ref, grad_mix_ref = refs[:4]
     sums, others, refs = refs[4 : 4 + count], refs[4 + count : 4 + 2 * count], refs[4 + 2 * count :]
-    masks, band, qs, ks, vs, ds, shifted, d_heads, d_rows, d_cols, diagonal, leaving, leave_sem = refs[:13]
-    reduce = Reduce(Ring(n), grads, sums, others, specs, refs[13:])
+    done_totals, refs = refs[:done], refs[done:]
+    final_size = len(FinalSum.scratch(done_specs))
+    masks, band, qs, ks, vs, ds, shifted, d_heads, d_rows, d_cols, near_keys, leaving, leave_sem = refs[:13]
+    reduce = Reduce(Ring(n), grads, sums, others, specs, refs[13 + final_size :])
+    final = FinalSum(reduce.ring, done_sums, done_totals, done_specs, refs[13 : 13 + final_size])
     seq = q_ref.shape[0]
     quad = pl.program_id(0)
 
@@ -346,6 +349,8 @@
         reduce.clear()
         reduce.ring.meet()
         reduce.start()
+        for i in range(done):
+            final.start(i)
 
     @pl.when(quad == 0)
     def _():
@@ -385,7 +390,7 @@
 
     def pair(p, carry):
         group = quad * 2 + p
-        mix = [[mix_ref[group, 2 * r + s] for s in range(2)] for r in range(2)]
+        mix = [[mix_ref[group, r, s] for s in range(2)] for r in range(2)]
         upstream_t = [ds[2 * p + r].T for r in range(2)]
         grad_mix = [[jnp.zeros((1, 1), F32) for _ in range(2)] for _ in range(2)]
         for r in range(2):
@@ -423,31 +428,32 @@
                 shifted[a] = moved
             keys = ks[h]
             d_cols[0] = jnp.zeros_like(d_cols[0])
-            diagonal[...] = jnp.zeros_like(diagonal)
             d_query = []
+            below = jnp.zeros((8, LANE * CQ), F32)
+            above = jnp.zeros((8, LANE * CQ), F32)
+            mirrored = []
             for r0, width, c0 in sets:
                 rows = slice(r0, r0 + LANE)
                 left, parts = masked_scores(shifted, keys, masks, r0, width, c0)
                 d_conv = d_rows[r, rows, :width]
                 blocks = width // LANE
-                flipped = jnp.concatenate(
-                    [
-                        nt(flip, d_conv[:, b * LANE : (b + 1) * LANE]).astype(BF16)
-                        for b in range(blocks)
-                    ],
-                    axis=0,
-                )
-                taken = nn(flipped, by_window(parts, width))
-                for a in range(CQ):
-                    total = diagonal[a]
-                    for jb in range(blocks):
-                        for qb in range(blocks):
-                            if abs(jb - qb) > 1:
-                                continue
-                            at = (qb * CQ + a) * LANE
-                            one = taken[jb * LANE : (jb + 1) * LANE, at : at + LANE]
-                            total = total + jnp.where(keeps[qb - jb], one, 0.0)
-                    diagonal[a] = total
+                flipped = [
+                    nt(flip, d_conv[:, b * LANE : (b + 1) * LANE]).astype(BF16) for b in range(blocks)
+                ]
+                start = len(mirrored) * LANE
+                mirrored += flipped
+                for b in range(blocks):
+                    near_keys[start + b * LANE : start + (b + 1) * LANE, :] = jnp.concatenate(
+                        [parts[a][:, b * LANE : (b + 1) * LANE] for a in range(CQ)], axis=1
+                    )
+                if blocks > 1:
+                    end = start + blocks * LANE
+                    below = below + nn(
+                        jnp.concatenate([f[:8] for f in flipped[:-1]], axis=1), near_keys[start + LANE : end, :]
+                    )
+                    above = above + nn(
+                        jnp.concatenate([f[LANE - 8 :] for f in flipped[1:]], axis=1), near_keys[start : end - LANE, :]
+                    )
                 spread = nn(d_conv, band[:width, : width * CQ]).astype(BF16)
                 stacked = jnp.concatenate(
                     [
@@ -473,8 +479,19 @@
                 total = whole if total is None else total + whole
             d_heads[0, h] = total
             d_heads[1, h] = d_cols[0].T
+            band_sum = nn(jnp.concatenate(mirrored, axis=1), near_keys[: len(mirrored) * LANE, :])
             for a in range(CQ):
-                aligned = pltpu.roll(diagonal[a], 0, axis=1, stride=1, stride_axis=0)
+                at = slice(a * LANE, (a + 1) * LANE)
+                whole = jnp.where(keeps[0], band_sum[:, at], 0.0)
+                whole = jnp.concatenate(
+                    [
+                        whole[:8] + jnp.where(keeps[1][:8], below[:, at], 0.0),
+                        whole[8 : LANE - 8],
+                        whole[LANE - 8 :] + jnp.where(keeps[-1][LANE - 8 :], above[:, at], 0.0),
+                    ],
+                    axis=0,
+                )
+                aligned = pltpu.roll(whole, 0, axis=1, stride=1, stride_axis=0)
                 grad_taps_ref[h, a : a + 1, :] = jnp.sum(aligned, axis=0, keepdims=True)
             work = reduce.each()
             middle = len(work) // 2
@@ -499,19 +516,22 @@
     def _():
         for part in range(3):
             leave(part).wait()
+        for i in range(done):
+            final.add(i)
 
     @pl.when(quad == pl.num_programs(0) - 1)
     def _():
         reduce.finish()
-
-
-def attend_backward(projected, conv_kernel, head_mixing, docs, gain, attended, d_grouped, soft, grads, n, collective):
+        final.finish()
+
+
+def attend_backward(projected, conv_kernel, head_mixing, docs, gain, attended, d_grouped, soft, grads, done_sums, done_specs, n, collective):
     seq = projected.shape[0]
     width = projected.shape[1] // 3
     block = QUAD * HEAD_DIM
     quads = HEADS // QUAD
     count = len(grads)
-    specs = Reduce.specs_of(grads, n, True)
+    specs = Reduce.specs_of(grads, n, (LESS, THIRD, THIRD))
     anywhere = pl.BlockSpec(memory_space=pl.ANY)
     whole = pl.BlockSpec(memory_space=pltpu.VMEM)
     smem = pl.BlockSpec(memory_space=pltpu.SMEM)
@@ -520,7 +540,7 @@
         return pl.BlockSpec((seq, block), lambda i: (0, first * quads + i))
 
     results = pl.pallas_call(
-        functools.partial(backward_kernel, n, specs),
+        functools.partial(backward_kernel, n, specs, done_specs),
         grid=(quads,),
         out_shape=[
             jax.ShapeDtypeStruct((seq, 3 * width), BF16),
@@ -528,21 +548,22 @@
             jax.ShapeDtypeStruct((HEADS, 8, LANE), F32),
             jax.ShapeDtypeStruct((quads, 8, LANE), F32),
         ]
-        + Reduce.results(specs, n),
+        + Reduce.results(specs, n)
+        + [jax.ShapeDtypeStruct(spec[:2], BF16) for spec in done_specs],
         in_specs=[
             smem, smem, whole,
             pl.BlockSpec((1, block), lambda i: (0, i)),
             columns(0), columns(1), columns(2), columns(0), columns(0),
             pl.BlockSpec((QUAD, seq, 3 * LANE), lambda i: (i, 0, 0)),
         ]
-        + [anywhere] * count,
+        + [anywhere] * (count + len(done_specs)),
         out_specs=[
             anywhere,
             pl.BlockSpec((1, block), lambda i: (0, i)),
             pl.BlockSpec((QUAD, 8, LANE), lambda i: (i, 0, 0)),
             pl.BlockSpec((1, 8, LANE), lambda i: (i, 0, 0)),
         ]
-        + [anywhere] * (2 * count),
+        + [anywhere] * (2 * count + len(done_specs)),
         scratch_shapes=[
             pltpu.VMEM((CQ, seq, 3 * LANE), BF16),
             pltpu.VMEM((3 * LANE, 3 * LANE * CQ), BF16),
@@ -554,22 +575,23 @@
             pltpu.VMEM((3, QUAD, seq, HEAD_DIM), F32),
             pltpu.VMEM((2, seq, 3 * LANE), BF16),
             pltpu.VMEM((2, HEAD_DIM, seq), F32),
-            pltpu.VMEM((CQ, LANE, LANE), F32),
+            pltpu.VMEM((sum(w for _, w, _ in row_sets(seq)), LANE * CQ), BF16),
             pltpu.VMEM((3, seq, block), BF16),
             pltpu.SemaphoreType.DMA((3,)),
         ]
+        + FinalSum.scratch(done_specs)
         + Reduce.scratch(specs, n),
         compiler_params=pltpu.CompilerParams(
             collective_id=collective, has_side_effects=True, vmem_limit_bytes=62 * 1024 * 1024
         ),
     )(
-        docs, head_mixing.reshape(HEADS // 2, 4), pad_taps(conv_kernel[:, :, ::-1]), gain.reshape(1, width),
-        projected, projected, projected, attended, d_grouped, soft, *grads,
+        docs, head_mixing, pad_taps(conv_kernel[:, :, ::-1]), gain.reshape(1, width),
+        projected, projected, projected, attended, d_grouped, soft, *grads, *done_sums,
     )
     d_projected, grad_gain, grad_taps, grad_mix = results[:4]
     return (
-        d_projected, grad_gain, grad_taps.reshape(-1, LANE), grad_mix.reshape(-1, LANE),
-    ), list(results[4 : 4 + count]), specs
+        d_projected, grad_gain, grad_taps, grad_mix,
+    ), list(results[4 : 4 + count]), specs, results[4 + 2 * count :]
 
 
 MESH = pl.DeviceIdType.MESH
@@ -743,12 +765,15 @@
     return axis, -(-units // 3) * unit
 
 
-def carried(columns, shared):
+THIRD = (1, 3)
+LESS = (7, 18)
+
+
+def carried(columns, portion):
     half = columns // 2
-    units = half // LANE
-    if not shared or units < 3:
+    lanes = -(-(half // LANE) * portion[0] // portion[1]) * LANE
+    if 2 * lanes >= half:
         return half // 2, 0
-    lanes = -(-units // 3) * LANE
     return lanes, half - 2 * lanes
 
 
@@ -946,8 +971,8 @@
         lax.fori_loop(0, self.ring.n, settle, 0)
 
     @staticmethod
-    def specs_of(grads, n, shared):
-        return [(g.shape[0] // n, g.shape[1], shared) for g in grads]
+    def specs_of(grads, n, portions):
+        return [(g.shape[0] // n, g.shape[1], portion) for g, portion in zip(grads, portions)]
 
     @staticmethod
     def results(specs, n):
@@ -1020,13 +1045,12 @@
     def shares(self, i):
         return carried(*self.specs[i][1:])[1] > 0
 
-    def start(self):
-        for i in range(len(self.specs)):
-            for name in ("across", "load"):
+    def start(self, i):
+        for name in ("across", "load"):
+            self.copy(i, name).start()
+        if self.shares(i):
+            for name in ("done across", "load done", "done sibling"):
                 self.copy(i, name).start()
-            if self.shares(i):
-                for name in ("done across", "load done", "done sibling"):
-                    self.copy(i, name).start()
 
     def add(self, i):
         self.copy(i, "load").wait()
@@ -1071,15 +1095,19 @@
     def copy(self, src, dst, at, device):
         return send(src, dst, self.pair.at[0, at], self.pair.at[1, at], device)
 
-    def start(self):
-        ring = self.ring
-        copy = self.copy(self.given, self.twin, 0, ring.sibling)
-        copy.start()
-        copy.wait()
+    def to_core(self):
+        return self.copy(self.given, self.twin, 0, self.ring.sibling)
+
+    def to_plane(self):
+        return self.copy(self.mine, self.plane, 1, self.ring.across)
+
+    def add_core(self):
+        self.to_core().wait()
         self.mine[...] = self.given[...] + self.twin[...]
-        copy = self.copy(self.mine, self.plane, 1, ring.across)
-        copy.start()
-        copy.wait()
+        self.to_plane().start()
+
+    def add_plane(self):
+        self.to_plane().wait()
         self.slots[0] = self.mine[...] + self.plane[...]
 
     def ring_copy(self, j):
@@ -1119,16 +1147,35 @@
 SMALL_SCRATCH = 7
 
 
-NORM_ROUNDS = 3
-
-
-def pack(given, at, value):
-    if value.shape[0] == 1:
-        for r in range(value.shape[1] // LANE):
-            given[at + r : at + r + 1, :] = value[:, r * LANE : (r + 1) * LANE]
-        return at + value.shape[1] // LANE
-    given[at : at + value.shape[0], :] = value
-    return at + value.shape[0]
+def pack(given, at, row):
+    for r in range(row.shape[1] // LANE):
+        given[at + r : at + r + 1, :] = row[:, r * LANE : (r + 1) * LANE]
+    return at + row.shape[1] // LANE
+
+
+SPOTS = 8
+
+
+def pack_taps(given, at, taps_ref, mix_ref):
+    rows = taps_ref.shape[1]
+    for first in range(0, HEADS, SPOTS):
+        together = taps_ref[first]
+        for h in range(1, SPOTS):
+            together = together + pltpu.roll(taps_ref[first + h], h * (LANE // SPOTS), axis=1)
+        given[at : at + rows, :] = together
+        at += rows
+    together = mix_ref[0]
+    for quad in range(1, mix_ref.shape[0]):
+        together = together + pltpu.roll(mix_ref[quad], 2 * quad, axis=0)
+    given[at : at + rows, :] = together
+
+
+def unpack_taps(summed):
+    rows = 8
+    taps = jnp.roll(summed[: HEADS // SPOTS * rows], CK // 2 + 1, axis=1).reshape(-1, rows, SPOTS, LANE // SPOTS)
+    taps = taps.transpose(0, 2, 1, 3).reshape(HEADS, rows, LANE // SPOTS)[:, :CQ, :CK]
+    mixing = summed[HEADS // SPOTS * rows :][: HEADS // 2, :4]
+    return taps[:, :, ::-1] * SCALE, mixing.reshape(HEADS // 2, 2, 2)
 
 
 def last_kernel(n, specs, early_specs, chunk, small_count, *refs):
@@ -1152,7 +1199,6 @@
     early_sum = FinalSum(ring, early_sums, early_totals, early_specs, take(len(FinalSum.scratch(early_specs))))
     reduce = Reduce(ring, grads, sums, others, specs, refs)
     chunks = d_projected.shape[1] // chunk
-    turns = -(-chunks // NORM_ROUNDS)
 
     def arrive(t, slot):
         at = cols(t * chunk, chunk)
@@ -1165,11 +1211,8 @@
         copy.start()
     reduce.clear()
     ring.meet()
-    d_normed[...] = jnp.zeros_like(d_normed)
-    given[...] = jnp.zeros_like(given)
-    reduce.start()
-
-    def turn(t):
+
+    def turn(t, carry):
         slot = lax.rem(t, 2)
         for copy in arrive(t, slot):
             copy.wait()
@@ -1180,42 +1223,49 @@
                 copy.start()
 
         d_normed[...] += nt(in_left[slot], in_right[slot])
-
-    def first(j, carry):
-        reduce.item(j, reduce.each())
-        for k in range(turns):
-            t = j * turns + k
-            pl.when(t < chunks)(functools.partial(turn, t))
         return carry
 
-    lax.fori_loop(0, NORM_ROUNDS, first, 0)
+    reduce.hand_over()
+    d_normed[...] = jnp.zeros_like(d_normed)
+    given[...] = jnp.zeros_like(given)
+    lax.fori_loop(0, chunks // 3, turn, 0)
+    for step in reduce.opening()[1:]:
+        step()
+    reduce.item(jnp.int32(0), reduce.each())
+    lax.fori_loop(chunks // 3, chunks, turn, 0)
     values = input_ref[...].astype(F32)
     scale = lax.rsqrt(jnp.mean(values * values, axis=1, keepdims=True) + EPSILON)
     upstream = d_normed[...]
     grad_gain = jnp.sum(upstream * (values * scale), axis=0, keepdims=True)
-    at = pack(given, 0, grad_gain)
-    for ref in small_refs:
-        at = pack(given, at, ref[...])
+    at = 0
+    for row in [grad_gain] + [ref[...] for ref in small_refs[:2]]:
+        at = pack(given, at, row)
+    pack_taps(given, at, small_refs[2], small_refs[3])
+    small.to_core().start()
     scaled = upstream * gain_ref[...]
     inner = jnp.mean(scaled * values, axis=1, keepdims=True)
     grad_input_ref[...] = d_middle_ref[...] + scale * scaled - values * (scale * scale * scale * inner)
-    small.start()
-    early_sum.start()
-    rounds = n - NORM_ROUNDS
-    hops = -(-n // rounds)
+    reduce.item(jnp.int32(1), reduce.each())
+    small.add_core()
+    reduce.item(jnp.int32(2), reduce.each())
+    small.add_plane()
+    hops = -(-n // (n - 4))
 
     def rest(j, carry):
+        for hop in range(hops):
+            at = (j - 3) * hops + hop
+            pl.when(at < n)(functools.partial(small.item, at))
+        for i in range(early):
+            pl.when(j == 3 + i)(functools.partial(early_sum.start, i))
         reduce.item(j, reduce.each())
-        for hop in range(hops):
-            at = (j - NORM_ROUNDS) * hops + hop
-            pl.when(at < n)(functools.partial(small.item, at))
         for i in range(early):
             pl.when(j == n - early + i)(functools.partial(early_sum.add, i))
         return carry
 
-    lax.fori_loop(NORM_ROUNDS, n, rest, 0)
+    lax.fori_loop(3, n, rest, 0)
     reduce.finish()
-    last_sum.start()
+    for i in range(count):
+        last_sum.start(i)
     small.finish()
     for i in range(count):
         last_sum.add(i)
@@ -1229,8 +1279,8 @@
     count, early = len(grads), len(early_specs)
     seq, width = layer_input.shape
     chunk = 512
-    specs = Reduce.specs_of(grads, n, False)
-    sizes = [v.size // LANE for v in [first_gain] + smalls]
+    specs = Reduce.specs_of(grads, n, (LESS,))
+    sizes = [width // LANE] * 3 + [(HEADS // SPOTS + 1) * 8]
     rows = -(-sum(sizes) // 8) * 8
     anywhere = pl.BlockSpec(memory_space=pl.ANY)
     whole = pl.BlockSpec(memory_space=pltpu.VMEM)
@@ -1265,6 +1315,7 @@
 
 TILES = 8
 EARLY_TILES = 3
+LATE_TILES = 3
 
 
 def mlp_kernel(n, specs, tile, *refs):
@@ -1275,27 +1326,46 @@
         del refs[:size]
         return taken
 
-    second_ref, upstream_ref, middle, inner, down = take(5)
+    second_ref, upstream_ref, middle, inner, down, coming = take(6)
     out_ref, d_second_ref = take(2)
-    (early, late, grad_down), sums, others = take(3), take(1), take(1)
+    (early, late, grad_down), sums, others, (came,) = take(3), take(1), take(1), take(1)
     turned, out_sum, in_gate, in_up, in_down, to_gate, to_up, to_down = take(8)
     middle_sem, in_sem, to_sem = take(3)
-    reduce = Reduce(Ring(n), [early], sums, others, specs, refs)
+    ring = Ring(n)
+    gather = Gather(ring, [coming], [came], [share(coming.shape)], take(len(Gather.scratch(1, n))))
+    reduce = Reduce(ring, [early], sums, others, specs, refs)
     hidden_size = down.shape[0]
     tiles = hidden_size // tile
     begun = EARLY_TILES
     each = -(-n // (tiles - begun - 1))
     due = -(-each // 2)
 
-    def arrive(t, slot):
-        at = pl.multiple_of(t * tile, tile)
+    split = tiles - LATE_TILES
+
+    def arrive(t, slot, weight, first, count):
+        at = pl.multiple_of((t - first) * tile, tile)
         return (
-            pltpu.make_async_copy(inner.at[:, pl.ds(at, tile)], in_gate.at[slot], in_sem.at[slot, 0]),
+            pltpu.make_async_copy(weight.at[:, pl.ds(at, tile)], in_gate.at[slot], in_sem.at[slot, 0]),
             pltpu.make_async_copy(
-                inner.at[:, pl.ds(pl.multiple_of(hidden_size + at, tile), tile)], in_up.at[slot], in_sem.at[slot, 1]
+                weight.at[:, pl.ds(pl.multiple_of(count * tile + at, tile), tile)], in_up.at[slot], in_sem.at[slot, 1]
             ),
-            pltpu.make_async_copy(down.at[pl.ds(at, tile), :], in_down.at[slot], in_sem.at[slot, 2]),
+            pltpu.make_async_copy(
+                down.at[pl.ds(pl.multiple_of(t * tile, tile), tile), :], in_down.at[slot], in_sem.at[slot, 2]
+            ),
         )
+
+    def arrivals(t, act):
+        slot = lax.rem(t, 2)
+
+        @pl.when(t < split)
+        def _():
+            for copy in arrive(t, slot, inner, 0, split):
+                act(copy)
+
+        @pl.when((t >= split) & (t < tiles))
+        def _():
+            for copy in arrive(t, slot, came, split, LATE_TILES):
+                act(copy)
 
     def leave(grad, t, slot, first, count):
         at = pl.multiple_of((t - first) * tile, tile)
@@ -1317,15 +1387,22 @@
 
     first = pltpu.make_async_copy(middle, out_sum, middle_sem)
     first.start()
-    for copy in arrive(0, 0):
-        copy.start()
+    arrivals(jnp.int32(0), lambda copy: copy.start())
     reduce.clear()
-    reduce.ring.meet()
+    ring.meet()
+    gather.start()
     turned[...] = second_ref[...].T
     d_second_ref[...] = jnp.zeros_like(d_second_ref)
     first.wait()
 
     def serve(t, point):
+        turns = 2 * (split - 1) - 1
+        if point % 2:
+            turn = 2 * t + point // 2
+            for k in in_turn(turn, turns, n - 1):
+                pl.when((turn < turns) & (k < n - 1))(functools.partial(gather.step, k))
+            pl.when(turn == turns)(gather.finish)
+
         @pl.when(t == begun)
         def _():
             if point == 0:
@@ -1341,14 +1418,8 @@
 
     def one(t, carry):
         slot = lax.rem(t, 2)
-        for copy in arrive(t, slot):
-            copy.wait()
-
-        @pl.when(t < tiles - 1)
-        def _():
-            for copy in arrive(t + 1, 1 - slot):
-                copy.start()
-
+        arrivals(t, lambda copy: copy.wait())
+        arrivals(t + 1, lambda copy: copy.start())
         second, upstream = second_ref[...], upstream_ref[...]
         gate = nn(second, in_gate[slot])
         up = nn(second, in_up[slot])
@@ -1400,12 +1471,12 @@
     reduce.finish()
 
 
-def feed_forward(second, upstream, middle, inner, down, n, collective):
+def feed_forward(second, upstream, middle, inner, down, coming, n, collective):
     seq, width = second.shape
     hidden_size = down.shape[0]
     tile = hidden_size // TILES
     early = EARLY_TILES * tile
-    specs = [(width // n, 2 * early, True)]
+    specs = [(width // n, 2 * early, THIRD)]
     whole = pl.BlockSpec(memory_space=pltpu.VMEM)
     anywhere = pl.BlockSpec(memory_space=pl.ANY)
     dma = pltpu.SemaphoreType.DMA
@@ -1420,9 +1491,10 @@
             jax.ShapeDtypeStruct((width, 2 * (hidden_size - early)), BF16),
             jax.ShapeDtypeStruct((hidden_size, width), BF16),
         ]
-        + Reduce.results(specs, n),
-        in_specs=[whole, whole, anywhere, anywhere, anywhere],
-        out_specs=[whole, whole] + [anywhere] * 5,
+        + Reduce.results(specs, n)
+        + [jax.ShapeDtypeStruct((n * coming.shape[0], coming.shape[1]), BF16)],
+        in_specs=[whole, whole] + [anywhere] * 4,
+        out_specs=[whole, whole] + [anywhere] * 6,
         scratch_shapes=[
             pltpu.VMEM((width, seq), BF16),
             pltpu.VMEM((seq, width), F32),
@@ -1434,12 +1506,13 @@
             pltpu.VMEM((2, tile, width), BF16),
             dma, dma((2, 3)), dma((2, 3)),
         ]
+        + Gather.scratch(1, n)
         + Reduce.scratch(specs, n),
         compiler_params=pltpu.CompilerParams(
             collective_id=collective, has_side_effects=True, vmem_limit_bytes=62 * 1024 * 1024
         ),
-    )(second, upstream, middle, inner, down)
-    out, d_second, _, late, grad_down, sums, _ = results
+    )(second, upstream, middle, inner, down, coming)
+    out, d_second, _, late, grad_down, sums, _, _ = results
     return out, d_second, late, grad_down, [sums], specs
 
 
@@ -1483,37 +1556,42 @@
     cotangent,
 ):
     n = lax.axis_size("fsdp")
-    kept, (qkv_weight, out_weight), (inner_weight, down_weight) = attend_forward(
+    hidden_size = inner_weight.shape[1] // 2
+    cut = hidden_size // TILES * (TILES - LATE_TILES)
+    gates, ups = inner_weight[:, :hidden_size], inner_weight[:, hidden_size:]
+    inner_first = jnp.concatenate([gates[:, :cut], ups[:, :cut]], axis=1)
+    inner_last = jnp.concatenate([gates[:, cut:], ups[:, cut:]], axis=1)
+    kept, (qkv_weight, out_weight), (inner_first, down_weight) = attend_forward(
         layer_input, conv_kernel, head_mixing, doc_lengths, (first_gain, group_gain, second_gain),
-        [qkv_weight, out_weight], [inner_weight, down_weight], n, 0,
+        [qkv_weight, out_weight], [inner_first, down_weight], n, 0,
     )
     grouped, attended, soft, normed, middle, second, projected = kept
     second_pull = jax.vjp(rms_norm, middle, second_gain)[1]
     layer_output, d_second, late_inner, grad_down, early_sums, early_specs = feed_forward(
-        second, cotangent, middle, inner_weight, down_weight, n, 2
+        second, cotangent, middle, inner_first, down_weight, inner_last, n, 2
     )
     d_middle, grad_second = second_pull(d_second)
     d_middle = cotangent.astype(F32) + d_middle
     d_branch = d_middle.astype(jnp.bfloat16)
     grad_proj = weight_grad(grouped, d_branch)
     d_grouped = project_back(d_branch, out_weight)
-    (d_projected, grad_group, grad_kernel, grad_mixing), sums, specs = attend_backward(
+    (d_projected, grad_group, grad_kernel, grad_mixing), sums, specs, (early_inner,) = attend_backward(
         projected, conv_kernel, head_mixing, doc_lengths, group_gain, attended, d_grouped, soft,
-        [late_inner, grad_down, grad_proj], n, 3,
+        [late_inner, grad_down, grad_proj], early_sums, early_specs, n, 3,
     )
     grad_qkv = weight_grad(normed, d_projected)
     grad_input, shards, small = last_step(
         d_projected, qkv_weight, layer_input, first_gain, d_middle, [grad_qkv],
-        [grad_group, grad_second.reshape(1, -1), grad_kernel, grad_mixing], early_sums + sums, early_specs + specs, n, 4,
+        [grad_group, grad_second.reshape(1, -1), grad_kernel, grad_mixing], sums, specs, n, 4,
     )
     grad_first, grad_group, grad_second = [g.reshape(-1) for g in small[:3]]
-    grad_kernel = jnp.roll(small[3].reshape(HEADS, 8, LANE), CK // 2 + 1, axis=2)[:, :CQ, :CK][:, :, ::-1] * SCALE
-    grad_mixing = small[4].reshape(-1, 8, LANE)[:, :2, :4].reshape(HEADS // 2, 2, 2)
-    early_half, late_half = shards[1].shape[1] // 2, shards[2].shape[1] // 2
+    grad_kernel, grad_mixing = unpack_taps(small[3])
+    grad_qkv, late_inner, grad_down, grad_proj = shards
+    cut, late_cut = early_inner.shape[1] // 2, late_inner.shape[1] // 2
     grad_inner = jnp.concatenate(
-        [shards[1][:, :early_half], shards[2][:, :late_half], shards[1][:, early_half:], shards[2][:, late_half:]], axis=1
+        [early_inner[:, :cut], late_inner[:, :late_cut], early_inner[:, cut:], late_inner[:, late_cut:]], axis=1
     )
-    shards = [g.astype(F32) for g in (shards[0], shards[4], grad_inner, shards[3])]
+    shards = [g.astype(F32) for g in (grad_qkv, grad_proj, grad_inner, grad_down)]
     return (
         layer_output, grad_input, grad_first, shards[0], grad_kernel, grad_mixing, grad_group, shards[1], grad_second,
         shards[2], shards[3],

time: 660 us -> 637 us (0.965)
  Pallas kernels: 594 us -> 571 us
    pallas_call x1, Pallas kernels: 224 us -> 197 us  [attend_forward(): pl.pallas_call(functools.partial(forward_kernel, n, first_widths, rest_wi...]
    pallas_call x1, Pallas kernels: 125 us -> 110 us  [last_step(): pl.pallas_call(functools.partial(last_kernel, n, specs, early_specs, chun...]
    pallas_call x1, Pallas kernels: 95.1 us -> 108 us  [feed_forward(): pl.pallas_call(functools.partial(mlp_kernel, n, specs, tile), out_shape=[...]
    reshape x8 -> x1, local copies, waits for them, and re-layouts: 6.94 us -> 0.08 us  [unpack_taps(): jnp.roll(summed[:HEADS // SPOTS * rows], CK // 2 + 1, axis=1)]
    pallas_call x1, Pallas kernels: 150 us -> 157 us  [attend_backward(): pl.pallas_call(functools.partial(backward_kernel, n, specs, done_specs),...]
where the time goes in v4:
time: 637 us; the launch traced here: 628 us
  Pallas kernels  571 us (90%)
  matrix products  21.1 us (3%)
  other arithmetic  19.3 us (3%)
  local copies, waits for them, and re-layouts  15.4 us (2%)
    pallas_call x1, Pallas kernels, attend_forward(): pl.pallas_call(functools.partial(forward_kernel, n, first_widths, rest_wi...  197 us
    pallas_call x1, Pallas kernels, attend_backward(): pl.pallas_call(functools.partial(backward_kernel, n, specs, done_specs),...  157 us
    pallas_call x1, Pallas kernels, last_step(): pl.pallas_call(functools.partial(last_kernel, n, specs, early_specs, chun...  110 us
    pallas_call x1, Pallas kernels, feed_forward(): pl.pallas_call(functools.partial(mlp_kernel, n, specs, tile), out_shape=[...  108 us
    dot_general x2, matrix products, weight_grad(): lax.dot_general(operand, upstream, (((0,), (0,)), ((), ())), preferred_el...  16.8 us

profile of v4, /device:TPU:0, one launch (start us, length us, event | category | flops | bytes accessed | tf_op | source)
XLA Modules:
  0.0 628.2 jit_solution(16791445894736755401)
XLA Ops:
  0.6 0.9 copy.23
  1.6 0.1 pad_slice_fusion.3
  1.7 0.7 pad_maximum_fusion.2.taps_ref
  2.4 1.7 fusion.6
  4.1 1.5 pad_maximum_fusion.refs_2_
  5.6 0.0 copy-done.15
  5.6 0.0 copy-start.13
  5.6 0.0 copy-start.12
  5.6 0.6 pad_maximum_fusion.4.gain_ref.gains_ref
  6.3 0.7 copy.24.mix_ref
  7.0 196.7 %shard_map.203 = (bf16[512,1536]{1,0:T(8,128)(2,1)}, f32[512,1536]{1,0:T(8,128)}, bf16[16,512,384]{2,1,0:T(8,128)(2,1)}, bf16[512,1536]{1,0:T(8,128)(2,1)}, f32[...) custom-call(s32[1,4]{1,0:T(1,128)} %docs_ref.3, ...), custom_call_target="tpu_custom_call" | custom-call | tf_op jit(solution)/shard_map/pallas_call | solution.py:285
  203.7 0.0 copy-done.13
  203.7 0.0 copy-done.12
  203.7 1.3 fusion.5
  205.0 1.1 pad_maximum_fusion.1.refs_5_
  206.2 107.5 %shard_map.204 = (bf16[512,1536]{1,0:T(8,128)(2,1)}, f32[512,1536]{1,0:T(8,128)}, bf16[1536,3072]{1,0:T(8,128)(2,1)}, bf16[1536,5120]{1,0:T(8,128)(2,1)}, bf16[4...) custom-call(bf16[512,1536]{1,0:T(8,128)(2,1)} %get-tuple-element.41.r, ...), custom_call_target="tpu_custom_call" | custom-call | tf_op jit(solution)/shard_map/pallas_call | solution.py:1483
  313.7 2.3 multiply_reduce_fusion.2
  316.0 0.5 copy-done
  316.5 3.0 multiply_reduce_fusion
  319.5 0.3 copy-done.3
  319.8 0.8 fusion.refs_6_
  320.6 0.0 copy-start.1
  320.7 0.6 copy-done.18
  321.3 4.3 convolution_convert_fusion.1.refs_2_
  325.5 4.3 fusion.2.d_grouped_ref
  329.8 0.1 rev.6
  330.0 0.1 pad_slice_fusion.1
  330.0 0.7 pad_maximum_fusion.3.taps_ref
  330.8 157.1 %shard_map.205 = (bf16[512,4608]{1,0:T(8,128)(2,1)}, f32[1,1536]{1,0:T(1,128)}, f32[16,8,128]{2,1,0:T(8,128)}, f32[4,8,128]{2,1,0:T(8,128)}, bf16[192,2048]{1,0:...) custom-call(s32[1,4]{1,0:T(1,128)} %docs_ref.3, ...), custom_call_target="tpu_custom_call" | custom-call | tf_op jit(solution)/shard_map/pallas_call | solution.py:542
  487.9 12.5 %convolution_convert_fusion.refs_9_ = bf16[1536,4608]{1,0:T(8,128)(2,1)} fusion(bf16[512,1536]{1,0:T(8,128)(2,1)S(1)} %copy-done.17, bf16[512,4608]{1,0:T(8,128)(2,1)} %get-tuple-element.58.refs_7_), kind=kOutput, calls=%fused_computation | convolution fusion | flops 7254835200 | bytes 20447232 | tf_op jit(solution)/shard_map/dot_general | solution.py:1539
  500.4 0.6 reshape.65.refs_1_
  501.0 109.7 %shard_map.206 = (f32[512,1536]{1,0:T(8,128)}, f32[64,128]{1,0:T(8,128)}, bf16[192,4608]{1,0:T(8,128)(2,1)}, bf16[192,5120]{1,0:T(8,128)(2,1)}, bf16[512,1536]{1...) custom-call(f32[1,1536]{1,0:T(1,128)} %get-tuple-element.55.refs_0_, ...), custom_call_target="tpu_custom_call" | custom-call | tf_op jit(solution)/shard_map/pallas_call | solution.py:1287
  610.7 1.7 fusion.7
  612.5 0.1 copy-done.7
  612.6 0.1 fusion.8
  612.7 3.0 maximum_convert_fusion
  615.7 0.1 slice.84
  615.8 0.1 pad_maximum_fusion.5
  615.9 0.1 reshape.67
  616.0 0.1 rev.7
  616.1 0.7 copy.29
  616.8 2.2 convert_element_type.31
  619.0 2.1 convert_element_type.34
  621.1 1.1 convert_element_type.32
  622.2 0.6 slice_bitcast_fusion
  622.9 0.7 copy.28
  623.5 2.7 copy.32
  626.2 1.7 copy.33
  (46 shorter events, 0.2 us)
Async XLA Ops:
  2.4 3.2 copy-start.14
  2.4 3.2 copy-start.15
  2.4 3.2 copy-start.9
  2.4 3.9 copy-start.16
  5.6 198.1 %copy-start.13 = (f32[1,1536]{1,0:T(1,128)}, f32[1,1536]{1,0:T(1,128)S(1)}, u32[]{:S(2)}) copy-start(f32[1,1536]{1,0:T(1,128)S(1)} %stack.12.refs_5_) | copy-start | bytes 18436
  5.6 198.1 %copy-start.12 = (f32[1,1536]{1,0:T(1,128)}, f32[1,1536]{1,0:T(1,128)S(1)}, u32[]{:S(2)}) copy-start(f32[1,1536]{1,0:T(1,128)S(1)} %stack.13.gain_ref) | copy-start | bytes 18436
  313.7 2.8 copy-start
  316.5 3.0 copy-start.2
  316.5 3.3 copy-start.3
  319.8 1.4 copy-start.18
  319.8 5.7 slice-start
  320.6 4.9 copy-start.1
  321.2 4.3 slice-start.1
  330.8 157.1 %copy-start.17 = (bf16[512,1536]{1,0:T(8,128)(2,1)S(1)}, bf16[512,1536]{1,0:T(8,128)(2,1)}, u32[]{:S(2)}) copy-start(bf16[512,1536]{1,0:T(8,128)(2,1)} %get-tuple-element.60) | copy-start | bytes 4718596
  610.7 1.9 copy-start.7
  612.7 3.0 copy-start.10
  612.7 4.1 copy-start.5
  615.7 3.3 copy-start.6
  619.0 2.1 copy-start.8
  619.0 3.2 copy-start.11
  621.1 5.1 copy-start.4

commit v5 on v4

--- a/solution.py
+++ b/solution.py
@@ -87,9 +87,11 @@
 
 
 def fill_backward_band(taps_ref, head, band):
-    for a, r, c, part in fill_toeplitz(taps_ref, head, band, 3):
-        at = (c * CQ + a) * LANE
-        band[r * LANE : (r + 1) * LANE, at : at + LANE] = part
+    near, after, before = circulant_masks()
+    for a in range(CQ):
+        whole = circulant(taps_ref[head, a : a + 1, :])
+        for at, keep in enumerate((after, near, before)):
+            band[at * LANE : (at + 1) * LANE, a * LANE : (a + 1) * LANE] = jnp.where(keep, whole, 0.0).astype(BF16)
 
 
 def shifted_rows(query):
@@ -152,6 +154,10 @@
 
     out_copy = pltpu.make_async_copy(first_fulls[1], out_weight, out_in)
 
+    def serve(turn):
+        for k in in_turn(turn, 2 + HEADS // 2, n - 2):
+            pl.when(k < n - 2)(functools.partial(rest.step, k + 1))
+
     @pl.when(quad == 0)
     def _():
         ring.meet()
@@ -164,11 +170,13 @@
 
         def one(k, carry):
             first.step(k)
-            pl.when(k == n - 3)(rest.start)
+            pl.when(k == n // 2 - 2)(rest.start)
+            pl.when(k == n - 3)(lambda: rest.step(jnp.int32(0)))
             return carry
 
         lax.fori_loop(0, n - 1, one, 0)
         first.finish()
+        serve(jnp.int32(0))
         block_copy(0).start()
         out_copy.start()
 
@@ -180,6 +188,7 @@
             return carry
 
         lax.fori_loop(0, count, project_block, 0)
+        serve(jnp.int32(1))
 
     for h in range(QUAD):
         at = slice(h * HEAD_DIM, (h + 1) * HEAD_DIM)
@@ -228,8 +237,7 @@
                     + mix_ref[group, r, 1] * soft_ref[2 * p + 1, r0 : r0 + LANE, :width].astype(F32)
                 ).astype(BF16)
                 outs[h, r0 : r0 + LANE] = nn(mixed, values[c0 : c0 + width])
-        for k in in_turn(group, HEADS // 2, n - 1):
-            pl.when(k < n - 1)(functools.partial(rest.step, k))
+        serve(2 + group)
         return carry
 
     lax.fori_loop(0, 2, pair, 0)
@@ -355,7 +363,6 @@
     @pl.when(quad == 0)
     def _():
         fill_masks(docs_ref, masks, seq)
-        band[...] = jnp.zeros_like(band)
 
     gains = []
     for h in range(QUAD):
@@ -454,12 +461,20 @@
                     above = above + nn(
                         jnp.concatenate([f[LANE - 8 :] for f in flipped[1:]], axis=1), near_keys[start : end - LANE, :]
                     )
-                spread = nn(d_conv, band[:width, : width * CQ]).astype(BF16)
+                spread = []
+                for b in range(blocks):
+                    low, high = max(b - 1, 0), min(b + 1, blocks - 1)
+                    spread.append(
+                        nn(
+                            d_conv[:, low * LANE : (high + 1) * LANE],
+                            band[(low - b + 1) * LANE : (high - b + 2) * LANE, :],
+                        ).astype(BF16)
+                    )
                 stacked = jnp.concatenate(
                     [
                         jnp.concatenate(
                             [
-                                spread[:, (b * CQ + a) * LANE : (b * CQ + a + 1) * LANE]
+                                spread[b][:, a * LANE : (a + 1) * LANE]
                                 for b in range(blocks)
                             ],
                             axis=1,
@@ -531,7 +546,7 @@
     block = QUAD * HEAD_DIM
     quads = HEADS // QUAD
     count = len(grads)
-    specs = Reduce.specs_of(grads, n, (LESS, THIRD, THIRD))
+    specs = Reduce.specs_of(grads, n, (THIRD, THIRD))
     anywhere = pl.BlockSpec(memory_space=pl.ANY)
     whole = pl.BlockSpec(memory_space=pltpu.VMEM)
     smem = pl.BlockSpec(memory_space=pltpu.SMEM)
@@ -566,7 +581,7 @@
         + [anywhere] * (2 * count + len(done_specs)),
         scratch_shapes=[
             pltpu.VMEM((CQ, seq, 3 * LANE), BF16),
-            pltpu.VMEM((3 * LANE, 3 * LANE * CQ), BF16),
+            pltpu.VMEM((3 * LANE, LANE * CQ), BF16),
             pltpu.VMEM((QUAD, seq, HEAD_DIM), BF16),
             pltpu.VMEM((QUAD, seq, HEAD_DIM), BF16),
             pltpu.VMEM((QUAD, seq, HEAD_DIM), BF16),
@@ -1279,7 +1294,7 @@
     count, early = len(grads), len(early_specs)
     seq, width = layer_input.shape
     chunk = 512
-    specs = Reduce.specs_of(grads, n, (LESS,))
+    specs = Reduce.specs_of(grads, n, (LESS, THIRD))
     sizes = [width // LANE] * 3 + [(HEADS // SPOTS + 1) * 8]
     rows = -(-sum(sizes) // 8) * 8
     anywhere = pl.BlockSpec(memory_space=pl.ANY)
@@ -1573,20 +1588,20 @@
     d_middle, grad_second = second_pull(d_second)
     d_middle = cotangent.astype(F32) + d_middle
     d_branch = d_middle.astype(jnp.bfloat16)
-    grad_proj = weight_grad(grouped, d_branch)
     d_grouped = project_back(d_branch, out_weight)
     (d_projected, grad_group, grad_kernel, grad_mixing), sums, specs, (early_inner,) = attend_backward(
         projected, conv_kernel, head_mixing, doc_lengths, group_gain, attended, d_grouped, soft,
-        [late_inner, grad_down, grad_proj], early_sums, early_specs, n, 3,
+        [late_inner, grad_down], early_sums, early_specs, n, 3,
     )
     grad_qkv = weight_grad(normed, d_projected)
+    grad_proj = weight_grad(grouped, d_branch)
     grad_input, shards, small = last_step(
-        d_projected, qkv_weight, layer_input, first_gain, d_middle, [grad_qkv],
+        d_projected, qkv_weight, layer_input, first_gain, d_middle, [grad_qkv, grad_proj],
         [grad_group, grad_second.reshape(1, -1), grad_kernel, grad_mixing], sums, specs, n, 4,
     )
     grad_first, grad_group, grad_second = [g.reshape(-1) for g in small[:3]]
     grad_kernel, grad_mixing = unpack_taps(small[3])
-    grad_qkv, late_inner, grad_down, grad_proj = shards
+    grad_qkv, grad_proj, late_inner, grad_down = shards
     cut, late_cut = early_inner.shape[1] // 2, late_inner.shape[1] // 2
     grad_inner = jnp.concatenate(
         [early_inner[:, :cut], late_inner[:, :late_cut], early_inner[:, cut:], late_inner[:, late_cut:]], axis=1

time: 637 us -> 630 us (0.989)
  Pallas kernels: 571 us -> 563 us
    pallas_call x1, Pallas kernels: 157 us -> 132 us  [attend_backward(): pl.pallas_call(functools.partial(backward_kernel, n, specs, done_specs),...]
    pallas_call x1, Pallas kernels: 110 us -> 121 us  [last_step(): pl.pallas_call(functools.partial(last_kernel, n, specs, early_specs, chun...]
where the time goes in v5:
time: 630 us; the launch traced here: 620 us
  Pallas kernels  563 us (89%)
  matrix products  21.1 us (3%)
  other arithmetic  19.3 us (3%)
  local copies, waits for them, and re-layouts  15.4 us (2%)
    pallas_call x1, Pallas kernels, attend_forward(): pl.pallas_call(functools.partial(forward_kernel, n, first_widths, rest_wi...  202 us
    pallas_call x1, Pallas kernels, attend_backward(): pl.pallas_call(functools.partial(backward_kernel, n, specs, done_specs),...  132 us
    pallas_call x1, Pallas kernels, last_step(): pl.pallas_call(functools.partial(last_kernel, n, specs, early_specs, chun...  121 us
    pallas_call x1, Pallas kernels, feed_forward(): pl.pallas_call(functools.partial(mlp_kernel, n, specs, tile), out_shape=[...  108 us
    dot_general x2, matrix products, weight_grad(): lax.dot_general(operand, upstream, (((0,), (0,)), ((), ())), preferred_el...  16.8 us

profile of v5, /device:TPU:0, one launch (start us, length us, event | category | flops | bytes accessed | tf_op | source)
XLA Modules:
  0.0 620.4 jit_solution(9776760136072907897)
XLA Ops:
  0.6 0.9 copy.23
  1.6 0.1 pad_slice_fusion.3
  1.7 0.7 pad_maximum_fusion.2.taps_ref
  2.4 1.7 fusion.6
  4.1 1.5 pad_maximum_fusion.refs_2_
  5.6 0.0 copy-done.14
  5.6 0.0 copy-done.15
  5.6 0.0 copy-start.12
  5.6 0.0 copy-done.9
  5.6 0.0 copy-start.13
  5.6 0.6 pad_maximum_fusion.4.gain_ref.gains_ref
  6.3 0.7 copy.24.mix_ref
  7.0 202.1 %shard_map.203 = (bf16[512,1536]{1,0:T(8,128)(2,1)}, f32[512,1536]{1,0:T(8,128)}, bf16[16,512,384]{2,1,0:T(8,128)(2,1)}, bf16[512,1536]{1,0:T(8,128)(2,1)}, f32[...) custom-call(s32[1,4]{1,0:T(1,128)} %docs_ref.3, ...), custom_call_target="tpu_custom_call" | custom-call | tf_op jit(solution)/shard_map/pallas_call | solution.py:293
  209.1 1.3 fusion.5
  210.4 1.1 pad_maximum_fusion.1.refs_5_
  211.5 108.4 %shard_map.204 = (bf16[512,1536]{1,0:T(8,128)(2,1)}, f32[512,1536]{1,0:T(8,128)}, bf16[1536,3072]{1,0:T(8,128)(2,1)}, bf16[1536,5120]{1,0:T(8,128)(2,1)}, bf16[4...) custom-call(bf16[512,1536]{1,0:T(8,128)(2,1)} %get-tuple-element.40.r, ...), custom_call_target="tpu_custom_call" | custom-call | tf_op jit(solution)/shard_map/pallas_call | solution.py:1498
  320.0 2.3 multiply_reduce_fusion.2
  322.3 0.5 copy-done
  322.8 3.0 multiply_reduce_fusion
  325.8 0.3 copy-done.3
  326.1 0.8 fusion.refs_6_
  326.9 0.0 copy-start.2
  326.9 0.6 copy-done.18
  327.5 4.3 convolution_convert_fusion.1.refs_10_
  331.8 4.3 fusion.2.d_grouped_ref
  336.1 0.1 rev.6
  336.2 0.1 pad_slice_fusion.1
  336.3 0.7 pad_maximum_fusion.3.taps_ref
  337.0 131.6 %shard_map.205 = (bf16[512,4608]{1,0:T(8,128)(2,1)}, f32[1,1536]{1,0:T(1,128)}, f32[16,8,128]{2,1,0:T(8,128)}, f32[4,8,128]{2,1,0:T(8,128)}, bf16[192,1792]{1,0:...) custom-call(s32[1,4]{1,0:T(1,128)} %docs_ref.3, ...), custom_call_target="tpu_custom_call" | custom-call | tf_op jit(solution)/shard_map/pallas_call | solution.py:557
  468.6 12.5 %convolution_convert_fusion.refs_9_ = bf16[1536,4608]{1,0:T(8,128)(2,1)} fusion(bf16[512,1536]{1,0:T(8,128)(2,1)S(1)} %copy-done.17, bf16[512,4608]{1,0:T(8,128)(2,1)} %get-tuple-element.56.refs_7_), kind=kOutput, calls=%fused_computation | convolution fusion | flops 7254835200 | bytes 20447232 | tf_op jit(solution)/shard_map/dot_general | solution.py:1554
  481.2 0.6 reshape.65.refs_1_
  481.8 121.2 %shard_map.206 = (f32[512,1536]{1,0:T(8,128)}, f32[64,128]{1,0:T(8,128)}, bf16[192,4608]{1,0:T(8,128)(2,1)}, bf16[192,1536]{1,0:T(8,128)(2,1)}, bf16[192,5120]{1...) custom-call(f32[1,1536]{1,0:T(1,128)} %get-tuple-element.53.refs_0_,, ...), custom_call_target="tpu_custom_call" | custom-call | tf_op jit(solution)/shard_map/pallas_call | solution.py:1302
  602.9 1.7 fusion.7
  604.7 0.1 copy-done.7
  604.8 0.1 fusion.8
  604.9 3.0 maximum_convert_fusion
  607.9 0.1 slice.84
  608.0 0.1 pad_maximum_fusion.5
  608.0 0.1 reshape.67
  608.2 0.1 rev.7
  608.3 0.7 copy.29
  609.0 2.2 convert_element_type.31
  611.2 2.1 convert_element_type.34
  613.3 1.1 convert_element_type.32
  614.4 0.6 slice_bitcast_fusion
  615.0 0.7 copy.28
  615.7 2.7 copy.32
  618.3 1.7 copy.33
  (46 shorter events, 0.2 us)
Async XLA Ops:
  2.4 3.2 copy-start.14
  2.4 3.2 copy-start.15
  2.4 3.2 copy-start.9
  2.4 3.9 copy-start.16
  5.6 203.5 %copy-start.12 = (f32[1,1536]{1,0:T(1,128)}, f32[1,1536]{1,0:T(1,128)S(1)}, u32[]{:S(2)}) copy-start(f32[1,1536]{1,0:T(1,128)S(1)} %stack.12.refs_5_) | copy-start | bytes 18436
  5.6 203.4 %copy-start.13 = (f32[1,1536]{1,0:T(1,128)}, f32[1,1536]{1,0:T(1,128)S(1)}, u32[]{:S(2)}) copy-start(f32[1,1536]{1,0:T(1,128)S(1)} %stack.13.gain_ref) | copy-start | bytes 18436
  320.0 2.8 copy-start
  322.8 3.0 copy-start.1
  322.8 3.3 copy-start.3
  326.1 1.4 copy-start.18
  326.1 5.7 slice-start
  326.9 4.9 copy-start.2
  327.5 4.3 slice-start.1
  337.0 131.6 %copy-start.17 = (bf16[512,1536]{1,0:T(8,128)(2,1)S(1)}, bf16[512,1536]{1,0:T(8,128)(2,1)}, u32[]{:S(2)}) copy-start(bf16[512,1536]{1,0:T(8,128)(2,1)} %get-tuple-element.58) | copy-start | bytes 4718596
  602.9 1.9 copy-start.7
  604.9 3.0 copy-start.10
  604.9 4.1 copy-start.5
  607.9 3.3 copy-start.6
  611.2 2.1 copy-start.8
  611.2 3.2 copy-start.11
  613.3 5.1 copy-start.4

commit v6 on v5

--- a/solution.py
+++ b/solution.py
@@ -14,6 +14,7 @@
 QUAD = 4
 LAG = 1
 LEAD = 3
+REST_AHEAD = 2
 SCALE = 1.0 / math.sqrt(HEAD_DIM)
 F32 = jnp.float32
 BF16 = jnp.bfloat16
@@ -155,8 +156,8 @@
     out_copy = pltpu.make_async_copy(first_fulls[1], out_weight, out_in)
 
     def serve(turn):
-        for k in in_turn(turn, 2 + HEADS // 2, n - 2):
-            pl.when(k < n - 2)(functools.partial(rest.step, k + 1))
+        for k in in_turn(turn, 2 + HEADS // 2, n - 1):
+            pl.when(k < n - 1)(functools.partial(rest.step, k))
 
     @pl.when(quad == 0)
     def _():
@@ -170,8 +171,7 @@
 
         def one(k, carry):
             first.step(k)
-            pl.when(k == n // 2 - 2)(rest.start)
-            pl.when(k == n - 3)(lambda: rest.step(jnp.int32(0)))
+            pl.when(k == n - REST_AHEAD)(rest.start)
             return carry
 
         lax.fori_loop(0, n - 1, one, 0)
@@ -356,9 +356,7 @@
     def _():
         reduce.clear()
         reduce.ring.meet()
-        reduce.start()
-        for i in range(done):
-            final.start(i)
+        reduce.hand_over()
 
     @pl.when(quad == 0)
     def _():
@@ -387,6 +385,16 @@
     grad_gain_ref[...] = jnp.concatenate(gains, axis=1)
     grad_taps_ref[...] = jnp.zeros_like(grad_taps_ref)
     grad_mix_ref[...] = jnp.zeros_like(grad_mix_ref)
+
+    @pl.when(quad == 0)
+    def _():
+        for step in reduce.opening()[1:]:
+            step()
+
+    @pl.when(quad == 1)
+    def _():
+        for i in range(done):
+            final.start(i)
 
     sets = row_sets(seq)
     up = lax.broadcasted_iota(jnp.int32, (LANE, LANE), 0)
@@ -782,6 +790,8 @@
 
 THIRD = (1, 3)
 LESS = (7, 18)
+HALF = (1, 2)
+LAST_PORTIONS = (LESS, THIRD)
 
 
 def carried(columns, portion):
@@ -1294,7 +1304,7 @@
     count, early = len(grads), len(early_specs)
     seq, width = layer_input.shape
     chunk = 512
-    specs = Reduce.specs_of(grads, n, (LESS, THIRD))
+    specs = Reduce.specs_of(grads, n, LAST_PORTIONS)
     sizes = [width // LANE] * 3 + [(HEADS // SPOTS + 1) * 8]
     rows = -(-sum(sizes) // 8) * 8
     anywhere = pl.BlockSpec(memory_space=pl.ANY)
@@ -1330,6 +1340,7 @@
 
 TILES = 8
 EARLY_TILES = 3
+POINTS = 4
 LATE_TILES = 3
 
 
@@ -1341,11 +1352,11 @@
         del refs[:size]
         return taken
 
-    second_ref, upstream_ref, middle, inner, down, coming = take(6)
-    out_ref, d_second_ref = take(2)
+    second_ref, upstream_ref, gain_ref, middle, out_weight, inner, down, coming = take(8)
+    out_ref, d_middle_ref, d_grouped_ref, grad_gain_ref = take(4)
     (early, late, grad_down), sums, others, (came,) = take(3), take(1), take(1), take(1)
-    turned, out_sum, in_gate, in_up, in_down, to_gate, to_up, to_down = take(8)
-    middle_sem, in_sem, to_sem = take(3)
+    turned, out_sum, d_second_ref, in_gate, in_up, in_down, to_gate, to_up, to_down = take(9)
+    middle_sem, in_sem, to_sem, out_sem = take(4)
     ring = Ring(n)
     gather = Gather(ring, [coming], [came], [share(coming.shape)], take(len(Gather.scratch(1, n))))
     reduce = Reduce(ring, [early], sums, others, specs, refs)
@@ -1411,12 +1422,16 @@
     first.wait()
 
     def serve(t, point):
-        turns = 2 * (split - 1) - 1
-        if point % 2:
-            turn = 2 * t + point // 2
-            for k in in_turn(turn, turns, n - 1):
-                pl.when((turn < turns) & (k < n - 1))(functools.partial(gather.step, k))
-            pl.when(turn == turns)(gather.finish)
+        ends = (split - 1) * POINTS + 1
+        turns = 7
+        for turn in range(turns):
+            at = 2 + turn * (ends - 3) // (turns - 1)
+            if at % POINTS == point:
+                for k in in_turn(turn, turns, n - 1):
+                    if k < n - 1:
+                        pl.when(t == at // POINTS)(functools.partial(gather.step, jnp.int32(k)))
+        if ends % POINTS == point:
+            pl.when(t == ends // POINTS)(gather.finish)
 
         @pl.when(t == begun)
         def _():
@@ -1434,7 +1449,6 @@
     def one(t, carry):
         slot = lax.rem(t, 2)
         arrivals(t, lambda copy: copy.wait())
-        arrivals(t + 1, lambda copy: copy.start())
         second, upstream = second_ref[...], upstream_ref[...]
         gate = nn(second, in_gate[slot])
         up = nn(second, in_up[slot])
@@ -1462,6 +1476,7 @@
         d_second_ref[...] += nt(d_gate, in_gate[slot])
         to_gate[slot] = nn(turned[...], d_gate).astype(BF16)
         serve(t, 2)
+        arrivals(t + 1, lambda copy: copy.start())
         d_second_ref[...] += nt(d_up, in_up[slot])
         to_up[slot] = nn(turned[...], d_up).astype(BF16)
         serve(t, 3)
@@ -1478,15 +1493,42 @@
 
         return carry
 
+    def out_piece(c):
+        into = (in_gate.at[0], in_up.at[0], in_gate.at[1])[c]
+        return pltpu.make_async_copy(out_weight.at[:, c * tile : (c + 1) * tile], into, out_sem.at[c])
+
     lax.fori_loop(0, tiles, one, 0)
+    pieces = out_weight.shape[1] // tile
+    for c in range(pieces):
+        out_piece(c).start()
     out_ref[...] = out_sum[...].astype(BF16)
+    first.start()
+    first.wait()
+    values = out_sum[...]
+    scale = lax.rsqrt(jnp.mean(values * values, axis=1, keepdims=True) + EPSILON)
+    d_second = d_second_ref[...]
+    grad_gain_ref[...] = jnp.sum(d_second * (values * scale), axis=0, keepdims=True)
+    scaled = d_second * gain_ref[...]
+    mean = jnp.mean(scaled * values, axis=1, keepdims=True)
+    d_middle_ref[...] = (
+        upstream_ref[...].astype(F32) + scale * scaled - values * (scale * scale * scale * mean)
+    )
+    for c in range(pieces):
+        out_piece(c).wait()
+        part = nt(
+            d_middle_ref[:, c * tile : (c + 1) * tile].astype(BF16), (in_gate.at[0], in_up.at[0], in_gate.at[1])[c][...]
+        )
+        if c == 0:
+            d_grouped_ref[...] = part
+        else:
+            d_grouped_ref[...] += part
     for t in (tiles - 2, tiles - 1):
         for copy in leave_late(t):
             copy.wait()
     reduce.finish()
 
 
-def feed_forward(second, upstream, middle, inner, down, coming, n, collective):
+def feed_forward(second, upstream, gain, middle, out_weight, inner, down, coming, n, collective):
     seq, width = second.shape
     hidden_size = down.shape[0]
     tile = hidden_size // TILES
@@ -1500,6 +1542,8 @@
         out_shape=[
             jax.ShapeDtypeStruct((seq, width), BF16),
             jax.ShapeDtypeStruct((seq, width), F32),
+            jax.ShapeDtypeStruct((seq, width), F32),
+            jax.ShapeDtypeStruct((1, width), F32),
         ]
         + [
             jax.ShapeDtypeStruct((width, 2 * early), BF16),
@@ -1508,10 +1552,11 @@
         ]
         + Reduce.results(specs, n)
         + [jax.ShapeDtypeStruct((n * coming.shape[0], coming.shape[1]), BF16)],
-        in_specs=[whole, whole] + [anywhere] * 4,
-        out_specs=[whole, whole] + [anywhere] * 6,
+        in_specs=[whole] * 3 + [anywhere] * 5,
+        out_specs=[whole] * 4 + [anywhere] * 6,
         scratch_shapes=[
             pltpu.VMEM((width, seq), BF16),
+            pltpu.VMEM((seq, width), F32),
             pltpu.VMEM((seq, width), F32),
             pltpu.VMEM((2, width, tile), BF16),
             pltpu.VMEM((2, width, tile), BF16),
@@ -1519,35 +1564,16 @@
             pltpu.VMEM((2, width, tile), BF16),
             pltpu.VMEM((2, width, tile), BF16),
             pltpu.VMEM((2, tile, width), BF16),
-            dma, dma((2, 3)), dma((2, 3)),
+            dma, dma((2, 3)), dma((2, 3)), dma((3,)),
         ]
         + Gather.scratch(1, n)
         + Reduce.scratch(specs, n),
         compiler_params=pltpu.CompilerParams(
             collective_id=collective, has_side_effects=True, vmem_limit_bytes=62 * 1024 * 1024
         ),
-    )(second, upstream, middle, inner, down, coming)
-    out, d_second, _, late, grad_down, sums, _, _ = results
-    return out, d_second, late, grad_down, [sums], specs
-
-
-def rms_norm(values, gains):
-    return values * lax.rsqrt(jnp.mean(values * values, axis=-1, keepdims=True) + EPSILON) * gains
-
-
-def swiglu(gate_up):
-    middle_col = gate_up.shape[1] // 2
-    return jax.nn.silu(gate_up[:, :middle_col]) * gate_up[:, middle_col:]
-
-
-def project(operand, weight):
-    return jnp.dot(operand, weight, preferred_element_type=F32)
-
-
-def project_back(upstream, weight):
-    return lax.dot_general(
-        upstream, weight, (((1,), (1,)), ((), ())), preferred_element_type=F32
-    )
+    )(second, upstream, gain.reshape(1, width), middle, out_weight, inner, down, coming)
+    out, d_middle, d_grouped, grad_gain, _, late, grad_down, sums, _, _ = results
+    return out, d_middle, d_grouped, grad_gain, late, grad_down, [sums], specs
 
 
 def weight_grad(operand, upstream):
@@ -1581,23 +1607,18 @@
         [qkv_weight, out_weight], [inner_first, down_weight], n, 0,
     )
     grouped, attended, soft, normed, middle, second, projected = kept
-    second_pull = jax.vjp(rms_norm, middle, second_gain)[1]
-    layer_output, d_second, late_inner, grad_down, early_sums, early_specs = feed_forward(
-        second, cotangent, middle, inner_first, down_weight, inner_last, n, 2
+    layer_output, d_middle, d_grouped, grad_second, late_inner, grad_down, early_sums, early_specs = feed_forward(
+        second, cotangent, second_gain, middle, out_weight, inner_first, down_weight, inner_last, n, 2
     )
-    d_middle, grad_second = second_pull(d_second)
-    d_middle = cotangent.astype(F32) + d_middle
-    d_branch = d_middle.astype(jnp.bfloat16)
-    d_grouped = project_back(d_branch, out_weight)
     (d_projected, grad_group, grad_kernel, grad_mixing), sums, specs, (early_inner,) = attend_backward(
         projected, conv_kernel, head_mixing, doc_lengths, group_gain, attended, d_grouped, soft,
         [late_inner, grad_down], early_sums, early_specs, n, 3,
     )
     grad_qkv = weight_grad(normed, d_projected)
-    grad_proj = weight_grad(grouped, d_branch)
+    grad_proj = weight_grad(grouped, d_middle.astype(BF16))
     grad_input, shards, small = last_step(
         d_projected, qkv_weight, layer_input, first_gain, d_middle, [grad_qkv, grad_proj],
-        [grad_group, grad_second.reshape(1, -1), grad_kernel, grad_mixing], sums, specs, n, 4,
+        [grad_group, grad_second, grad_kernel, grad_mixing], sums, specs, n, 4,
     )
     grad_first, grad_group, grad_second = [g.reshape(-1) for g in small[:3]]
     grad_kernel, grad_mixing = unpack_taps(small[3])

time: 630 us -> 619 us (0.983)
    pallas_call x1, Pallas kernels: 202 us -> 186 us  [attend_forward(): pl.pallas_call(functools.partial(forward_kernel, n, first_widths, rest_wi...]
    pallas_call x1, Pallas kernels: 108 us -> 121 us  [feed_forward(): pl.pallas_call(functools.partial(mlp_kernel, n, specs, tile), out_shape=[...]
where the time goes in v6:
time: 619 us; the launch traced here: 609 us
  Pallas kernels  558 us (90%)
  matrix products  18.8 us (3%)
  local copies, waits for them, and re-layouts  16.8 us (3%)
  other arithmetic  14.3 us (2%)
    pallas_call x1, Pallas kernels, attend_forward(): pl.pallas_call(functools.partial(forward_kernel, n, first_widths, rest_wi...  186 us
    pallas_call x1, Pallas kernels, attend_backward(): pl.pallas_call(functools.partial(backward_kernel, n, specs, done_specs),...  131 us
    pallas_call x1, Pallas kernels, last_step(): pl.pallas_call(functools.partial(last_kernel, n, specs, early_specs, chun...  121 us
    pallas_call x1, Pallas kernels, feed_forward(): pl.pallas_call(functools.partial(mlp_kernel, n, specs, tile), out_shape=[...  121 us
    dot_general x2, matrix products, weight_grad(): lax.dot_general(operand, upstream, (((0,), (0,)), ((), ())), preferred_el...  18.8 us

profile of v6, /device:TPU:0, one launch (start us, length us, event | category | flops | bytes accessed | tf_op | source)
XLA Modules:
  0.0 609.5 jit_solution(1122033507050047668)
XLA Ops:
  0.6 0.0 copy-start.1
  0.7 0.9 stack.12.refs_5_
  1.5 0.8 stack.13.gain_ref
  2.3 0.7 stack.14.refs_2_
  3.0 1.4 copy.24.mix_ref
  4.4 0.6 pad_maximum_fusion.4.gain_ref.gains_ref
  5.0 0.9 copy.23
  5.9 0.1 rev.6
  6.1 0.1 pad_slice_fusion.1
  6.1 0.7 pad_maximum_fusion.3.taps_ref
  6.9 0.1 pad_slice_fusion.3
  6.9 0.7 pad_maximum_fusion.2.taps_ref
  7.7 1.3 fusion.1
  9.0 1.1 pad_maximum_fusion.1.refs_7_
  10.1 0.0 copy-done.1
  10.1 0.1 fusion.2
  10.3 0.0 copy-done.6
  10.3 0.0 copy-done.7
  10.3 0.0 copy-done.8
  10.3 1.5 pad_maximum_fusion.refs_2_
  11.8 186.5 %shard_map.203 = (bf16[512,1536]{1,0:T(8,128)(2,1)}, f32[512,1536]{1,0:T(8,128)}, bf16[16,512,384]{2,1,0:T(8,128)(2,1)}, bf16[512,1536]{1,0:T(8,128)(2,1)}, f32[...) custom-call(s32[1,4]{1,0:T(1,128)} %docs_ref.3, ...), custom_call_target="tpu_custom_call" | custom-call | tf_op jit(solution)/shard_map/pallas_call | solution.py:293
  198.3 0.0 copy-start.10
  198.3 120.5 %shard_map.204 = (bf16[512,1536]{1,0:T(8,128)(2,1)}, f32[512,1536]{1,0:T(8,128)}, f32[512,1536]{1,0:T(8,128)}, f32[1,1536]{1,0:T(1,128)}, bf16[1536,3072]{1,0:T(...) custom-call(bf16[512,1536]{1,0:T(8,128)(2,1)} %get-tuple-element.42., ...), custom_call_target="tpu_custom_call" | custom-call | tf_op jit(solution)/shard_map/pallas_call | solution.py:1540
  318.8 0.0 copy-done.10
  318.8 6.2 %convolution_convert_fusion.1.refs_10_ = bf16[1536,1536]{1,0:T(8,128)(2,1)} fusion(bf16[512,1536]{1,0:T(8,128)(2,1)S(1)} %copy-done.10, f32[512,1536]{1,0:T(8,128)} %get-tuple-element.59.refs_6_), kind=kOutput, calls=%fused_computation.1 | convolution fusion | flops 2419064832 | bytes 9437184 | tf_op jit(solution)/shard_map/dot_general | solution.py:1580
  325.0 130.7 %shard_map.205 = (bf16[512,4608]{1,0:T(8,128)(2,1)}, f32[1,1536]{1,0:T(1,128)}, f32[16,8,128]{2,1,0:T(8,128)}, f32[4,8,128]{2,1,0:T(8,128)}, bf16[192,1792]{1,0:...) custom-call(s32[1,4]{1,0:T(1,128)} %docs_ref.3, ...), custom_call_target="tpu_custom_call" | custom-call | tf_op jit(solution)/shard_map/pallas_call | solution.py:565
  455.8 1.3 fusion.4
  457.1 0.0 copy-done.9
  457.1 12.6 %convolution_convert_fusion.refs_9_ = bf16[1536,4608]{1,0:T(8,128)(2,1)} fusion(bf16[512,1536]{1,0:T(8,128)(2,1)S(1)} %copy-done.9, bf16[512,4608]{1,0:T(8,128)(2,1)} %get-tuple-element.60.refs_7_), kind=kOutput, calls=%fused_computation | convolution fusion | flops 7254835200 | bytes 20447232 | tf_op jit(solution)/shard_map/dot_general | solution.py:1580
  469.6 120.7 %shard_map.206 = (f32[512,1536]{1,0:T(8,128)}, f32[64,128]{1,0:T(8,128)}, bf16[192,4608]{1,0:T(8,128)(2,1)}, bf16[192,1536]{1,0:T(8,128)(2,1)}, bf16[192,5120]{1...) custom-call(f32[1,1536]{1,0:T(1,128)} %get-tuple-element.55.refs_0_,, ...), custom_call_target="tpu_custom_call" | custom-call | tf_op jit(solution)/shard_map/pallas_call | solution.py:1312
  590.4 0.8 slice.87
  591.2 0.7 copy.28
  591.9 0.7 slice.85
  592.6 0.8 slice.84
  593.4 0.1 pad_maximum_fusion.5
  593.5 1.4 slice_bitcast_fusion
  594.8 0.1 reshape.44
  595.0 0.1 rev.7
  595.1 0.7 copy.29
  595.8 2.2 convert_element_type.28
  598.0 0.0 copy-done.2
  598.0 0.1 fusion.3
  598.2 3.0 maximum_convert_fusion
  601.2 2.1 convert_element_type.30
  603.2 2.2 convert_element_type.27
  605.4 1.1 copy.32
  606.6 0.9 copy-done
  607.4 1.7 copy.33
  (18 shorter events, 0.1 us)
Async XLA Ops:
  0.6 9.5 %copy-start.1 = (bf16[192,8192]{1,0:T(8,128)(2,1)S(1)}, bf16[192,8192]{1,0:T(8,128)(2,1)}, u32[]{:S(2)}) copy-start(bf16[192,8192]{1,0:T(8,128)(2,1)} %param.20) | copy-start | bytes 9437188
  1.5 8.8 %copy-start.6 = (f32[1,1536]{1,0:T(1,128)}, f32[1,1536]{1,0:T(1,128)S(1)}, u32[]{:S(2)}) copy-start(f32[1,1536]{1,0:T(1,128)S(1)} %stack.12.refs_5_) | copy-start | bytes 18436
  2.3 8.0 %copy-start.7 = (f32[1,1536]{1,0:T(1,128)}, f32[1,1536]{1,0:T(1,128)S(1)}, u32[]{:S(2)}) copy-start(f32[1,1536]{1,0:T(1,128)S(1)} %stack.13.gain_ref) | copy-start | bytes 18436
  3.0 7.3 %copy-start.8 = (f32[1,1536]{1,0:T(1,128)}, f32[1,1536]{1,0:T(1,128)S(1)}, u32[]{:S(2)}) copy-start(f32[1,1536]{1,0:T(1,128)S(1)} %stack.14.refs_2_) | copy-start | bytes 18436
  198.3 120.5 %copy-start.10 = (bf16[512,1536]{1,0:T(8,128)(2,1)S(1)}, bf16[512,1536]{1,0:T(8,128)(2,1)}, u32[]{:S(2)}) copy-start(bf16[512,1536]{1,0:T(8,128)(2,1)} %get-tuple-element.63) | copy-start | bytes 4718596
  325.0 132.0 %copy-start.9 = (bf16[512,1536]{1,0:T(8,128)(2,1)S(1)}, bf16[512,1536]{1,0:T(8,128)(2,1)}, u32[]{:S(2)}) copy-start(bf16[512,1536]{1,0:T(8,128)(2,1)} %get-tuple-element.62) | copy-start | bytes 4718596
  590.4 7.6 %copy-start.2 = (bf16[192,5120]{1,0:T(8,128)(2,1)S(1)}, bf16[192,5120]{1,0:T(8,128)(2,1)}, u32[]{:S(2)}) copy-start(bf16[192,5120]{1,0:T(8,128)(2,1)} %get-tuple-element.71) | copy-start | bytes 5898244
  598.1 3.0 copy-start.5
  601.2 2.1 copy-start.3
  603.2 2.2 copy-start.4
  603.2 4.2 copy-start

commit v7 on v6

--- a/solution.py
+++ b/solution.py
@@ -121,7 +121,7 @@
 
 
 def forward_kernel(
-    n, first_widths, rest_widths, docs_ref, mix_ref, taps_ref, gain_ref, input_ref, gains_ref, *refs
+    n, first_widths, cut, docs_ref, mix_ref, taps_ref, gain_ref, input_ref, gains_ref, *refs
 ):
     refs = list(refs)
 
@@ -130,14 +130,18 @@
         del refs[:size]
         return taken
 
-    first_count, rest_count = len(first_widths), len(rest_widths)
-    first_weights, rest_weights = take(first_count), take(rest_count)
+    first_count = len(first_widths)
+    first_weights, (inner, down) = take(first_count), take(2)
     grouped_ref, attended_ref, soft_ref, normed_ref, middle_ref, second_ref, projected = take(7)
-    first_fulls, rest_fulls = take(first_count), take(rest_count)
+    first_fulls, (inner_full, down_full) = take(first_count), take(2)
     masks, band, qs, ks, vs, shifted, outs = take(7)
     blocks, block_weight, every, out_weight, block_in, block_out, out_in = take(7)
     ring = Ring(n)
     sems = len(Gather.scratch(first_count, n))
+    hidden_size = inner.shape[1] // 2
+    rest_weights = [inner.at[:, :cut], inner.at[:, hidden_size : hidden_size + cut], down]
+    rest_fulls = [inner_full.at[:, :cut], inner_full.at[:, cut:], down_full]
+    rest_widths = [share((inner.shape[0], cut))] * 2 + [share(down.shape)]
     first = Gather(ring, first_weights, first_fulls, first_widths, take(sems))
     rest = Gather(ring, rest_weights, rest_fulls, rest_widths, take(sems))
     seq = input_ref.shape[0]
@@ -279,19 +283,19 @@
     return [turn * each + t for t in range(each)]
 
 
-def attend_forward(layer_input, conv_kernel, head_mixing, docs, gains, first, rest, n, collective):
+def attend_forward(layer_input, conv_kernel, head_mixing, docs, gains, first, inner, down, n, collective):
     seq, width = layer_input.shape
     block = QUAD * HEAD_DIM
     quads = HEADS // QUAD
-    first_widths, rest_widths = [share(w.shape) for w in first], [share(w.shape) for w in rest]
+    first_widths = [share(w.shape) for w in first]
+    cut = inner.shape[1] // 2 // TILES * (TILES - LATE_TILES)
     whole = pl.BlockSpec(memory_space=pltpu.VMEM)
     smem = pl.BlockSpec(memory_space=pltpu.SMEM)
     anywhere = pl.BlockSpec(memory_space=pl.ANY)
     columns = pl.BlockSpec((seq, block), lambda i: (0, i))
     dma = pltpu.SemaphoreType.DMA
-    gains = jnp.stack(gains)
     results = pl.pallas_call(
-        functools.partial(forward_kernel, n, first_widths, rest_widths),
+        functools.partial(forward_kernel, n, first_widths, cut),
         grid=(quads,),
         out_shape=[
             jax.ShapeDtypeStruct((seq, width), BF16),
@@ -302,15 +306,16 @@
             jax.ShapeDtypeStruct((seq, width), BF16),
             jax.ShapeDtypeStruct((seq, 3 * width), BF16),
         ]
-        + [jax.ShapeDtypeStruct((n * w.shape[0], w.shape[1]), w.dtype) for w in first + rest],
+        + [jax.ShapeDtypeStruct((n * w.shape[0], w.shape[1]), w.dtype) for w in first]
+        + [jax.ShapeDtypeStruct((width, 2 * cut), BF16), jax.ShapeDtypeStruct((n * down.shape[0], width), BF16)],
         in_specs=[smem, smem, whole, pl.BlockSpec((3, block), lambda i: (0, i)), whole, whole]
-        + [anywhere] * len(first + rest),
+        + [anywhere] * (2 + len(first)),
         out_specs=[
             columns, columns,
             pl.BlockSpec((QUAD, seq, 3 * LANE), lambda i: (i, 0, 0)),
             whole, whole, whole,
         ]
-        + [anywhere] * (1 + len(first + rest)),
+        + [anywhere] * (3 + len(first)),
         scratch_shapes=[
             pltpu.VMEM((CQ, seq, 3 * LANE), BF16),
             pltpu.VMEM((3 * LANE * CQ, 3 * LANE), BF16),
@@ -326,13 +331,13 @@
             dma((2,)), dma((3 * quads,)), dma,
         ]
         + Gather.scratch(len(first), n)
-        + Gather.scratch(len(rest), n),
+        + Gather.scratch(3, n),
         compiler_params=pltpu.CompilerParams(
             collective_id=collective, has_side_effects=True, vmem_limit_bytes=60 * 1024 * 1024
         ),
     )(
         docs, head_mixing, pad_taps(conv_kernel), gains, layer_input, gains,
-        *first, *rest,
+        *first, inner, down,
     )
     return results[:7], results[7 : 7 + len(first)], results[7 + len(first) :]
 
@@ -375,7 +380,7 @@
         scale = lax.rsqrt(var + EPSILON)
         unit = centred * scale
         gains.append(jnp.sum(d_grouped * unit, axis=0, keepdims=True))
-        w = d_grouped * gain_ref[:, at]
+        w = d_grouped * gain_ref[1:2, at]
         d_attended = scale * (
             w
             - jnp.mean(w, axis=1, keepdims=True)
@@ -548,7 +553,7 @@
         final.finish()
 
 
-def attend_backward(projected, conv_kernel, head_mixing, docs, gain, attended, d_grouped, soft, grads, done_sums, done_specs, n, collective):
+def attend_backward(projected, conv_kernel, head_mixing, docs, gains, attended, d_grouped, soft, grads, done_sums, done_specs, n, collective):
     seq = projected.shape[0]
     width = projected.shape[1] // 3
     block = QUAD * HEAD_DIM
@@ -575,7 +580,7 @@
         + [jax.ShapeDtypeStruct(spec[:2], BF16) for spec in done_specs],
         in_specs=[
             smem, smem, whole,
-            pl.BlockSpec((1, block), lambda i: (0, i)),
+            pl.BlockSpec((3, block), lambda i: (0, i)),
             columns(0), columns(1), columns(2), columns(0), columns(0),
             pl.BlockSpec((QUAD, seq, 3 * LANE), lambda i: (i, 0, 0)),
         ]
@@ -608,7 +613,7 @@
             collective_id=collective, has_side_effects=True, vmem_limit_bytes=62 * 1024 * 1024
         ),
     )(
-        docs, head_mixing, pad_taps(conv_kernel[:, :, ::-1]), gain.reshape(1, width),
+        docs, head_mixing, pad_taps(conv_kernel[:, :, ::-1]), gains,
         projected, projected, projected, attended, d_grouped, soft, *grads, *done_sums,
     )
     d_projected, grad_gain, grad_taps, grad_mix = results[:4]
@@ -911,29 +916,32 @@
                     rows = self.specs[i][0]
                     self.x_slots[i][:, :, cols(at, width)] = jnp.zeros((self.ring.n, rows, width), BF16)
 
-    def hand_over(self):
+    def all(self):
+        return range(len(self.grads))
+
+    def hand_over(self, which=None):
         for j in range(min(LEAD, self.ring.n)):
-            for i in range(len(self.grads)):
+            for i in which or self.all():
                 for kind in reversed(range(self.kinds(i))):
                     self.core_copy(i, kind, j).start()
 
     def hand_next(self, i, kind, j):
         pl.when(j + LEAD < self.ring.n)(lambda: self.core_copy(i, kind, j + LEAD).start())
 
-    def fetch_first(self):
-        for i in range(len(self.grads)):
+    def fetch_first(self, which=None):
+        for i in which or self.all():
             for kind in reversed(range(self.kinds(i))):
                 self.fetch(i, kind, 0)
 
-    def give_all(self, j):
-        for i in range(len(self.grads)):
+    def give_all(self, j, which=None):
+        for i in which or self.all():
             if self.kinds(i) == 3:
                 self.give(i, j)
 
-    def opening(self):
+    def opening(self, which=None):
         return [
-            self.hand_over, self.fetch_first,
-            functools.partial(self.give_all, 0), functools.partial(self.give_all, 1),
+            functools.partial(self.hand_over, which), functools.partial(self.fetch_first, which),
+            functools.partial(self.give_all, 0, which), functools.partial(self.give_all, 1, which),
         ]
 
     def start(self):
@@ -1214,15 +1222,15 @@
         return taken
 
     small_refs = take(small_count)
-    input_ref, gain_ref, d_middle_ref, d_projected, weight = take(5)
-    grads, early_sums = take(count), take(early)
-    grad_input_ref, total_ref = take(2)
+    input_ref, normed_ref, gain_ref, d_middle_ref, d_projected, weight = take(6)
+    grads, early_sums = take(count - 1), take(early)
+    grad_input_ref, total_ref, grad_qkv = take(3)
     totals, early_totals, sums, others = take(count), take(early), take(count), take(count)
-    given, d_normed, in_left, in_right, in_sem = take(5)
+    given, d_normed, in_left, in_right, turned, leaving, in_sem, leave_sem = take(8)
     small = SmallSum(ring, given, total_ref, take(SMALL_SCRATCH))
     last_sum = FinalSum(ring, sums, totals, specs, take(len(FinalSum.scratch(specs))))
     early_sum = FinalSum(ring, early_sums, early_totals, early_specs, take(len(FinalSum.scratch(early_specs))))
-    reduce = Reduce(ring, grads, sums, others, specs, refs)
+    reduce = Reduce(ring, [grad_qkv] + grads, sums, others, specs, refs)
     chunks = d_projected.shape[1] // chunk
 
     def arrive(t, slot):
@@ -1232,32 +1240,46 @@
             pltpu.make_async_copy(weight.at[:, at], in_right.at[slot], in_sem.at[slot, 1]),
         )
 
+    def leave(t):
+        slot = lax.rem(t, 2)
+        return pltpu.make_async_copy(leaving.at[slot], grad_qkv.at[:, cols(t * chunk, chunk)], leave_sem.at[slot])
+
+    def turn(t, carry):
+        slot = lax.rem(t, 2)
+        for copy in arrive(t, slot):
+            copy.wait()
+
+        @pl.when(t < chunks - 1)
+        def _():
+            for copy in arrive(t + 1, 1 - slot):
+                copy.start()
+
+        pl.when(t >= 2)(lambda: leave(t - 2).wait())
+        leaving[slot] = nn(turned[...], in_left[slot]).astype(BF16)
+        leave(t).start()
+        d_normed[...] += nt(in_left[slot], in_right[slot])
+        return carry
+
+    ahead = 3
+    qkv, others_at = [0], list(range(1, count))
+    behind = [(i, d) for i, d in reduce.each() if i > 0]
+
     for copy in arrive(0, 0):
         copy.start()
     reduce.clear()
     ring.meet()
-
-    def turn(t, carry):
-        slot = lax.rem(t, 2)
-        for copy in arrive(t, slot):
-            copy.wait()
-
-        @pl.when(t < chunks - 1)
-        def _():
-            for copy in arrive(t + 1, 1 - slot):
-                copy.start()
-
-        d_normed[...] += nt(in_left[slot], in_right[slot])
-        return carry
-
-    reduce.hand_over()
+    reduce.hand_over(others_at)
     d_normed[...] = jnp.zeros_like(d_normed)
     given[...] = jnp.zeros_like(given)
-    lax.fori_loop(0, chunks // 3, turn, 0)
-    for step in reduce.opening()[1:]:
+    turned[...] = normed_ref[...].T
+    for step in reduce.opening(others_at)[1:]:
         step()
-    reduce.item(jnp.int32(0), reduce.each())
-    lax.fori_loop(chunks // 3, chunks, turn, 0)
+    for j in range(ahead):
+        lax.fori_loop(j * chunks // ahead, (j + 1) * chunks // ahead, turn, 0)
+        reduce.item(jnp.int32(j), behind)
+    for t in (chunks - 2, chunks - 1):
+        leave(jnp.int32(t)).wait()
+    reduce.hand_over(qkv)
     values = input_ref[...].astype(F32)
     scale = lax.rsqrt(jnp.mean(values * values, axis=1, keepdims=True) + EPSILON)
     upstream = d_normed[...]
@@ -1267,27 +1289,34 @@
         at = pack(given, at, row)
     pack_taps(given, at, small_refs[2], small_refs[3])
     small.to_core().start()
-    scaled = upstream * gain_ref[...]
+    for step in reduce.opening(qkv)[1:]:
+        step()
+
+    def items(j):
+        reduce.item(j, [(0, 1), (0, 0)])
+        pl.when(j + ahead < n)(lambda: reduce.item(j + ahead, behind))
+
+    items(jnp.int32(0))
+    scaled = upstream * gain_ref[0:1, :]
     inner = jnp.mean(scaled * values, axis=1, keepdims=True)
     grad_input_ref[...] = d_middle_ref[...] + scale * scaled - values * (scale * scale * scale * inner)
-    reduce.item(jnp.int32(1), reduce.each())
     small.add_core()
-    reduce.item(jnp.int32(2), reduce.each())
+    items(jnp.int32(1))
     small.add_plane()
-    hops = -(-n // (n - 4))
+    hops = -(-n // (n - 3))
 
     def rest(j, carry):
         for hop in range(hops):
-            at = (j - 3) * hops + hop
+            at = (j - 2) * hops + hop
             pl.when(at < n)(functools.partial(small.item, at))
         for i in range(early):
-            pl.when(j == 3 + i)(functools.partial(early_sum.start, i))
-        reduce.item(j, reduce.each())
+            pl.when(j == 2 + i)(functools.partial(early_sum.start, i))
+        items(j)
         for i in range(early):
             pl.when(j == n - early + i)(functools.partial(early_sum.add, i))
         return carry
 
-    lax.fori_loop(3, n, rest, 0)
+    lax.fori_loop(2, n, rest, 0)
     reduce.finish()
     for i in range(count):
         last_sum.start(i)
@@ -1299,29 +1328,33 @@
 
 
 def last_step(
-    d_projected, qkv_weight, layer_input, first_gain, d_middle, grads, smalls, early_sums, early_specs, n, collective
+    d_projected, qkv_weight, layer_input, normed, gains, d_middle, grads, smalls, early_sums, early_specs, n, collective
 ):
-    count, early = len(grads), len(early_specs)
+    count, early = 1 + len(grads), len(early_specs)
     seq, width = layer_input.shape
     chunk = 512
-    specs = Reduce.specs_of(grads, n, LAST_PORTIONS)
+    grad_qkv = jax.ShapeDtypeStruct((width, d_projected.shape[1]), BF16)
+    specs = Reduce.specs_of([grad_qkv] + grads, n, LAST_PORTIONS)
     sizes = [width // LANE] * 3 + [(HEADS // SPOTS + 1) * 8]
     rows = -(-sum(sizes) // 8) * 8
     anywhere = pl.BlockSpec(memory_space=pl.ANY)
     whole = pl.BlockSpec(memory_space=pltpu.VMEM)
     results = pl.pallas_call(
         functools.partial(last_kernel, n, specs, early_specs, chunk, len(smalls)),
-        out_shape=[jax.ShapeDtypeStruct((seq, width), F32), jax.ShapeDtypeStruct((rows, LANE), F32)]
+        out_shape=[jax.ShapeDtypeStruct((seq, width), F32), jax.ShapeDtypeStruct((rows, LANE), F32), grad_qkv]
         + [jax.ShapeDtypeStruct(spec[:2], BF16) for spec in specs + early_specs]
         + Reduce.results(specs, n),
-        in_specs=[whole] * (len(smalls) + 3) + [anywhere] * (2 + count + early),
-        out_specs=[whole] * 2 + [anywhere] * (3 * count + early),
+        in_specs=[whole] * (len(smalls) + 4) + [anywhere] * (1 + count + early),
+        out_specs=[whole] * 2 + [anywhere] * (1 + 3 * count + early),
         scratch_shapes=[
             pltpu.VMEM((rows, LANE), F32),
             pltpu.VMEM((seq, width), F32),
             pltpu.VMEM((2, seq, chunk), BF16),
             pltpu.VMEM((2, width, chunk), BF16),
+            pltpu.VMEM((width, seq), BF16),
+            pltpu.VMEM((2, width, chunk), BF16),
             pltpu.SemaphoreType.DMA((2, 2)),
+            pltpu.SemaphoreType.DMA((2,)),
         ]
         + SmallSum.scratch(rows, n)
         + FinalSum.scratch(specs)
@@ -1330,12 +1363,12 @@
         compiler_params=pltpu.CompilerParams(
             collective_id=collective, has_side_effects=True, vmem_limit_bytes=60 * 1024 * 1024
         ),
-    )(*smalls, layer_input, first_gain.reshape(1, width), d_middle, d_projected, qkv_weight, *grads, *early_sums)
+    )(*smalls, layer_input, normed, gains, d_middle, d_projected, qkv_weight, *grads, *early_sums)
     out, at = [], 0
     for size in sizes:
         out.append(results[1][at : at + size])
         at += size
-    return results[0], results[2 : 2 + count + early], out
+    return results[0], results[3 : 3 + count + early], out
 
 
 TILES = 8
@@ -1358,9 +1391,15 @@
     turned, out_sum, d_second_ref, in_gate, in_up, in_down, to_gate, to_up, to_down = take(9)
     middle_sem, in_sem, to_sem, out_sem = take(4)
     ring = Ring(n)
-    gather = Gather(ring, [coming], [came], [share(coming.shape)], take(len(Gather.scratch(1, n))))
+    hidden_size = down.shape[0]
+    cut = hidden_size - LATE_TILES * tile
+    size = hidden_size - cut
+    pieces = [coming.at[:, cut:hidden_size], coming.at[:, hidden_size + cut :]]
+    gather = Gather(
+        ring, pieces, [came.at[:, :size], came.at[:, size:]], [share((coming.shape[0], size))] * 2,
+        take(len(Gather.scratch(2, n))),
+    )
     reduce = Reduce(ring, [early], sums, others, specs, refs)
-    hidden_size = down.shape[0]
     tiles = hidden_size // tile
     begun = EARLY_TILES
     each = -(-n // (tiles - begun - 1))
@@ -1411,8 +1450,10 @@
     def leave_late(t):
         return leave(late, t, lax.rem(t, 2), begun, tiles - begun)
 
-    first = pltpu.make_async_copy(middle, out_sum, middle_sem)
+    first = pltpu.make_async_copy(middle, out_sum, middle_sem.at[0])
+    again = pltpu.make_async_copy(middle, d_middle_ref, middle_sem.at[1])
     first.start()
+    again.start()
     arrivals(jnp.int32(0), lambda copy: copy.start())
     reduce.clear()
     ring.meet()
@@ -1502,13 +1543,12 @@
     for c in range(pieces):
         out_piece(c).start()
     out_ref[...] = out_sum[...].astype(BF16)
-    first.start()
-    first.wait()
-    values = out_sum[...]
+    again.wait()
+    values = d_middle_ref[...]
     scale = lax.rsqrt(jnp.mean(values * values, axis=1, keepdims=True) + EPSILON)
     d_second = d_second_ref[...]
     grad_gain_ref[...] = jnp.sum(d_second * (values * scale), axis=0, keepdims=True)
-    scaled = d_second * gain_ref[...]
+    scaled = d_second * gain_ref[2:3, :]
     mean = jnp.mean(scaled * values, axis=1, keepdims=True)
     d_middle_ref[...] = (
         upstream_ref[...].astype(F32) + scale * scaled - values * (scale * scale * scale * mean)
@@ -1528,7 +1568,7 @@
     reduce.finish()
 
 
-def feed_forward(second, upstream, gain, middle, out_weight, inner, down, coming, n, collective):
+def feed_forward(second, upstream, gains, middle, out_weight, inner, down, coming, n, collective):
     seq, width = second.shape
     hidden_size = down.shape[0]
     tile = hidden_size // TILES
@@ -1551,7 +1591,7 @@
             jax.ShapeDtypeStruct((hidden_size, width), BF16),
         ]
         + Reduce.results(specs, n)
-        + [jax.ShapeDtypeStruct((n * coming.shape[0], coming.shape[1]), BF16)],
+        + [jax.ShapeDtypeStruct((width, 2 * LATE_TILES * tile), BF16)],
         in_specs=[whole] * 3 + [anywhere] * 5,
         out_specs=[whole] * 4 + [anywhere] * 6,
         scratch_shapes=[
@@ -1564,14 +1604,14 @@
             pltpu.VMEM((2, width, tile), BF16),
             pltpu.VMEM((2, width, tile), BF16),
             pltpu.VMEM((2, tile, width), BF16),
-            dma, dma((2, 3)), dma((2, 3)), dma((3,)),
+            dma((2,)), dma((2, 3)), dma((2, 3)), dma((3,)),
         ]
-        + Gather.scratch(1, n)
+        + Gather.scratch(2, n)
         + Reduce.scratch(specs, n),
         compiler_params=pltpu.CompilerParams(
             collective_id=collective, has_side_effects=True, vmem_limit_bytes=62 * 1024 * 1024
         ),
-    )(second, upstream, gain.reshape(1, width), middle, out_weight, inner, down, coming)
+    )(second, upstream, gains, middle, out_weight, inner, down, coming)
     out, d_middle, d_grouped, grad_gain, _, late, grad_down, sums, _, _ = results
     return out, d_middle, d_grouped, grad_gain, late, grad_down, [sums], specs
 
@@ -1597,27 +1637,21 @@
     cotangent,
 ):
     n = lax.axis_size("fsdp")
-    hidden_size = inner_weight.shape[1] // 2
-    cut = hidden_size // TILES * (TILES - LATE_TILES)
-    gates, ups = inner_weight[:, :hidden_size], inner_weight[:, hidden_size:]
-    inner_first = jnp.concatenate([gates[:, :cut], ups[:, :cut]], axis=1)
-    inner_last = jnp.concatenate([gates[:, cut:], ups[:, cut:]], axis=1)
-    kept, (qkv_weight, out_weight), (inner_first, down_weight) = attend_forward(
-        layer_input, conv_kernel, head_mixing, doc_lengths, (first_gain, group_gain, second_gain),
-        [qkv_weight, out_weight], [inner_first, down_weight], n, 0,
+    gains = jnp.stack([first_gain, group_gain, second_gain])
+    kept, (qkv_weight, out_weight), (inner_first, down_full) = attend_forward(
+        layer_input, conv_kernel, head_mixing, doc_lengths, gains, [qkv_weight, out_weight], inner_weight, down_weight, n, 0,
     )
     grouped, attended, soft, normed, middle, second, projected = kept
     layer_output, d_middle, d_grouped, grad_second, late_inner, grad_down, early_sums, early_specs = feed_forward(
-        second, cotangent, second_gain, middle, out_weight, inner_first, down_weight, inner_last, n, 2
+        second, cotangent, gains, middle, out_weight, inner_first, down_full, inner_weight, n, 2
     )
     (d_projected, grad_group, grad_kernel, grad_mixing), sums, specs, (early_inner,) = attend_backward(
-        projected, conv_kernel, head_mixing, doc_lengths, group_gain, attended, d_grouped, soft,
+        projected, conv_kernel, head_mixing, doc_lengths, gains, attended, d_grouped, soft,
         [late_inner, grad_down], early_sums, early_specs, n, 3,
     )
-    grad_qkv = weight_grad(normed, d_projected)
     grad_proj = weight_grad(grouped, d_middle.astype(BF16))
     grad_input, shards, small = last_step(
-        d_projected, qkv_weight, layer_input, first_gain, d_middle, [grad_qkv, grad_proj],
+        d_projected, qkv_weight, layer_input, normed, gains, d_middle, [grad_proj],
         [grad_group, grad_second, grad_kernel, grad_mixing], sums, specs, n, 4,
     )
     grad_first, grad_group, grad_second = [g.reshape(-1) for g in small[:3]]

time: 619 us -> 613 us (level)
  matrix products: 18.8 us -> 6.2 us
  Pallas kernels: 558 us -> 569 us
    dot_general x2 -> x1, matrix products: 18.8 us -> 6.2 us  [weight_grad(): lax.dot_general(operand, upstream, (((0,), (0,)), ((), ())), preferred_el...]
    pallas_call x1, Pallas kernels: 121 us -> 133 us  [last_step(): pl.pallas_call(functools.partial(last_kernel, n, specs, early_specs, chun...]
where the time goes in v7:
time: 613 us; the launch traced here: 603 us
  Pallas kernels  569 us (93%)
  local copies, waits for them, and re-layouts  15 us (2%)
  other arithmetic  11.7 us (2%)
  matrix products  6.2 us (1%)
    pallas_call x1, Pallas kernels, attend_forward(): pl.pallas_call(functools.partial(forward_kernel, n, first_widths, cut), g...  187 us
    pallas_call x1, Pallas kernels, last_step(): pl.pallas_call(functools.partial(last_kernel, n, specs, early_specs, chun...  133 us
    pallas_call x1, Pallas kernels, attend_backward(): pl.pallas_call(functools.partial(backward_kernel, n, specs, done_specs),...  130 us
    pallas_call x1, Pallas kernels, feed_forward(): pl.pallas_call(functools.partial(mlp_kernel, n, specs, tile), out_shape=[...  119 us

profile of v7, /device:TPU:0, one launch (start us, length us, event | category | flops | bytes accessed | tf_op | source)
XLA Modules:
  0.0 603.1 jit_solution(4654471954374232800)
XLA Ops:
  0.6 0.7 stack.12
  1.3 0.7 stack.13
  2.0 0.7 stack.14
  2.7 0.6 pad_maximum_fusion.2.gain_ref.gains_ref.refs_2_.refs_6_
  3.4 1.4 copy.24.mix_ref
  4.7 0.9 copy.23
  5.7 0.1 rev.6
  5.8 0.1 pad_slice_fusion.1
  5.9 0.7 pad_maximum_fusion.1.taps_ref
  6.6 0.1 pad_slice_fusion.3
  6.7 0.7 pad_maximum_fusion.taps_ref
  7.4 187.2 %shard_map.203 = (bf16[512,1536]{1,0:T(8,128)(2,1)}, f32[512,1536]{1,0:T(8,128)}, bf16[16,512,384]{2,1,0:T(8,128)(2,1)}, bf16[512,1536]{1,0:T(8,128)(2,1)}, f32[...) custom-call(s32[1,4]{1,0:T(1,128)} %docs_ref.3, ...), custom_call_target="tpu_custom_call" | custom-call | tf_op jit(solution)/shard_map/pallas_call | solution.py:297
  194.6 0.0 copy-start.5
  194.6 118.6 %shard_map.204 = (bf16[512,1536]{1,0:T(8,128)(2,1)}, f32[512,1536]{1,0:T(8,128)}, f32[512,1536]{1,0:T(8,128)}, f32[1,1536]{1,0:T(1,128)}, bf16[1536,3072]{1,0:T(...) custom-call(bf16[512,1536]{1,0:T(8,128)(2,1)} %get-tuple-element.42., ...), custom_call_target="tpu_custom_call" | custom-call | tf_op jit(solution)/shard_map/pallas_call | solution.py:1580
  313.3 0.0 copy-done.5
  313.3 6.2 %convolution_convert_fusion.refs_10_ = bf16[1536,1536]{1,0:T(8,128)(2,1)} fusion(bf16[512,1536]{1,0:T(8,128)(2,1)S(1)} %copy-done.5, f32[512,1536]{1,0:T(8,128)} %get-tuple-element.60.refs_7_), kind=kOutput, calls=%fused_computation | convolution fusion | flops 2419064832 | bytes 9437184 | tf_op jit(solution)/shard_map/dot_general | solution.py:1620
  319.5 130.5 %shard_map.205 = (bf16[512,4608]{1,0:T(8,128)(2,1)}, f32[1,1536]{1,0:T(1,128)}, f32[16,8,128]{2,1,0:T(8,128)}, f32[4,8,128]{2,1,0:T(8,128)}, bf16[192,1792]{1,0:...) custom-call(s32[1,4]{1,0:T(1,128)} %docs_ref.3, ...), custom_call_target="tpu_custom_call" | custom-call | tf_op jit(solution)/shard_map/pallas_call | solution.py:570
  450.0 1.3 fusion.2
  451.3 132.7 %shard_map.206 = (f32[512,1536]{1,0:T(8,128)}, f32[64,128]{1,0:T(8,128)}, bf16[1536,4608]{1,0:T(8,128)(2,1)}, bf16[192,4608]{1,0:T(8,128)(2,1)}, bf16[192,1536]{...) custom-call(f32[1,1536]{1,0:T(1,128)} %get-tuple-element.55.refs_0_,, ...), custom_call_target="tpu_custom_call" | custom-call | tf_op jit(solution)/shard_map/pallas_call | solution.py:1342
  584.0 0.0 copy-start.1
  584.0 0.8 slice.65
  584.9 0.7 copy.28
  585.5 0.7 slice.63
  586.2 0.8 slice.62
  587.0 0.1 pad_maximum_fusion.3
  587.1 1.4 slice_bitcast_fusion
  588.5 0.1 reshape.41
  588.6 0.1 rev.7
  588.7 0.7 copy.29
  589.4 2.2 convert_element_type.24
  591.6 0.0 copy-done.1
  591.6 0.1 fusion.1
  591.8 0.0 copy-start.4
  591.8 3.0 maximum_convert_fusion
  594.8 0.0 copy-done.4
  594.8 0.0 copy-start.2
  594.8 2.1 convert_element_type.26
  596.8 0.0 copy-done.2
  596.8 0.0 copy-start.3
  596.9 0.0 copy-start
  596.9 2.2 convert_element_type.23
  599.1 0.0 copy-done.3
  599.1 1.1 copy.32
  600.2 0.9 copy-done
  601.1 1.7 copy.33
  (6 shorter events, 0.1 us)
Async XLA Ops:
  194.6 118.7 %copy-start.5 = (bf16[512,1536]{1,0:T(8,128)(2,1)S(1)}, bf16[512,1536]{1,0:T(8,128)(2,1)}, u32[]{:S(2)}) copy-start(bf16[512,1536]{1,0:T(8,128)(2,1)} %get-tuple-element.63) | copy-start | bytes 4718596
  584.0 7.6 %copy-start.1 = (bf16[192,5120]{1,0:T(8,128)(2,1)S(1)}, bf16[192,5120]{1,0:T(8,128)(2,1)}, u32[]{:S(2)}) copy-start(bf16[192,5120]{1,0:T(8,128)(2,1)} %get-tuple-element.71) | copy-start | bytes 5898244
  591.8 3.0 copy-start.4
  594.8 2.1 copy-start.2
  596.8 2.2 copy-start.3
  596.9 4.2 copy-start

commit v8 on v7

--- a/solution.py
+++ b/solution.py
@@ -951,8 +951,6 @@
     def item(self, j, work):
         last = self.ring.n - 1
         for i, d in work:
-            if d == 0 and self.kinds(i) == 3:
-                pl.when(j < last - 1)(functools.partial(self.give, i, j + 2))
             for copy in self.loads(i, d, j):
                 copy.wait()
             slot = self.slots[i][d]
@@ -976,6 +974,8 @@
                 self.fetch(i, d, j + 1)
 
             self.hand_next(i, d, j)
+            if d == 0 and self.kinds(i) == 3:
+                pl.when(j < last - 1)(functools.partial(self.give, i, j + 2))
 
             @pl.when(j == last)
             def _():
@@ -1297,10 +1297,10 @@
         pl.when(j + ahead < n)(lambda: reduce.item(j + ahead, behind))
 
     items(jnp.int32(0))
+    small.add_core()
     scaled = upstream * gain_ref[0:1, :]
     inner = jnp.mean(scaled * values, axis=1, keepdims=True)
     grad_input_ref[...] = d_middle_ref[...] + scale * scaled - values * (scale * scale * scale * inner)
-    small.add_core()
     items(jnp.int32(1))
     small.add_plane()
     hops = -(-n // (n - 3))
@@ -1637,7 +1637,7 @@
     cotangent,
 ):
     n = lax.axis_size("fsdp")
-    gains = jnp.stack([first_gain, group_gain, second_gain])
+    gains = jnp.concatenate([first_gain, group_gain, second_gain]).reshape(3, -1)
     kept, (qkv_weight, out_weight), (inner_first, down_full) = attend_forward(
         layer_input, conv_kernel, head_mixing, doc_lengths, gains, [qkv_weight, out_weight], inner_weight, down_weight, n, 0,
     )

time: 613 us -> 611 us (level)
  no operation moved by 1% of the time
where the time goes in v8:
time: 611 us; the launch traced here: 602 us
  Pallas kernels  569 us (93%)
  local copies, waits for them, and re-layouts  13.6 us (2%)
  other arithmetic  11.8 us (2%)
  matrix products  6.2 us (1%)
    pallas_call x1, Pallas kernels, attend_forward(): pl.pallas_call(functools.partial(forward_kernel, n, first_widths, cut), g...  187 us
    pallas_call x1, Pallas kernels, last_step(): pl.pallas_call(functools.partial(last_kernel, n, specs, early_specs, chun...  133 us
    pallas_call x1, Pallas kernels, attend_backward(): pl.pallas_call(functools.partial(backward_kernel, n, specs, done_specs),...  131 us
    pallas_call x1, Pallas kernels, feed_forward(): pl.pallas_call(functools.partial(mlp_kernel, n, specs, tile), out_shape=[...  119 us

profile of v8, /device:TPU:0, one launch (start us, length us, event | category | flops | bytes accessed | tf_op | source)
XLA Modules:
  0.0 601.7 jit_solution(15357095989161833803)
XLA Ops:
  0.6 1.4 copy.24.mix_ref
  2.0 0.7 pad_maximum_fusion.2
  2.7 0.6 reshape.43.gain_ref.gains_ref.refs_2_.refs_6_
  3.4 0.9 copy.23
  4.3 0.1 rev.6
  4.4 0.1 pad_slice_fusion.1
  4.5 0.7 pad_maximum_fusion.1.taps_ref
  5.2 0.1 pad_slice_fusion.3
  5.3 0.7 pad_maximum_fusion.taps_ref
  6.0 187.2 %shard_map.203 = (bf16[512,1536]{1,0:T(8,128)(2,1)}, f32[512,1536]{1,0:T(8,128)}, bf16[16,512,384]{2,1,0:T(8,128)(2,1)}, bf16[512,1536]{1,0:T(8,128)(2,1)}, f32[...) custom-call(s32[1,4]{1,0:T(1,128)} %docs_ref.3, ...), custom_call_target="tpu_custom_call" | custom-call | tf_op jit(solution)/shard_map/pallas_call | solution.py:297
  193.3 0.0 copy-start.5
  193.3 118.6 %shard_map.204 = (bf16[512,1536]{1,0:T(8,128)(2,1)}, f32[512,1536]{1,0:T(8,128)}, f32[512,1536]{1,0:T(8,128)}, f32[1,1536]{1,0:T(1,128)}, bf16[1536,3072]{1,0:T(...) custom-call(bf16[512,1536]{1,0:T(8,128)(2,1)} %get-tuple-element.42., ...), custom_call_target="tpu_custom_call" | custom-call | tf_op jit(solution)/shard_map/pallas_call | solution.py:1580
  311.9 0.0 copy-done.5
  311.9 6.2 %convolution_convert_fusion.refs_10_ = bf16[1536,1536]{1,0:T(8,128)(2,1)} fusion(bf16[512,1536]{1,0:T(8,128)(2,1)S(1)} %copy-done.5, f32[512,1536]{1,0:T(8,128)} %get-tuple-element.60.refs_7_), kind=kOutput, calls=%fused_computation | convolution fusion | flops 2419064832 | bytes 9437184 | tf_op jit(solution)/shard_map/dot_general | solution.py:1620
  318.1 130.6 %shard_map.205 = (bf16[512,4608]{1,0:T(8,128)(2,1)}, f32[1,1536]{1,0:T(1,128)}, f32[16,8,128]{2,1,0:T(8,128)}, f32[4,8,128]{2,1,0:T(8,128)}, bf16[192,1792]{1,0:...) custom-call(s32[1,4]{1,0:T(1,128)} %docs_ref.3, ...), custom_call_target="tpu_custom_call" | custom-call | tf_op jit(solution)/shard_map/pallas_call | solution.py:570
  448.7 1.3 fusion.2
  450.0 132.6 %shard_map.206 = (f32[512,1536]{1,0:T(8,128)}, f32[64,128]{1,0:T(8,128)}, bf16[1536,4608]{1,0:T(8,128)(2,1)}, bf16[192,4608]{1,0:T(8,128)(2,1)}, bf16[192,1536]{...) custom-call(f32[1,1536]{1,0:T(1,128)} %get-tuple-element.55.refs_0_,, ...), custom_call_target="tpu_custom_call" | custom-call | tf_op jit(solution)/shard_map/pallas_call | solution.py:1342
  582.6 0.0 copy-start.1
  582.6 0.8 slice.65
  583.4 0.7 copy.28
  584.1 0.7 slice.63
  584.8 0.8 slice.62
  585.6 0.1 pad_maximum_fusion.3
  585.7 1.4 slice_bitcast_fusion
  587.1 0.1 reshape.45
  587.2 0.1 rev.7
  587.3 0.7 copy.29
  588.0 2.2 convert_element_type.24
  590.2 0.0 copy-done.1
  590.2 0.1 fusion.1
  590.3 0.0 copy-start.4
  590.4 3.0 maximum_convert_fusion
  593.4 0.0 copy-done.4
  593.4 0.0 copy-start.2
  593.4 2.1 convert_element_type.26
  595.4 0.0 copy-done.2
  595.4 0.0 copy-start.3
  595.4 0.0 copy-start
  595.4 2.2 convert_element_type.23
  597.6 0.0 copy-done.3
  597.6 1.1 copy.32
  598.8 0.9 copy-done
  599.6 1.7 copy.33
  (6 shorter events, 0.1 us)
Async XLA Ops:
  193.3 118.6 %copy-start.5 = (bf16[512,1536]{1,0:T(8,128)(2,1)S(1)}, bf16[512,1536]{1,0:T(8,128)(2,1)}, u32[]{:S(2)}) copy-start(bf16[512,1536]{1,0:T(8,128)(2,1)} %get-tuple-element.63) | copy-start | bytes 4718596
  582.6 7.6 %copy-start.1 = (bf16[192,5120]{1,0:T(8,128)(2,1)S(1)}, bf16[192,5120]{1,0:T(8,128)(2,1)}, u32[]{:S(2)}) copy-start(bf16[192,5120]{1,0:T(8,128)(2,1)} %get-tuple-element.71) | copy-start | bytes 5898244
  590.3 3.0 copy-start.4
  593.4 2.1 copy-start.2
  595.4 2.2 copy-start.3
  595.4 4.2 copy-start
